TPU v7x, 32 devices: a whole 2x2x4 slice. The times are simulated.
32 devices in a mesh: fsdp: 4 (over x, core), ctx: 2 (over y), tp: 4 (over z).
Axes of the slice: x: 2, y: 2, z: 4, core: 2. Of those that a mesh axis runs over, the one named last changes fastest.
Arguments:
- layer_input: bfloat16 [6144, 2048], P(('fsdp', 'ctx'), 'tp'), may hold values from -6 to 6
- token_order: int32 [4, 1536], P('fsdp', 'ctx'), may hold values from 0 to 1535, each once within a row
- doc_lengths: int32 [4, 3], P('fsdp'), may hold values from 1 to 1024, 1536 in all within a row
- expert_routes: int32 [6144, 8], P(('fsdp', 'ctx')), may hold values from 0 to 31, all different within a row; in each aligned block of 768 rows (0 to 767, 768 to 1535, ...) at most 240 rows name the same one
- attn_gain: bfloat16 [2048], P(('fsdp', 'ctx')), may hold values from 0.5 to 1.5
- query_weight: bfloat16 [2048, 2048], P(('fsdp', 'ctx'), 'tp'), may hold values from -0.125 to 0.125
- key_weight: bfloat16 [2048, 2048], P(('fsdp', 'ctx'), 'tp'), may hold values from -0.125 to 0.125
- value_weight: bfloat16 [2048, 2048], P(('fsdp', 'ctx'), 'tp'), may hold values from -0.125 to 0.125
- query_gain: float32 [128], replicated, may hold values from 1 to 2
- key_gain: float32 [128], replicated, may hold values from 1 to 2
- out_weight: bfloat16 [2048, 2048], P('tp', ('fsdp', 'ctx')), may hold values from -0.5 to 0.5
- moe_gain: bfloat16 [2048], P(('fsdp', 'ctx')), may hold values from 0.5 to 1.5
- router_weight: bfloat16 [2048, 32], P(('fsdp', 'ctx')), may hold values from -0.0625 to 0.0625
- gate_weight: bfloat16 [32, 2048, 1024], P(('fsdp', 'ctx'), None, 'tp'), may hold values from -0.125 to 0.125
- up_weight: bfloat16 [32, 2048, 1024], P(('fsdp', 'ctx'), None, 'tp'), may hold values from -0.125 to 0.125
- down_weight: bfloat16 [32, 1024, 2048], P(('fsdp', 'ctx'), 'tp'), may hold values from -0.5 to 0.5
- out_grad: bfloat16 [6144, 2048], P(('fsdp', 'ctx'), 'tp'), may hold values from -6 to 6
Outputs:
- layer_output: bfloat16 [6144, 2048], P(('fsdp', 'ctx'), 'tp')
- grad_input: float32 [6144, 2048], P(('fsdp', 'ctx'), 'tp')
- grad_attn_gain: float32 [2048], P(('fsdp', 'ctx'))
- grad_query_weight: float32 [2048, 2048], P(('fsdp', 'ctx'), 'tp')
- grad_key_weight: float32 [2048, 2048], P(('fsdp', 'ctx'), 'tp')
- grad_value_weight: float32 [2048, 2048], P(('fsdp', 'ctx'), 'tp')
- grad_query_gain: float32 [128], replicated
- grad_key_gain: float32 [128], replicated
- grad_out_weight: float32 [2048, 2048], P('tp', ('fsdp', 'ctx'))
- grad_moe_gain: float32 [2048], P(('fsdp', 'ctx'))
- grad_router_weight: float32 [2048, 32], P(('fsdp', 'ctx'))
- grad_gate_weight: float32 [32, 2048, 1024], P(('fsdp', 'ctx'), None, 'tp')
- grad_up_weight: float32 [32, 2048, 1024], P(('fsdp', 'ctx'), None, 'tp')
- grad_down_weight: float32 [32, 1024, 2048], P(('fsdp', 'ctx'), 'tp')
Inputs may be any that keep to these rules, and one draw needn't show every extreme that they name: `token_order`: each row is a permutation of 0 to 1535. `doc_lengths`: each row holds the lengths of its group's 3 documents and sums to 1536. `expert_routes`: each row names 8 different experts; within the rows of one device no expert is named more than 240 times.
All inputs are finite; a program needn't handle non-finite values.
Results may differ from a plain program's by a relative error of at most 0.028.
Values may be sent and summed in bfloat16 or wider, within the bound.
A program may use at most 512 MiB of HBM per device.

v0:
```python
import jax
import jax.numpy as jnp
from jax import lax
from jax.sharding import PartitionSpec as P

KEY_BLOCK = 512


epsilon = 1e-05
rope_base = 50000.0
masked_score = -1e30
highest = lax.Precision.HIGHEST


def quarter_join(values):
    return lax.all_gather(values, "tp", axis=3, tiled=True)


def token_rows(values):
    joined = quarter_join(values.reshape(1, 1, values.shape[0], values.shape[1]))
    return joined.reshape(values.shape[0], joined.shape[3])


def share_sums(values):
    return lax.psum_scatter(
        values.astype(jnp.bfloat16), "tp", scatter_dimension=3, tiled=True
    ).astype(jnp.float32)


def head_sums(values):
    return lax.psum(values.astype(jnp.bfloat16), "tp").astype(jnp.float32)


def send_experts(values):
    return lax.all_to_all(values, ("fsdp", "ctx"), split_axis=0, concat_axis=0, tiled=True)


def return_experts(values):
    return lax.all_to_all(values, ("fsdp", "ctx"), split_axis=0, concat_axis=0, tiled=True)


def doc_places(order_row, length_row):
    ends = jnp.cumsum(length_row, dtype=jnp.int32)
    passed = (order_row[:, None] >= ends[None, :]).astype(jnp.int32)
    segment = jnp.sum(passed, axis=1, dtype=jnp.int32)
    start = jnp.sum(passed * length_row[None, :], axis=1, dtype=jnp.int32)
    return (segment, order_row - start)


def rope_tables(position, head_dim):
    half = head_dim // 2
    freqs = rope_base ** (-(jnp.arange(half, dtype=jnp.float32) * (2.0 / head_dim)))
    angles = position.astype(jnp.float32)[:, None] * freqs[None, :]
    return (jnp.cos(angles)[:, None, :], jnp.sin(angles)[:, None, :])


def rotate(values, cosine, sine):
    half = values.shape[-1] // 2
    first = values[..., :half]
    second = values[..., half:]
    return jnp.concatenate(
        [first * cosine - second * sine, second * cosine + first * sine], axis=-1
    )


def rotate_back(grads, cosine, sine):
    half = grads.shape[-1] // 2
    first = grads[..., :half]
    second = grads[..., half:]
    return jnp.concatenate(
        [first * cosine + second * sine, second * cosine - first * sine], axis=-1
    )


def norm_scale(values):
    return lax.rsqrt(jnp.mean(values * values, axis=-1, keepdims=True) + epsilon)


def norm_back(incoming, values, inverse, gain):
    scaled = incoming * gain
    value_grad = inverse * (
        scaled - values * inverse * inverse * jnp.mean(scaled * values, axis=-1, keepdims=True)
    )
    return (value_grad, incoming * values * inverse)


def on_device(
    layer_input,
    token_order,
    doc_lengths,
    expert_routes,
    attn_gain,
    query_weight,
    key_weight,
    value_weight,
    query_gain,
    key_gain,
    out_weight,
    moe_gain,
    router_weight,
    gate_weight,
    up_weight,
    down_weight,
    out_grad,
):
    tp_index = lax.axis_index("tp")
    tok_count, quarter = layer_input.shape
    head_dim = query_gain.shape[0]
    heads = query_weight.shape[1] // head_dim
    scale = head_dim ** (-0.5)
    full_attn_gain, full_query, full_key, full_value, full_out, full_moe_gain, full_router = (
        lax.all_gather(attn_gain, ("fsdp", "ctx"), axis=0, tiled=True),
        lax.all_gather(query_weight, ("fsdp", "ctx"), axis=0, tiled=True),
        lax.all_gather(key_weight, ("fsdp", "ctx"), axis=0, tiled=True),
        lax.all_gather(value_weight, ("fsdp", "ctx"), axis=0, tiled=True),
        lax.all_gather(out_weight, ("fsdp", "ctx"), axis=1, tiled=True),
        lax.all_gather(moe_gain, ("fsdp", "ctx"), axis=0, tiled=True),
        lax.all_gather(router_weight, ("fsdp", "ctx"), axis=0, tiled=True),
    )
    input_f = token_rows(layer_input).astype(jnp.float32)
    segment, position = doc_places(token_order[0], doc_lengths[0])
    cosine, sine = rope_tables(position, head_dim)
    inverse_one = norm_scale(input_f)
    normed = (input_f * inverse_one * full_attn_gain.astype(jnp.float32)).astype(jnp.bfloat16)
    query_pre = jnp.dot(normed, full_query, preferred_element_type=jnp.float32).reshape(
        tok_count, heads, head_dim
    )
    key_pre = jnp.dot(normed, full_key, preferred_element_type=jnp.float32).reshape(
        tok_count, heads, head_dim
    )
    value_b = jnp.dot(normed, full_value, preferred_element_type=jnp.float32).astype(jnp.bfloat16)
    query_inv = norm_scale(query_pre)
    key_inv = norm_scale(key_pre)
    query_b = rotate(query_pre * query_inv * query_gain, cosine, sine).astype(jnp.bfloat16)
    key_b = rotate(key_pre * key_inv * key_gain, cosine, sine).astype(jnp.bfloat16)
    seg_b = segment.astype(jnp.bfloat16)
    key_all, value_all, seg_all = (
        lax.all_gather(key_b.reshape(tok_count, heads * head_dim), "ctx", axis=0, tiled=True),
        lax.all_gather(value_b, "ctx", axis=0, tiled=True),
        lax.all_gather(seg_b, "ctx", axis=0, tiled=True),
    )
    blocks = key_all.shape[0] // KEY_BLOCK
    key_blocks = key_all.reshape(blocks, KEY_BLOCK, heads, head_dim)
    value_blocks = value_all.reshape(blocks, KEY_BLOCK, heads, head_dim)
    seg_blocks = seg_all.reshape(blocks, KEY_BLOCK)

    def forward_step(carry, pieces):
        run_max, run_sum, accum = carry
        key_blk, value_blk, seg_blk = pieces
        scores = (
            jnp.einsum("qhd,khd->hqk", query_b, key_blk, preferred_element_type=jnp.float32) * scale
        )
        allowed = (seg_b[:, None] == seg_blk[None, :])[None]
        scores = jnp.where(allowed, scores, masked_score)
        new_max = jnp.maximum(run_max, jnp.max(scores, axis=-1))
        probs = jnp.where(allowed, jnp.exp(scores - new_max[..., None]), 0.0)
        factor = jnp.exp(run_max - new_max)
        run_sum = run_sum * factor + jnp.sum(probs, axis=-1)
        accum = accum * factor[..., None] + jnp.einsum(
            "hqk,khd->hqd",
            probs.astype(jnp.bfloat16),
            value_blk,
            preferred_element_type=jnp.float32,
        )
        return ((new_max, run_sum, accum), None)

    start_carry = (
        jnp.full((heads, tok_count), masked_score, jnp.float32),
        jnp.zeros((heads, tok_count), jnp.float32),
        jnp.zeros((heads, tok_count, head_dim), jnp.float32),
    )
    (run_max, run_sum, accum), unused = lax.scan(
        forward_step, start_carry, (key_blocks, value_blocks, seg_blocks)
    )
    log_total = run_max + jnp.log(run_sum)
    attn_heads = jnp.transpose(accum / run_sum[..., None], (1, 0, 2))
    attn_b = attn_heads.reshape(tok_count, heads * head_dim).astype(jnp.bfloat16)
    attn_out = head_sums(jnp.dot(attn_b, full_out, preferred_element_type=jnp.float32))
    resid = input_f + attn_out
    inverse_two = norm_scale(resid)
    moe_gain_f = full_moe_gain.astype(jnp.float32)
    moe_in = (resid * inverse_two * moe_gain_f).astype(jnp.bfloat16)
    logits = jnp.dot(moe_in, full_router, preferred_element_type=jnp.float32)
    experts = full_router.shape[1]
    top = expert_routes.shape[1]
    pick_f = (
        expert_routes[:, :, None] == jnp.arange(experts, dtype=jnp.int32)[None, None, :]
    ).astype(jnp.float32)
    chosen = jnp.einsum("tke,te->tk", pick_f, logits, precision=highest)
    gates = jax.nn.softmax(chosen, axis=-1)
    assign = tok_count * top
    capacity = tok_count * top * 5 // (4 * experts)
    local_experts = gate_weight.shape[0]
    groups = experts // local_experts
    flat_routes = expert_routes.reshape(assign)
    one_hot = (flat_routes[:, None] == jnp.arange(experts, dtype=jnp.int32)[None, :]).astype(
        jnp.int32
    )
    ranks = jnp.cumsum(one_hot, axis=0, dtype=jnp.int32) - one_hot
    place = flat_routes * capacity + jnp.sum(ranks * one_hot, axis=1, dtype=jnp.int32)
    assign_ids = jnp.arange(assign, dtype=jnp.int32)
    source_token = jnp.zeros((experts * capacity,), jnp.int32).at[place].set(assign_ids // top)
    source_assign = jnp.zeros((experts * capacity,), jnp.int32).at[place].set(assign_ids)
    filled = jnp.zeros((experts * capacity,), jnp.bfloat16).at[place].set(1.0)[:, None]
    sent = (moe_in[source_token] * filled).reshape(groups, local_experts, capacity, moe_in.shape[1])
    expert_in = send_experts(sent)
    gate_act = jnp.einsum(
        "gecd,edf->gecf", expert_in, gate_weight, preferred_element_type=jnp.float32
    )
    up_act = jnp.einsum("gecd,edf->gecf", expert_in, up_weight, preferred_element_type=jnp.float32)
    sigmoid_g = jax.nn.sigmoid(gate_act)
    silu_g = gate_act * sigmoid_g
    hidden_b = (silu_g * up_act).astype(jnp.bfloat16)
    expert_part = jnp.einsum(
        "gecf,efd->gecd", hidden_b, down_weight, preferred_element_type=jnp.float32
    )
    expert_out = share_sums(expert_part).astype(jnp.bfloat16)
    returned = return_experts(quarter_join(expert_out))
    row_width = returned.shape[3]
    picked = returned.reshape(experts * capacity, row_width)[place].reshape(
        tok_count, top, row_width
    )
    moe_out = jnp.einsum(
        "tk,tkw->tw", gates, picked, precision=highest, preferred_element_type=jnp.float32
    )
    layer_output = lax.dynamic_slice_in_dim(resid + moe_out, tp_index * quarter, quarter, 1).astype(
        jnp.bfloat16
    )
    grad_rows_b = token_rows(out_grad)
    grad_rows = grad_rows_b.astype(jnp.float32)
    picked_grad = (gates[:, :, None] * grad_rows[:, None, :]).astype(jnp.bfloat16)
    gate_grad = jnp.einsum("tkw,tw->tk", picked, grad_rows_b, preferred_element_type=jnp.float32)
    grad_sent = (picked_grad.reshape(assign, row_width)[source_assign] * filled).reshape(
        groups, local_experts, capacity, row_width
    )
    grad_in = send_experts(grad_sent)
    grad_down = jnp.einsum("gecf,gecd->efd", hidden_b, grad_in, preferred_element_type=jnp.float32)
    hidden_grad = jnp.einsum(
        "gecd,efd->gecf", grad_in, down_weight, preferred_element_type=jnp.float32
    )
    gate_act_grad = (
        hidden_grad * up_act * sigmoid_g * (1.0 + gate_act * (1.0 - sigmoid_g))
    ).astype(jnp.bfloat16)
    up_act_grad = (hidden_grad * silu_g).astype(jnp.bfloat16)
    grad_gate = jnp.einsum(
        "gecd,gecf->edf", expert_in, gate_act_grad, preferred_element_type=jnp.float32
    )
    grad_up = jnp.einsum(
        "gecd,gecf->edf", expert_in, up_act_grad, preferred_element_type=jnp.float32
    )
    back_part = jnp.einsum(
        "gecf,edf->gecd", gate_act_grad, gate_weight, preferred_element_type=jnp.float32
    ) + jnp.einsum("gecf,edf->gecd", up_act_grad, up_weight, preferred_element_type=jnp.float32)
    back_share = share_sums(back_part).astype(jnp.bfloat16)
    back_rows = return_experts(quarter_join(back_share))
    full_width = back_rows.shape[3]
    routed_grad = back_rows.reshape(experts * capacity, full_width)[place].reshape(
        tok_count, top, full_width
    )
    moe_in_grad = jnp.sum(routed_grad.astype(jnp.float32), axis=1)
    sel_grad = gates * (gate_grad - jnp.sum(gates * gate_grad, axis=-1, keepdims=True))
    logit_grad = jnp.einsum("tke,tk->te", pick_f, sel_grad, precision=highest)
    grad_router = jnp.dot(moe_in.astype(jnp.float32).T, logit_grad, precision=highest)
    moe_in_grad = moe_in_grad + jnp.dot(
        logit_grad, full_router.astype(jnp.float32).T, precision=highest
    )
    resid_norm_grad, gain_terms = norm_back(moe_in_grad, resid, inverse_two, moe_gain_f)
    grad_moe_gain = jnp.sum(gain_terms, axis=0)
    resid_grad = grad_rows + resid_norm_grad
    resid_grad_b = resid_grad.astype(jnp.bfloat16)
    grad_out = jnp.einsum("tf,td->fd", attn_b, resid_grad_b, preferred_element_type=jnp.float32)
    attn_grad = jnp.dot(resid_grad_b, full_out.T, preferred_element_type=jnp.float32).astype(
        jnp.bfloat16
    )
    attn_grad = attn_grad.reshape(tok_count, heads, head_dim)
    delta = jnp.transpose(jnp.sum(attn_grad.astype(jnp.float32) * attn_heads, axis=-1))

    def backward_step(query_accum, pieces):
        key_blk, value_blk, seg_blk = pieces
        scores = (
            jnp.einsum("qhd,khd->hqk", query_b, key_blk, preferred_element_type=jnp.float32) * scale
        )
        allowed = (seg_b[:, None] == seg_blk[None, :])[None]
        probs = jnp.where(allowed, jnp.exp(scores - log_total[..., None]), 0.0)
        prob_grad = jnp.einsum(
            "qhd,khd->hqk", attn_grad, value_blk, preferred_element_type=jnp.float32
        )
        score_grad = (probs * (prob_grad - delta[..., None])).astype(jnp.bfloat16)
        query_accum = (
            query_accum
            + jnp.einsum("hqk,khd->qhd", score_grad, key_blk, preferred_element_type=jnp.float32)
            * scale
        )
        key_blk_grad = (
            jnp.einsum("hqk,qhd->khd", score_grad, query_b, preferred_element_type=jnp.float32)
            * scale
        )
        value_blk_grad = jnp.einsum(
            "hqk,qhd->khd",
            probs.astype(jnp.bfloat16),
            attn_grad,
            preferred_element_type=jnp.float32,
        )
        return (query_accum, (key_blk_grad, value_blk_grad))

    query_rot_grad, (key_stack, value_stack) = lax.scan(
        backward_step,
        jnp.zeros((tok_count, heads, head_dim), jnp.float32),
        (key_blocks, value_blocks, seg_blocks),
    )
    group_rows = blocks * KEY_BLOCK
    key_grad, value_grad = (
        lax.psum_scatter(
            key_stack.reshape(group_rows, heads * head_dim).astype(jnp.bfloat16),
            "ctx",
            scatter_dimension=0,
            tiled=True,
        ).astype(jnp.float32),
        lax.psum_scatter(
            value_stack.reshape(group_rows, heads * head_dim).astype(jnp.bfloat16),
            "ctx",
            scatter_dimension=0,
            tiled=True,
        ).astype(jnp.float32),
    )
    key_rot_grad = key_grad.reshape(tok_count, heads, head_dim)
    query_pre_grad, query_gain_terms = norm_back(
        rotate_back(query_rot_grad, cosine, sine), query_pre, query_inv, query_gain
    )
    key_pre_grad, key_gain_terms = norm_back(
        rotate_back(key_rot_grad, cosine, sine), key_pre, key_inv, key_gain
    )
    query_pre_b = query_pre_grad.reshape(tok_count, heads * head_dim).astype(jnp.bfloat16)
    key_pre_b = key_pre_grad.reshape(tok_count, heads * head_dim).astype(jnp.bfloat16)
    value_grad_b = value_grad.astype(jnp.bfloat16)
    grad_query = jnp.einsum("td,tf->df", normed, query_pre_b, preferred_element_type=jnp.float32)
    grad_key = jnp.einsum("td,tf->df", normed, key_pre_b, preferred_element_type=jnp.float32)
    grad_value = jnp.einsum("td,tf->df", normed, value_grad_b, preferred_element_type=jnp.float32)
    normed_grad = head_sums(
        jnp.dot(query_pre_b, full_query.T, preferred_element_type=jnp.float32)
        + jnp.dot(key_pre_b, full_key.T, preferred_element_type=jnp.float32)
        + jnp.dot(value_grad_b, full_value.T, preferred_element_type=jnp.float32)
    )
    input_norm_grad, attn_terms = norm_back(
        normed_grad, input_f, inverse_one, full_attn_gain.astype(jnp.float32)
    )
    grad_attn = jnp.sum(attn_terms, axis=0)
    grad_input = lax.dynamic_slice_in_dim(
        resid_grad + input_norm_grad, tp_index * quarter, quarter, 1
    )
    owned = (
        lax.psum_scatter(
            grad_attn.astype(jnp.bfloat16), ("fsdp", "ctx"), scatter_dimension=0, tiled=True
        ).astype(jnp.float32),
        lax.psum_scatter(
            grad_query.astype(jnp.bfloat16), ("fsdp", "ctx"), scatter_dimension=0, tiled=True
        ).astype(jnp.float32),
        lax.psum_scatter(
            grad_key.astype(jnp.bfloat16), ("fsdp", "ctx"), scatter_dimension=0, tiled=True
        ).astype(jnp.float32),
        lax.psum_scatter(
            grad_value.astype(jnp.bfloat16), ("fsdp", "ctx"), scatter_dimension=0, tiled=True
        ).astype(jnp.float32),
        lax.psum_scatter(
            grad_out.astype(jnp.bfloat16), ("fsdp", "ctx"), scatter_dimension=1, tiled=True
        ).astype(jnp.float32),
        lax.psum_scatter(
            grad_moe_gain.astype(jnp.bfloat16), ("fsdp", "ctx"), scatter_dimension=0, tiled=True
        ).astype(jnp.float32),
        lax.psum_scatter(
            grad_router.astype(jnp.bfloat16), ("fsdp", "ctx"), scatter_dimension=0, tiled=True
        ).astype(jnp.float32),
    )
    grad_query_gain, grad_key_gain = lax.psum(
        (jnp.sum(query_gain_terms, axis=(0, 1)), jnp.sum(key_gain_terms, axis=(0, 1))),
        ("fsdp", "ctx", "tp"),
    )
    return (
        layer_output,
        grad_input,
        owned[0],
        owned[1],
        owned[2],
        owned[3],
        grad_query_gain,
        grad_key_gain,
        owned[4],
        owned[5],
        owned[6],
        grad_gate,
        grad_up,
        grad_down,
    )


def solution(mesh):
    in_specs = (
        P(("fsdp", "ctx"), "tp"),
        P("fsdp", "ctx"),
        P("fsdp", None),
        P(("fsdp", "ctx"), None),
        P(("fsdp", "ctx")),
        P(("fsdp", "ctx"), "tp"),
        P(("fsdp", "ctx"), "tp"),
        P(("fsdp", "ctx"), "tp"),
        P(),
        P(),
        P("tp", ("fsdp", "ctx")),
        P(("fsdp", "ctx")),
        P(("fsdp", "ctx"), None),
        P(("fsdp", "ctx"), None, "tp"),
        P(("fsdp", "ctx"), None, "tp"),
        P(("fsdp", "ctx"), "tp", None),
        P(("fsdp", "ctx"), "tp"),
    )
    out_specs = (
        P(("fsdp", "ctx"), "tp"),
        P(("fsdp", "ctx"), "tp"),
        P(("fsdp", "ctx")),
        P(("fsdp", "ctx"), "tp"),
        P(("fsdp", "ctx"), "tp"),
        P(("fsdp", "ctx"), "tp"),
        P(),
        P(),
        P("tp", ("fsdp", "ctx")),
        P(("fsdp", "ctx")),
        P(("fsdp", "ctx"), None),
        P(("fsdp", "ctx"), None, "tp"),
        P(("fsdp", "ctx"), None, "tp"),
        P(("fsdp", "ctx"), "tp", None),
    )
    return jax.shard_map(
        on_device, mesh=mesh, in_specs=in_specs, out_specs=out_specs, check_vma=False
    )
```

profile of v0, /device:TPU:0, one launch (start us, length us, event | category | flops | bytes accessed | tf_op | source)
XLA Modules:
  0.0 5018.7 jit_solution(17042022577943621507)
XLA Ops:
  12.2 14.6 all-gather.3
  28.9 11.6 all-gather.16.cloned.1.call-done
  44.4 25.9 all-gather.20.cloned.1.call-done
  74.2 61.2 %all-gather.32.cloned.1.call-done = bf16[768,2048]{1,0:T(8,128)(2,1)} async-done(((bf16[768,512]{1,0:T(8,128)(2,1)}), bf16[768,2048]{1,0:T(8,128)(2,1)}) %all-gather.32.cloned.1.call-update) | async-done | bytes 3145744 | tf_op jit(solution)/shard_map/all_gather | solution.py:16
  138.0 25.8 all-gather.22.cloned.1.call-done
  163.8 5.4 convolution_convert_fusion.4
  181.8 5.0 all-gather.2
  203.0 22.9 all-gather.18.cloned.1.call-done
  232.2 28.6 while.30
  266.3 5.3 convolution_convert_fusion
  274.2 13.3 all-gather.4
  292.3 18.4 reduce-window.19
  314.8 42.6 scatter_custom_fusion.1
  357.5 23.0 scatter_custom_fusion
  380.5 12.4 all-reduce.7.cloned.1.call-done
  398.6 29.4 gather_fusion
  428.0 21.3 broadcast_multiply_fusion.1
  449.4 351.3 %all_to_all.20 = bf16[8,4,240,2048]{3,2,1,0:T(8,128)(2,1)} all-to-all(bf16[8,4,240,2048]{3,2,1,0:T(8,128)(2,1)} %broadcast_multiply_fusion.1), channel_id=1, replica_groups=mesh['fsdp'=4,'ctx'=2,'tp'=4] {'fsdp','ctx'}, dimensions={0} | all-to-all | bytes 62914560 | tf_op jit(solution)/shard_map/all_to_all | solution.py:35
  800.7 17.3 fusion.53
  818.0 22.0 fusion.63
  840.0 16.4 convert_bitcast_fusion
  856.5 513.6 %reduce-scatter.10.cloned.1.call-done = bf16[8,4,240,512]{3,2,0,1:T(8,128)(2,1)} async-done(((bf16[8,4,240,2048]{3,2,0,1:T(8,128)(2,1)}), bf16[8,4,240,512]{3,2,0,1:T(8,128)(2,1)}) %reduce-scatter.10.cloned.1.call-update) | async-done | bytes 7864336 | tf_op jit(solution)/shard_map/reduce_scatter | solution.py:25
  1370.1 530.7 %all-gather.28.cloned.1.call-done = bf16[8,4,240,2048]{3,2,0,1:T(8,128)(2,1)} async-done(((bf16[8,4,240,512]{3,2,0,1:T(8,128)(2,1)}), bf16[8,4,240,2048]{3,2,0,1:T(8,128)(2,1)}) %all-gather.28.cloned.1.call-update) | async-done | bytes 31457296 | tf_op jit(solution)/shard_map/all_gather | solution.py:16
  1900.9 21.3 copy.142
  1922.2 7.0 all-to-all-start.1
  1930.1 23.0 scatter_custom_fusion.2
  1953.1 325.6 %all_gather.52 = bf16[2048,32]{0,1:T(8,128)(2,1)S(1)} all-gather(bf16[256,32]{0,1:T(8,128)(2,1)S(1)} %copy-done.77), channel_id=1, replica_groups=mesh['fsdp'=4,'ctx'=2,'tp'=4] {'fsdp','ctx'}, dimensions={0}, use_global_device_ids=true | all-gather | bytes 147456 | tf_op jit(solution)/shard_map/all_gather | solution.py:118
  2279.9 5.4 convert_element_type.241
  2287.1 143.9 %gather_fusion.1 = bf16[6144,2048]{1,0:T(8,128)(2,1)} fusion(bf16[7680,2048]{1,0:T(8,128)(2,1)} %bitcast.32, s32[6144]{0:T(1024)} %broadcast_clamp_fusion), kind=kCustom, calls=%fused_computation.1 | custom fusion | bytes 50356224 | tf_op jit(solution)/shard_map/gather | solution.py:220
  2431.0 14.0 fusion.55
  2446.2 14.2 fusion.45
  2460.4 68.9 %gather_fusion.2 = bf16[7680,2048]{1,0:T(8,128)(2,1)} fusion(bf16[6144,2048]{1,0:T(8,128)(2,1)} %fusion.45, s32[8192]{0:T(1024)S(1)} %copy-done.64), kind=kCustom, calls=%fused_computation.2 | custom fusion | bytes 62945280 | tf_op jit(solution)/shard_map/gather | solution.py:233
  2529.3 21.3 broadcast_multiply_fusion
  2550.6 351.3 %all_to_all.21 = bf16[8,4,240,2048]{3,2,1,0:T(8,128)(2,1)} all-to-all(bf16[8,4,240,2048]{3,2,1,0:T(8,128)(2,1)} %broadcast_multiply_fusion), channel_id=1, replica_groups=mesh['fsdp'=4,'ctx'=2,'tp'=4] {'fsdp','ctx'}, dimensions={0} | all-to-all | bytes 62914560 | tf_op jit(solution)/shard_map/all_to_all | solution.py:35
  2901.9 23.1 fusion.62
  2925.0 25.5 fusion.81
  2950.5 33.6 fusion.46
  2984.2 512.8 %reduce-scatter.12.cloned.1.call-done = bf16[8,4,240,512]{3,2,0,1:T(8,128)(2,1)} async-done(((bf16[8,4,240,2048]{3,2,0,1:T(8,128)(2,1)}), bf16[8,4,240,512]{3,2,0,1:T(8,128)(2,1)}) %reduce-scatter.12.cloned.1.call-update) | async-done | bytes 7864336 | tf_op jit(solution)/shard_map/reduce_scatter | solution.py:25
  3497.1 530.8 %all-gather.30.cloned.1.call-done = bf16[8,4,240,2048]{3,2,0,1:T(8,128)(2,1)} async-done(((bf16[8,4,240,512]{3,2,0,1:T(8,128)(2,1)}), bf16[8,4,240,2048]{3,2,0,1:T(8,128)(2,1)}) %all-gather.30.cloned.1.call-update) | async-done | bytes 31457296 | tf_op jit(solution)/shard_map/all_gather | solution.py:16
  4027.9 21.3 copy.144
  4049.3 7.0 all-to-all-start.3
  4061.8 334.9 %all-to-all-done.3 = bf16[8,4,240,2048]{3,2,1,0:T(8,128)(2,1)} async-done(((bf16[8,4,240,2048]{3,2,1,0:T(8,128)(2,1)}), bf16[8,4,240,2048]{3,2,1,0:T(8,128)(2,1)}, u32[]{:S(2)}, u32[]{:S(2)}) %all-to-all-start.3) | async-done | bytes 31457312 | tf_op jit(solution)/shard_map/all_to_all | solution.py:39
  4396.7 143.6 %gather_fusion.3 = bf16[6144,2048]{1,0:T(8,128)(2,1)} fusion(bf16[7680,2048]{1,0:T(8,128)(2,1)} %bitcast.42, s32[6144]{0:T(1024)S(1)} %copy-done.54), kind=kCustom, calls=%fused_computation.3 | custom fusion | bytes 50356224 | tf_op jit(solution)/shard_map/gather | solution.py:257
  4540.3 20.7 convert_reduce_fusion
  4561.0 7.8 multiply_reduce_fusion
  4568.9 5.5 multiply_add_fusion
  4578.5 37.3 while.31
  4627.3 5.9 convolution_convert_fusion.1
  4633.3 10.1 reduce-scatter.14.cloned.1.call-done
  4665.5 23.7 fusion.57
  4689.2 5.7 copy.204
  4696.2 6.5 fusion.137
  4702.7 4.5 fusion.136
  4708.8 9.0 add_convert_fusion.1
  4717.9 20.1 convolution_bitcast_fusion
  4738.0 17.8 fusion.76
  4759.2 19.5 convolution_bitcast_fusion.1
  4783.5 39.5 all-reduce.2
  4824.8 18.1 reduce-scatter.20.cloned.1.call-done
  4844.8 121.5 %all-reduce.9.cloned.1.call-done = bf16[768,2048]{1,0:T(8,128)(2,1)} async-done(((bf16[768,2048]{1,0:T(8,128)(2,1)}), bf16[768,2048]{1,0:T(8,128)(2,1)}) %all-reduce.9.cloned.1.call-update) | async-done | bytes 3145744 | tf_op jit(solution)/shard_map/psum | solution.py:31
  4966.3 7.1 fusion.69
  4973.4 14.0 all-reduce.3
  4988.7 4.2 dynamic-slice_add_fusion
  4993.0 16.9 reduce-scatter.22.cloned.1.call-done
  (410 shorter events, 205.5 us)
Async XLA Ops:
  7.2 33.3 all-gather.16.cloned.1.call-start
  7.9 62.4 %all-gather.20.cloned.1.call-start = ((), (), s32[]{:S(2)}) async-start(), calls=%async_computation.15 | async-start | bytes 2359296 | tf_op jit(solution)/shard_map/all_gather | solution.py:113
  8.7 126.7 %all-gather.32.cloned.1.call-start = ((), (), s32[]{:S(2)}) async-start(), calls=%async_computation.32 | async-start | bytes 3932160 | tf_op jit(solution)/shard_map/all_gather | solution.py:16
  9.4 154.4 %all-gather.22.cloned.1.call-start = ((), (), s32[]{:S(2)}) async-start(), calls=%async_computation.16 | async-start | bytes 2359296 | tf_op jit(solution)/shard_map/all_gather | solution.py:115
  10.0 186.7 %all-gather.24.cloned.1.call-start = ((), (), s32[]{:S(2)}) async-start(), calls=%async_computation.17 | async-start | bytes 2359296 | tf_op jit(solution)/shard_map/all_gather | solution.py:139
  26.8 146.2 %copy-start.73 = (f32[8,1,256]{2,1,0:T(1,128)}, f32[8,1,256]{2,1,0:T(1,128)S(1)}, u32[]{:S(2)}) copy-start(f32[8,1,256]{2,1,0:T(1,128)S(1)} %convert_element_type.280) | copy-start | bytes 24580
  28.9 146.7 %copy-start.28 = (f32[768,64]{0,1:T(8,128)}, f32[768,64]{0,1:T(8,128)S(1)}, u32[]{:S(2)}) copy-start(f32[768,64]{0,1:T(8,128)S(1)} %get-tuple-element.387) | copy-start | bytes 589828
  28.9 146.7 %copy-start.30 = (f32[768,64]{0,1:T(8,128)}, f32[768,64]{0,1:T(8,128)S(1)}, u32[]{:S(2)}) copy-start(f32[768,64]{0,1:T(8,128)S(1)} %get-tuple-element.388) | copy-start | bytes 589828
  138.0 35.0 copy-start.71
  169.2 56.6 %all-gather.18.cloned.1.call-start = ((), (), s32[]{:S(2)}) async-start(), calls=%async_computation.14 | async-start | bytes 2359296 | tf_op jit(solution)/shard_map/all_gather | solution.py:138
  176.9 12.4 copy-start.38
  180.3 86.0 %all-gather.26.cloned.1.call-start = ((), (), s32[]{:S(2)}) async-start(), calls=%async_computation.18 | async-start | bytes 2359296 | tf_op jit(solution)/shard_map/all_gather | solution.py:116
  181.0 211.9 %all-reduce.7.cloned.1.call-start = ((), (), s32[]{:S(2)}) async-start(), calls=%async_computation.19 | async-start | bytes 6291456 | tf_op jit(solution)/shard_map/psum | solution.py:31
  200.1 32.0 copy-start.45
  200.1 32.0 copy-start.61
  260.8 10.8 copy-start.41
  260.8 10.8 copy-start.46
  260.8 10.8 copy-start.52
  271.7 1098.5 %reduce-scatter.10.cloned.1.call-start = ((), (), s32[]{:S(2)}) async-start(), calls=%async_computation.20 | async-start | bytes 39321600 | tf_op jit(solution)/shard_map/reduce_scatter | solution.py:25
  287.5 108.5 %copy-start.62 = (f32[8,1,256]{2,1,0:T(1,128)}, f32[8,1,256]{2,1,0:T(1,128)S(1)}, u32[]{:S(2)}) copy-start(f32[8,1,256]{2,1,0:T(1,128)S(1)} %convert_element_type.281) | copy-start | bytes 24580
  290.6 23.7 copy-start.65
  290.6 24.1 copy-start.66
  314.7 42.7 copy-start.67
  357.4 70.6 %copy-start.59 = (bf16[8,4,240]{2,1,0:T(4,128)(2,1)}, bf16[8,4,240]{2,1,0:T(4,128)(2,1)S(1)}, u32[]{:S(2)}) copy-start(bf16[8,4,240]{2,1,0:T(4,128)(2,1)S(1)} %mul.571) | copy-start | bytes 46084
  398.6 1886.8 %copy-start = (bf16[768,2048]{1,0:T(8,128)(2,1)}, bf16[768,2048]{1,0:T(8,128)(2,1)S(1)}, u32[]{:S(2)}) copy-start(bf16[768,2048]{1,0:T(8,128)(2,1)S(1)} %multiply_convert_fusion) | copy-start | bytes 9437188
  856.4 1044.4 %all-gather.28.cloned.1.call-start = ((), (), s32[]{:S(2)}) async-start(), calls=%async_computation.21 | async-start | bytes 39321600 | tf_op jit(solution)/shard_map/all_gather | solution.py:16
  1922.2 7.9 copy-start.68
  1922.2 30.9 copy-start.77
  1922.2 364.8 %all-to-all-start.1 = ((bf16[8,4,240,2048]{3,2,1,0:T(8,128)(2,1)}), bf16[8,4,240,2048]{3,2,1,0:T(8,128)(2,1)}, u32[]{:S(2)}, u32[]{:S(2)}) async-start(bf16[8,4,240,2048]{3,2,1,0:T(8,128)(2,1)} %copy.142), calls=%async_computation.2 | async-start | bytes 62914560 | tf_op jit(solution)/shard_map/all_to_all | solution.py:39
  1929.3 350.7 %all-gather.34.cloned.1.call-start = ((), (), s32[]{:S(2)}) async-start(), calls=%async_computation.33 | async-start | bytes 3932160 | tf_op jit(solution)/shard_map/all_gather | solution.py:16
  1930.0 1567.1 %reduce-scatter.12.cloned.1.call-start = ((), (), s32[]{:S(2)}) async-start(), calls=%async_computation.22 | async-start | bytes 39321600 | tf_op jit(solution)/shard_map/reduce_scatter | solution.py:25
  2287.0 143.9 %copy-start.16 = (bf16[768,2048]{1,0:T(8,128)(2,1)S(1)}, bf16[768,2048]{1,0:T(8,128)(2,1)}, u32[]{:S(2)}) copy-start(bf16[768,2048]{1,0:T(8,128)(2,1)} %all-gather.34.cloned.1.call-done) | copy-start | bytes 9437188
  2446.0 14.4 copy-start.19
  2446.2 14.2 copy-start.64
  2460.4 68.9 %copy-start.60 = (bf16[8,4,240]{2,1,0:T(4,128)(2,1)S(1)}, bf16[8,4,240]{2,1,0:T(4,128)(2,1)}, u32[]{:S(2)}) copy-start(bf16[8,4,240]{2,1,0:T(4,128)(2,1)} %copy-done.59) | copy-start | bytes 46084
  2984.2 1043.7 %all-gather.30.cloned.1.call-start = ((), (), s32[]{:S(2)}) async-start(), calls=%async_computation.23 | async-start | bytes 39321600 | tf_op jit(solution)/shard_map/all_gather | solution.py:16
  4049.2 7.2 copy-start.51
  4049.2 8.9 copy-start.42
  4049.2 8.9 copy-start.47
  4049.2 9.5 copy-start.20
  4049.2 9.5 copy-start.40
  4049.2 9.5 copy-start.75
  4049.3 347.4 %all-to-all-start.3 = ((bf16[8,4,240,2048]{3,2,1,0:T(8,128)(2,1)}), bf16[8,4,240,2048]{3,2,1,0:T(8,128)(2,1)}, u32[]{:S(2)}, u32[]{:S(2)}) async-start(bf16[8,4,240,2048]{3,2,1,0:T(8,128)(2,1)} %copy.144), calls=%async_computation.5 | async-start | bytes 62914560 | tf_op jit(solution)/shard_map/all_to_all | solution.py:39
  4056.3 340.4 %copy-start.54 = (s32[6144]{0:T(1024)S(1)}, s32[6144]{0:T(1024)}, u32[]{:S(2)}) copy-start(s32[6144]{0:T(1024)} %broadcast_clamp_fusion) | copy-start | bytes 73732
  4056.3 587.2 %reduce-scatter.14.cloned.1.call-start = ((), (), s32[]{:S(2)}) async-start(), calls=%async_computation.24 | async-start | bytes 2359296 | tf_op jit(solution)/shard_map/reduce_scatter | solution.py:313
  4540.3 20.7 copy-start.4
  4540.3 20.7 copy-start.70
  4561.0 7.8 copy-start.9
  4561.0 7.8 copy-start.17
  4561.0 7.8 copy-start.63
  4620.0 74.8 %reduce-scatter.26.cloned.1.call-start = ((), (), s32[]{:S(2)}) async-start(), calls=%async_computation.31 | async-start | bytes 147456 | tf_op jit(solution)/shard_map/reduce_scatter | solution.py:370
  4622.5 86.3 %reduce-scatter.16.cloned.1.call-start = ((), (), s32[]{:S(2)}) async-start(), calls=%async_computation.25 | async-start | bytes 2359296 | tf_op jit(solution)/shard_map/reduce_scatter | solution.py:319
  4627.3 154.5 %reduce-scatter.24.cloned.1.call-start = ((), (), s32[]{:S(2)}) async-start(), calls=%async_computation.30 | async-start | bytes 2359296 | tf_op jit(solution)/shard_map/reduce_scatter | solution.py:364
  4633.2 11.6 copy-start.29
  4633.3 11.6 copy-start.31
  4633.3 14.6 copy-start.58
  4633.3 14.6 copy-start.81
  4633.3 189.7 %reduce-scatter.18.cloned.1.call-start = ((), (), s32[]{:S(2)}) async-start(), calls=%async_computation.27 | async-start | bytes 2359296 | tf_op jit(solution)/shard_map/reduce_scatter | solution.py:355
  4654.8 188.2 %reduce-scatter.20.cloned.1.call-start = ((), (), s32[]{:S(2)}) async-start(), calls=%async_computation.28 | async-start | bytes 2359296 | tf_op jit(solution)/shard_map/reduce_scatter | solution.py:358
  4665.2 301.1 %all-reduce.9.cloned.1.call-start = ((), (), s32[]{:S(2)}) async-start(), calls=%async_computation.26 | async-start | bytes 6291456 | tf_op jit(solution)/shard_map/psum | solution.py:31
  4717.8 292.0 %reduce-scatter.22.cloned.1.call-start = ((), (), s32[]{:S(2)}) async-start(), calls=%async_computation.29 | async-start | bytes 2359296 | tf_op jit(solution)/shard_map/reduce_scatter | solution.py:361
  4717.9 20.1 copy-start.22
  4738.0 17.8 copy-start.44
  4844.8 128.7 %copy-start.76 = (bf16[2048]{0:T(1024)(128)(2,1)S(1)}, bf16[2048]{0:T(1024)(128)(2,1)}, u32[]{:S(2)}) copy-start(bf16[2048]{0:T(1024)(128)(2,1)} %get-tuple-element.307) | copy-start | bytes 12292
  (64 other events, 187.7 us)
Sparse Core Ops, SparseCore 0:
  9.9 30.5 all-gather.15
  42.4 27.8 all-gather.19
  71.9 63.4 all-gather.31
  137.1 26.5 all-gather.21
  169.3 27.2 all-gather.23
  198.6 27.2 all-gather.17
  227.7 28.1 all-gather.25
  271.8 121.0 all-reduce.6
  856.5 513.5 reduce-scatter.9
  1371.6 529.1 all-gather.27
  1931.7 62.1 all-gather.33
  2984.3 512.7 reduce-scatter.11
  3498.6 529.1 all-gather.29
  4620.1 23.3 reduce-scatter.13
  4647.2 33.3 reduce-scatter.25
  4682.7 26.0 reduce-scatter.15
  4712.2 41.2 reduce-scatter.23
  4756.7 41.2 reduce-scatter.17
  4801.6 41.3 reduce-scatter.19
  4845.2 121.0 all-reduce.8
  4969.6 40.2 reduce-scatter.21
where the time goes:
time: 5040 us; the launch traced here: 5020 us
  waiting for transfers between devices  2760 us (55%)
  blocking collectives  1110 us (22%)
  local copies, waits for them, and re-layouts  586 us (12%)
  matrix products  352 us (7%)
  other arithmetic  177 us (4%)
    all_gather x4, waiting for transfers between devices, quarter_join(): return lax.all_gather(values, 'tp', axis=3, tiled=True)  1120 us
    reduce_scatter x2, waiting for transfers between devices, share_sums(): lax.psum_scatter(values.astype(jnp.bfloat16), 'tp', scatter_dimension=3,...  1030 us
    all_to_all x2, blocking collectives, send_experts(): lax.all_to_all(values, ('fsdp', 'ctx'), split_axis=0, concat_axis=0, tile...  703 us
    all_to_all x2, waiting for transfers between devices, return_experts(): lax.all_to_all(values, ('fsdp', 'ctx'), split_axis=0, concat_axis=0, tile...  335 us
    all_gather x1, blocking collectives, on_device(): lax.all_gather(router_weight, ('fsdp', 'ctx'), axis=0, tiled=True)  326 us
    gather x1, local copies, waits for them, and re-layouts, on_device(): returned.reshape(experts * capacity, row_width)[place]  144 us
    gather x1, local copies, waits for them, and re-layouts, on_device(): back_rows.reshape(experts * capacity, full_width)[place]  144 us
    psum x2, waiting for transfers between devices, head_sums(): return lax.psum(values.astype(jnp.bfloat16), 'tp').astype(jnp.float32)  134 us
  transfers between devices with their start and end apart: 23, of which 17 were waited for; matrix products, arithmetic and copies ran while one was open for 7% of the time, Pallas kernels for 0%

commit v1 on v0

v1 whole, which is shorter than its diff:
```python
import functools

import jax
import jax.numpy as jnp
from jax import lax
from jax.experimental import pallas as pl
from jax.experimental.pallas import tpu as pltpu
from jax.sharding import PartitionSpec as P

KEY_BLOCK = 512
CHUNK = 768
SLOTS = 256
EXTRA = 128
VMEM_BYTES = 60 * 1024 * 1024


epsilon = 1e-05
rope_base = 50000.0
masked_score = -1e30
highest = lax.Precision.HIGHEST
bf16 = jnp.bfloat16
f32 = jnp.float32
ROWS = ("fsdp", "ctx")
ALL = ("fsdp", "ctx", "tp")


def doc_places(order_row, length_row):
    ends = jnp.cumsum(length_row, dtype=jnp.int32)
    passed = (order_row[:, None] >= ends[None, :]).astype(jnp.int32)
    segment = jnp.sum(passed, axis=1, dtype=jnp.int32)
    start = jnp.sum(passed * length_row[None, :], axis=1, dtype=jnp.int32)
    return (segment, order_row - start)


def rope_tables(position, head_dim):
    half = head_dim // 2
    freqs = rope_base ** (-(jnp.arange(half, dtype=jnp.float32) * (2.0 / head_dim)))
    angles = position.astype(jnp.float32)[:, None] * freqs[None, :]
    return (jnp.cos(angles)[:, None, :], jnp.sin(angles)[:, None, :])


def rotate(values, cosine, sine):
    half = values.shape[-1] // 2
    first = values[..., :half]
    second = values[..., half:]
    return jnp.concatenate(
        [first * cosine - second * sine, second * cosine + first * sine], axis=-1
    )


def rotate_back(grads, cosine, sine):
    half = grads.shape[-1] // 2
    first = grads[..., :half]
    second = grads[..., half:]
    return jnp.concatenate(
        [first * cosine + second * sine, second * cosine - first * sine], axis=-1
    )


def norm_scale(values):
    return lax.rsqrt(jnp.mean(values * values, axis=-1, keepdims=True) + epsilon)


def norm_back(incoming, values, inverse, gain):
    scaled = incoming * gain
    value_grad = inverse * (
        scaled - values * inverse * inverse * jnp.mean(scaled * values, axis=-1, keepdims=True)
    )
    return (value_grad, incoming * values * inverse)


def matmul(left, right):
    return jnp.dot(left, right, preferred_element_type=f32)


def matmul_nt(left, right):
    return lax.dot_general(left, right, (((1,), (1,)), ((), ())), preferred_element_type=f32)


def slot_rows(rank_row):
    slots = lax.broadcasted_iota(jnp.int32, (SLOTS, rank_row.shape[1]), 0)
    return slots == rank_row


def slot_columns(rank_column):
    slots = lax.broadcasted_iota(jnp.int32, (rank_column.shape[0], SLOTS), 1)
    return jnp.where(slots == rank_column, 1.0, 0.0).astype(bf16)


def as_one_hot(mask):
    return jnp.where(mask, 1.0, 0.0).astype(bf16)


def select_grads(rank_ref, grad_ref, down_ref, rows_ref, product_ref):
    expert = pl.program_id(1)
    rows = matmul(as_one_hot(slot_rows(rank_ref[...])), grad_ref[...]).astype(bf16)
    rows_ref[...] = rows
    product_ref[...] = matmul_nt(rows, down_ref[expert])


def expert_pass(
    first_ref,
    rank_ref,
    column_ref,
    token_ref,
    product_ref,
    gate_ref,
    up_ref,
    rows_ref,
    hidden_ref,
    gate_grad_ref,
    up_grad_ref,
    route_ref,
    back_ref,
    held_ref,
):
    expert = pl.program_id(1)
    local = pl.num_programs(1)
    width = rows_ref.shape[1]
    mask = slot_rows(rank_ref[...])
    picked = matmul(as_one_hot(mask), token_ref[...])
    rows = picked[:, :width].astype(bf16)
    rows_ref[...] = rows
    lane = lax.broadcasted_iota(jnp.int32, (SLOTS, EXTRA), 1)
    mine = jnp.logical_and(lax.rem(lane, 32) == first_ref[0] + expert, lane < 96)
    gate = jnp.sum(jnp.where(mine, picked[:, width:], 0.0), axis=1, keepdims=True)
    gate_act = matmul(rows, gate_ref[expert])
    up_act = matmul(rows, up_ref[expert])
    sigmoid_g = 1.0 / (1.0 + jnp.exp(-gate_act))
    silu_g = gate_act * sigmoid_g
    hidden = silu_g * up_act
    hidden_ref[...] = (gate * hidden).astype(bf16)
    product = product_ref[...]
    route = jnp.sum(hidden.astype(bf16).astype(f32) * product, axis=1, keepdims=True)
    route_ref[...] = jnp.sum(jnp.where(mask, route, 0.0), axis=0, keepdims=True)
    hidden_grad = gate * product
    gate_grad = (
        hidden_grad * up_act * sigmoid_g * (1.0 + gate_act * (1.0 - sigmoid_g))
    ).astype(bf16)
    up_grad = (hidden_grad * silu_g).astype(bf16)
    gate_grad_ref[...] = gate_grad
    up_grad_ref[...] = up_grad
    back = matmul_nt(gate_grad, gate_ref[expert]) + matmul_nt(up_grad, up_ref[expert])
    held_ref[pl.ds(pl.multiple_of(expert * SLOTS, SLOTS), SLOTS), :] = back.astype(bf16)

    @pl.when(expert == local - 1)
    def _():
        columns = column_ref[...]
        places = jnp.concatenate(
            [slot_columns(columns[:, e : e + 1]) for e in range(columns.shape[1])], axis=1
        )
        back_ref[...] = matmul(places, held_ref[...]).astype(bf16)


def expert_sums(column_ref, hidden_ref, down_ref, out_ref):
    columns = column_ref[...]
    dense = [
        matmul(slot_columns(columns[:, e : e + 1]), hidden_ref[e]).astype(bf16)
        for e in range(columns.shape[1])
    ]
    out_ref[...] = matmul(jnp.concatenate(dense, axis=1), down_ref[...]).astype(bf16)


def params(dims):
    return pltpu.CompilerParams(
        dimension_semantics=("arbitrary",) * dims, vmem_limit_bytes=VMEM_BYTES
    )


def once(shape):
    return pl.BlockSpec(
        shape, lambda *ids: (0,) * len(shape), pipeline_mode=pl.Buffered(1)
    )


def run_select_grads(rank_rows, grad_all, down_weight):
    chunks, local = rank_rows.shape[:2]
    hidden, width = down_weight.shape[1:]
    slots = chunks * local * SLOTS
    return pl.pallas_call(
        select_grads,
        grid=(chunks, local),
        in_specs=[
            pl.BlockSpec((None, None, 1, CHUNK), lambda g, e: (g, e, 0, 0)),
            pl.BlockSpec((CHUNK, width), lambda g, e: (g, 0)),
            once(down_weight.shape),
        ],
        out_specs=[
            pl.BlockSpec((None, None, SLOTS, width), lambda g, e: (g, e, 0, 0)),
            pl.BlockSpec((None, None, SLOTS, hidden), lambda g, e: (g, e, 0, 0)),
        ],
        out_shape=[
            jax.ShapeDtypeStruct((chunks, local, SLOTS, width), bf16),
            jax.ShapeDtypeStruct((chunks, local, SLOTS, hidden), f32),
        ],
        compiler_params=params(2),
        cost_estimate=pl.CostEstimate(
            flops=2 * slots * width * (CHUNK + hidden),
            bytes_accessed=2 * (chunks * CHUNK + slots) * width,
            transcendentals=0,
        ),
        name="select_grads",
    )(rank_rows, grad_all, down_weight)


def run_expert_pass(first, rank_rows, rank_columns, token_all, product, gate_weight, up_weight):
    chunks, local = rank_rows.shape[:2]
    width, hidden = gate_weight.shape[1:]
    slots = chunks * local * SLOTS
    per_expert = lambda g, e: (g, e, 0, 0)
    narrow = pl.BlockSpec((None, None, SLOTS, hidden), per_expert)
    return pl.pallas_call(
        expert_pass,
        grid=(chunks, local),
        in_specs=[
            pl.BlockSpec(memory_space=pltpu.SMEM),
            pl.BlockSpec((None, None, 1, CHUNK), per_expert),
            pl.BlockSpec((None, CHUNK, local), lambda g, e: (g, 0, 0)),
            pl.BlockSpec((CHUNK, width + EXTRA), lambda g, e: (g, 0)),
            narrow,
            once(gate_weight.shape),
            once(up_weight.shape),
        ],
        out_specs=[
            pl.BlockSpec((None, None, SLOTS, width), per_expert),
            narrow,
            narrow,
            narrow,
            pl.BlockSpec((None, None, 1, CHUNK), per_expert),
            pl.BlockSpec((CHUNK, width), lambda g, e: (g, 0)),
        ],
        out_shape=[
            jax.ShapeDtypeStruct((chunks, local, SLOTS, width), bf16),
            jax.ShapeDtypeStruct((chunks, local, SLOTS, hidden), bf16),
            jax.ShapeDtypeStruct((chunks, local, SLOTS, hidden), bf16),
            jax.ShapeDtypeStruct((chunks, local, SLOTS, hidden), bf16),
            jax.ShapeDtypeStruct((chunks, local, 1, CHUNK), f32),
            jax.ShapeDtypeStruct((chunks * CHUNK, width), bf16),
        ],
        scratch_shapes=[pltpu.VMEM((local * SLOTS, width), bf16)],
        compiler_params=params(2),
        cost_estimate=pl.CostEstimate(
            flops=2 * slots * width * (2 * CHUNK + 4 * hidden),
            bytes_accessed=2 * (2 * chunks * CHUNK + slots) * width,
            transcendentals=slots * hidden,
        ),
        name="expert_pass",
    )(first, rank_rows, rank_columns, token_all, product, gate_weight, up_weight)


def run_expert_sums(rank_columns, hidden_rows, down_weight):
    chunks, local, unused, hidden = hidden_rows.shape
    width = down_weight.shape[2]
    flat = down_weight.reshape(local * hidden, width)
    return pl.pallas_call(
        expert_sums,
        grid=(chunks,),
        in_specs=[
            pl.BlockSpec((None, CHUNK, local), lambda g: (g, 0, 0)),
            pl.BlockSpec((None, local, SLOTS, hidden), lambda g: (g, 0, 0, 0)),
            once(flat.shape),
        ],
        out_specs=pl.BlockSpec((CHUNK, width), lambda g: (g, 0)),
        out_shape=jax.ShapeDtypeStruct((chunks * CHUNK, width), bf16),
        compiler_params=params(1),
        cost_estimate=pl.CostEstimate(
            flops=2 * chunks * CHUNK * local * hidden * (width + SLOTS),
            bytes_accessed=2 * chunks * CHUNK * width,
            transcendentals=0,
        ),
        name="expert_sums",
    )(rank_columns, hidden_rows, flat)


def attend(query_b, seg_b, key_blocks, value_blocks, seg_blocks, scale):
    tok_count, heads, head_dim = query_b.shape

    def forward_step(carry, pieces):
        run_max, run_sum, accum = carry
        key_blk, value_blk, seg_blk = pieces
        scores = (
            jnp.einsum("qhd,khd->hqk", query_b, key_blk, preferred_element_type=f32) * scale
        )
        allowed = (seg_b[:, None] == seg_blk[None, :])[None]
        scores = jnp.where(allowed, scores, masked_score)
        new_max = jnp.maximum(run_max, jnp.max(scores, axis=-1))
        probs = jnp.where(allowed, jnp.exp(scores - new_max[..., None]), 0.0)
        factor = jnp.exp(run_max - new_max)
        run_sum = run_sum * factor + jnp.sum(probs, axis=-1)
        accum = accum * factor[..., None] + jnp.einsum(
            "hqk,khd->hqd", probs.astype(bf16), value_blk, preferred_element_type=f32
        )
        return ((new_max, run_sum, accum), None)

    start_carry = (
        jnp.full((heads, tok_count), masked_score, f32),
        jnp.zeros((heads, tok_count), f32),
        jnp.zeros((heads, tok_count, head_dim), f32),
    )
    (run_max, run_sum, accum), unused = lax.scan(
        forward_step, start_carry, (key_blocks, value_blocks, seg_blocks)
    )
    log_total = run_max + jnp.log(run_sum)
    return (jnp.transpose(accum / run_sum[..., None], (1, 0, 2)), log_total)


def attend_back(
    query_b, seg_b, key_blocks, value_blocks, seg_blocks, scale, attn_grad, log_total, delta
):
    tok_count, heads, head_dim = query_b.shape

    def backward_step(query_accum, pieces):
        key_blk, value_blk, seg_blk = pieces
        scores = (
            jnp.einsum("qhd,khd->hqk", query_b, key_blk, preferred_element_type=f32) * scale
        )
        allowed = (seg_b[:, None] == seg_blk[None, :])[None]
        probs = jnp.where(allowed, jnp.exp(scores - log_total[..., None]), 0.0)
        prob_grad = jnp.einsum("qhd,khd->hqk", attn_grad, value_blk, preferred_element_type=f32)
        score_grad = (probs * (prob_grad - delta[..., None])).astype(bf16)
        query_accum = (
            query_accum
            + jnp.einsum("hqk,khd->qhd", score_grad, key_blk, preferred_element_type=f32) * scale
        )
        key_blk_grad = (
            jnp.einsum("hqk,qhd->khd", score_grad, query_b, preferred_element_type=f32) * scale
        )
        value_blk_grad = jnp.einsum(
            "hqk,qhd->khd", probs.astype(bf16), attn_grad, preferred_element_type=f32
        )
        return (query_accum, (key_blk_grad.astype(bf16), value_blk_grad.astype(bf16)))

    return lax.scan(
        backward_step,
        jnp.zeros((tok_count, heads, head_dim), f32),
        (key_blocks, value_blocks, seg_blocks),
    )


def split_three(values):
    high = values.astype(bf16)
    rest = values - high.astype(f32)
    middle = rest.astype(bf16)
    return (high, middle, (rest - middle.astype(f32)).astype(bf16))


def on_device(
    layer_input,
    token_order,
    doc_lengths,
    expert_routes,
    attn_gain,
    query_weight,
    key_weight,
    value_weight,
    query_gain,
    key_gain,
    out_weight,
    moe_gain,
    router_weight,
    gate_weight,
    up_weight,
    down_weight,
    out_grad,
):
    tp_index = lax.axis_index("tp")
    ctx_size = lax.axis_size("ctx")
    fc_size = lax.axis_size("fsdp") * ctx_size
    fc_index = lax.axis_index("fsdp") * ctx_size + lax.axis_index("ctx")
    tok_count, quarter = layer_input.shape
    share = tok_count // lax.axis_size("tp")
    head_dim = query_gain.shape[0]
    head_width = query_weight.shape[1]
    heads = head_width // head_dim
    scale = head_dim ** (-0.5)
    experts = router_weight.shape[1]
    top = expert_routes.shape[1]
    local_experts = gate_weight.shape[0]
    capacity = tok_count * top * 5 // (4 * experts)
    own_rows = lambda values: lax.dynamic_slice_in_dim(values, tp_index * share, share, 0)
    own_width = lambda values: lax.dynamic_slice_in_dim(values, tp_index * quarter, quarter, 1)

    packed = jnp.concatenate(
        [
            query_weight,
            key_weight,
            value_weight,
            router_weight,
            attn_gain[:, None],
            moe_gain[:, None],
            jnp.zeros((attn_gain.shape[0], EXTRA - experts - 2), bf16),
        ],
        axis=1,
    )
    full = lax.all_gather(packed, ROWS, axis=0, tiled=True)
    full_out = lax.all_gather(out_weight.T, ROWS, axis=0, tiled=True)
    side = 3 * head_width
    qkv_weight = full[:, :side]
    full_router = full[:, side : side + experts]
    attn_gain_f = full[:, side + experts].astype(f32)
    moe_gain_f = full[:, side + experts + 1].astype(f32)
    input_f = lax.all_gather(layer_input, "tp", axis=1, tiled=True).astype(f32)
    width = input_f.shape[1]

    expert_ids = jnp.arange(experts, dtype=jnp.int32)
    named = jnp.any(expert_routes[:, :, None] == expert_ids[None, None, :], axis=1)
    earlier = jnp.tri(tok_count, tok_count, -1, dtype=bf16)
    before = matmul(earlier, named.astype(bf16))
    first_slot = (lax.rem(fc_index, CHUNK // tok_count) * capacity).astype(f32)
    ranks = jnp.where(named, before + first_slot, -1.0).astype(bf16)
    grad_rows_b = lax.all_gather(out_grad, "tp", axis=1, tiled=True)
    grad_packed = jnp.concatenate(
        [grad_rows_b, ranks, jnp.zeros((tok_count, EXTRA - experts), bf16)], axis=1
    )
    grad_all = lax.all_gather(grad_packed, ROWS, axis=0, tiled=True)
    chunks = grad_all.shape[0] // CHUNK
    first_expert = fc_index * local_experts
    local_ranks = lax.dynamic_slice_in_dim(
        grad_all[:, width:], first_expert, local_experts, 1
    ).astype(jnp.int32)
    rank_columns = local_ranks.reshape(chunks, CHUNK, local_experts)
    rank_rows = jnp.transpose(rank_columns, (0, 2, 1))[:, :, None, :]

    segment, position = doc_places(token_order[0], doc_lengths[0])
    cosine, sine = rope_tables(position, head_dim)
    inverse_one = norm_scale(input_f)
    normed = (input_f * inverse_one * attn_gain_f).astype(bf16)
    qkv = matmul(normed, qkv_weight)
    query_pre = qkv[:, :head_width].reshape(tok_count, heads, head_dim)
    key_pre = qkv[:, head_width : 2 * head_width].reshape(tok_count, heads, head_dim)
    value_b = qkv[:, 2 * head_width :].astype(bf16)
    query_inv = norm_scale(query_pre)
    key_inv = norm_scale(key_pre)
    query_b = rotate(query_pre * query_inv * query_gain, cosine, sine).astype(bf16)
    key_b = rotate(key_pre * key_inv * key_gain, cosine, sine).astype(bf16)
    seg_b = segment.astype(bf16)
    group = lax.all_gather(
        jnp.concatenate(
            [
                key_b.reshape(tok_count, head_width),
                value_b,
                jnp.broadcast_to(seg_b[:, None], (tok_count, EXTRA)),
            ],
            axis=1,
        ),
        "ctx",
        axis=0,
        tiled=True,
    )
    blocks = group.shape[0] // KEY_BLOCK
    key_blocks = group[:, :head_width].reshape(blocks, KEY_BLOCK, heads, head_dim)
    value_blocks = group[:, head_width : 2 * head_width].reshape(
        blocks, KEY_BLOCK, heads, head_dim
    )
    seg_blocks = group[:, 2 * head_width].reshape(blocks, KEY_BLOCK)
    attn_heads, log_total = attend(query_b, seg_b, key_blocks, value_blocks, seg_blocks, scale)
    attn_b = attn_heads.reshape(tok_count, head_width).astype(bf16)
    attn_part = matmul_nt(attn_b, full_out).astype(bf16)
    attn_out = lax.psum_scatter(attn_part, "tp", scatter_dimension=0, tiled=True).astype(f32)
    resid = own_rows(input_f) + attn_out
    inverse_two = norm_scale(resid)
    moe_in = (resid * inverse_two * moe_gain_f).astype(bf16)
    logits = matmul(moe_in, full_router)
    own_named = own_rows(named)
    chosen = jnp.where(own_named, logits, -jnp.inf)
    gates = jax.nn.softmax(chosen, axis=-1)
    token_all = lax.all_gather(
        jnp.concatenate(
            [moe_in, *split_three(gates), jnp.zeros((share, EXTRA - 3 * experts), bf16)], axis=1
        ),
        ALL,
        axis=0,
        tiled=True,
    )

    grad_slots, product = run_select_grads(rank_rows, grad_all, down_weight)
    token_slots, hidden_rows, gate_act_grad, up_act_grad, route_part, back_part = run_expert_pass(
        first_expert.reshape(1), rank_rows, rank_columns, token_all, product, gate_weight, up_weight
    )
    back_sum = lax.psum_scatter(back_part, ROWS, scatter_dimension=0, tiled=True)
    route_sum = lax.psum(route_part, "tp")
    route_sum = jnp.transpose(route_sum[:, :, 0, :], (1, 0, 2)).reshape(
        local_experts, fc_size, tok_count
    )
    gate_grad = lax.all_to_all(
        jnp.transpose(route_sum, (1, 0, 2)), ROWS, split_axis=0, concat_axis=0, tiled=True
    ).reshape(experts, tok_count)
    out_part = run_expert_sums(rank_columns, hidden_rows, down_weight)
    grad_down = jnp.einsum(
        "gesf,gesd->efd", hidden_rows, grad_slots, preferred_element_type=f32
    )
    grad_gate = jnp.einsum(
        "gesd,gesf->edf", token_slots, gate_act_grad, preferred_element_type=f32
    )
    grad_up = jnp.einsum("gesd,gesf->edf", token_slots, up_act_grad, preferred_element_type=f32)

    own_tokens = lax.dynamic_slice_in_dim(token_all, fc_index * tok_count, tok_count, 0)
    parts = own_tokens[:, width : width + 3 * experts].astype(f32)
    all_gates = parts[:, :experts] + parts[:, experts : 2 * experts] + parts[:, 2 * experts :]
    gate_grad = gate_grad.T
    logit_grad = all_gates * (
        gate_grad - jnp.sum(all_gates * gate_grad, axis=-1, keepdims=True)
    )
    grad_router = lax.dot_general(
        own_tokens[:, :width].astype(f32),
        logit_grad,
        (((0,), (0,)), ((), ())),
        precision=highest,
    )
    own_logit_grad = own_rows(logit_grad)
    router_back = lax.dot_general(
        own_logit_grad, full_router.astype(f32), (((1,), (1,)), ((), ())), precision=highest
    )
    moe_in_grad = (
        lax.psum_scatter(back_sum, "tp", scatter_dimension=0, tiled=True).astype(f32) + router_back
    )
    resid_norm_grad, gain_terms = norm_back(moe_in_grad, resid, inverse_two, moe_gain_f)
    grad_moe_gain = jnp.sum(gain_terms, axis=0)
    resid_grad = own_rows(grad_rows_b).astype(f32) + resid_norm_grad
    resid_grad_b = lax.all_gather(resid_grad.astype(bf16), "tp", axis=0, tiled=True)

    out_sum = lax.psum_scatter(out_part, ROWS, scatter_dimension=0, tiled=True)
    out_sum = lax.psum_scatter(out_sum, "tp", scatter_dimension=0, tiled=True).astype(f32)
    layer_output = lax.all_to_all(
        (resid + out_sum).astype(bf16), "tp", split_axis=1, concat_axis=0, tiled=True
    )

    grad_out = lax.dot_general(
        resid_grad_b, attn_b, (((0,), (0,)), ((), ())), preferred_element_type=f32
    )
    attn_grad = matmul(resid_grad_b, full_out).astype(bf16).reshape(tok_count, heads, head_dim)
    delta = jnp.transpose(jnp.sum(attn_grad.astype(f32) * attn_heads, axis=-1))
    query_rot_grad, (key_stack, value_stack) = attend_back(
        query_b, seg_b, key_blocks, value_blocks, seg_blocks, scale, attn_grad, log_total, delta
    )
    group_rows = blocks * KEY_BLOCK
    group_grad = lax.psum_scatter(
        jnp.concatenate(
            [
                key_stack.reshape(group_rows, head_width),
                value_stack.reshape(group_rows, head_width),
            ],
            axis=1,
        ),
        "ctx",
        scatter_dimension=0,
        tiled=True,
    )
    key_rot_grad = group_grad[:, :head_width].astype(f32).reshape(tok_count, heads, head_dim)
    query_pre_grad, query_gain_terms = norm_back(
        rotate_back(query_rot_grad, cosine, sine), query_pre, query_inv, query_gain
    )
    key_pre_grad, key_gain_terms = norm_back(
        rotate_back(key_rot_grad, cosine, sine), key_pre, key_inv, key_gain
    )
    qkv_grad = jnp.concatenate(
        [
            query_pre_grad.reshape(tok_count, head_width).astype(bf16),
            key_pre_grad.reshape(tok_count, head_width).astype(bf16),
            group_grad[:, head_width:],
        ],
        axis=1,
    )
    normed_part = matmul_nt(qkv_grad, qkv_weight)
    normed_grad = lax.psum_scatter(
        normed_part.astype(bf16), "tp", scatter_dimension=1, tiled=True
    ).astype(f32)
    attn_terms = jnp.sum(normed_part * input_f * inverse_one, axis=0)
    along = jnp.sum(normed_part * input_f * attn_gain_f, axis=1)
    along = lax.psum(along, "tp")[:, None] / width
    input_quarter = layer_input.astype(f32)
    gain_quarter = lax.dynamic_slice_in_dim(attn_gain_f, tp_index * quarter, quarter, 0)
    grad_input = own_width(resid_grad_b).astype(f32) + inverse_one * (
        normed_grad * gain_quarter - input_quarter * inverse_one * inverse_one * along
    )
    grad_qkv = lax.dot_general(
        normed, qkv_grad, (((0,), (0,)), ((), ())), preferred_element_type=f32
    )
    owned_out = lax.psum_scatter(
        jnp.concatenate(
            [grad_out, grad_router, jnp.zeros((width, EXTRA - experts), f32)], axis=1
        ).astype(bf16),
        ROWS,
        scatter_dimension=0,
        tiled=True,
    ).astype(f32)
    owned_qkv = lax.psum_scatter(
        grad_qkv.astype(bf16), ROWS, scatter_dimension=0, tiled=True
    ).astype(f32)
    gains = lax.psum(
        jnp.concatenate(
            [
                attn_terms,
                grad_moe_gain,
                jnp.sum(query_gain_terms, axis=(0, 1)),
                jnp.sum(key_gain_terms, axis=(0, 1)),
            ]
        ),
        ALL,
    )
    owned_gain = attn_gain.shape[0]
    own_gain = lambda at: lax.dynamic_slice_in_dim(
        gains, at * width + fc_index * owned_gain, owned_gain, 0
    )
    return (
        layer_output,
        grad_input,
        own_gain(0),
        owned_qkv[:, :head_width],
        owned_qkv[:, head_width : 2 * head_width],
        owned_qkv[:, 2 * head_width :],
        gains[2 * width : 2 * width + head_dim],
        gains[2 * width + head_dim :],
        owned_out[:, :head_width].T,
        own_gain(1),
        owned_out[:, head_width : head_width + experts],
        grad_gate,
        grad_up,
        grad_down,
    )


def solution(mesh):
    in_specs = (
        P(("fsdp", "ctx"), "tp"),
        P("fsdp", "ctx"),
        P("fsdp", None),
        P(("fsdp", "ctx"), None),
        P(("fsdp", "ctx")),
        P(("fsdp", "ctx"), "tp"),
        P(("fsdp", "ctx"), "tp"),
        P(("fsdp", "ctx"), "tp"),
        P(),
        P(),
        P("tp", ("fsdp", "ctx")),
        P(("fsdp", "ctx")),
        P(("fsdp", "ctx"), None),
        P(("fsdp", "ctx"), None, "tp"),
        P(("fsdp", "ctx"), None, "tp"),
        P(("fsdp", "ctx"), "tp", None),
        P(("fsdp", "ctx"), "tp"),
    )
    out_specs = (
        P(("fsdp", "ctx"), "tp"),
        P(("fsdp", "ctx"), "tp"),
        P(("fsdp", "ctx")),
        P(("fsdp", "ctx"), "tp"),
        P(("fsdp", "ctx"), "tp"),
        P(("fsdp", "ctx"), "tp"),
        P(),
        P(),
        P("tp", ("fsdp", "ctx")),
        P(("fsdp", "ctx")),
        P(("fsdp", "ctx"), None),
        P(("fsdp", "ctx"), None, "tp"),
        P(("fsdp", "ctx"), None, "tp"),
        P(("fsdp", "ctx"), "tp", None),
    )
    return jax.shard_map(
        on_device, mesh=mesh, in_specs=in_specs, out_specs=out_specs, check_vma=False
    )
```

time: 5040 us -> 1640 us (0.33)
  waiting for transfers between devices: 2760 us -> 1020 us
  blocking collectives: 1110 us -> 48.5 us
  local copies, waits for them, and re-layouts: 586 us -> 87.6 us
  Pallas kernels: 0 us -> 207 us
  matrix products: 352 us -> 173 us
  other arithmetic: 177 us -> 64.9 us
    all_gather x10 -> x8, waiting for transfers between devices: 1210 us -> 478 us  [the longest x1 129 us: on_device(): grad_all = lax.all_gather(grad_packed, ROWS, axis=0, tiled=True)]
    all_to_all x2 -> x0, blocking collectives: 703 us -> none  [send_experts(): lax.all_to_all(values, ('fsdp', 'ctx'), split_axis=0, concat_axis=0, tile...]
    reduce_scatter x9, waiting for transfers between devices: 1070 us -> 478 us  [the longest x1 160 us: on_device(): out_sum = lax.psum_scatter(out_part, ROWS, scatter_dimension=0, tiled=True)]
    gather x4 -> x0, local copies, waits for them, and re-layouts: 386 us -> none  [the longest x1 144 us: on_device(): returned.reshape(experts * capacity, row_width)[place]]
    all_gather x4 -> x0, blocking collectives: 358 us -> none  [the longest x1 326 us: on_device(): lax.all_gather(router_weight, ('fsdp', 'ctx'), axis=0, tiled=True)]
    all_to_all x2, waiting for transfers between devices: 335 us -> 23.8 us  [the longest x1 20.4 us: on_device(): lax.all_to_all((resid + out_sum).astype(bf16), 'tp', split_axis=1, concat...]
    pallas_call x0 -> x3, Pallas kernels: none -> 207 us  [the longest x1 115 us: run_expert_pass(): pl.pallas_call(expert_pass, grid=(chunks, local), in_specs=[pl.BlockSpec(...]
    dot_general x48 -> x34, matrix products: 352 us -> 173 us  [the longest x1 19.7 us: on_device(): jnp.einsum('gesd,gesf->edf', token_slots, up_act_grad, preferred_element_...]
  transfers between devices with their start and end apart: 23 -> 20, of which waited for: 17 -> 17; matrix products, arithmetic and copies ran while one was open for 7% -> 13% of each run, Pallas kernels for 0% -> 6%
where the time goes in v1:
time: 1640 us; the launch traced here: 1630 us
  waiting for transfers between devices  1020 us (62%)
  Pallas kernels  207 us (13%)
  matrix products  173 us (11%)
  local copies, waits for them, and re-layouts  87.6 us (5%)
  other arithmetic  64.9 us (4%)
  blocking collectives  48.5 us (3%)
    reduce_scatter x1, waiting for transfers between devices, on_device(): out_sum = lax.psum_scatter(out_part, ROWS, scatter_dimension=0, tiled=True)  160 us
    all_gather x1, waiting for transfers between devices, on_device(): grad_all = lax.all_gather(grad_packed, ROWS, axis=0, tiled=True)  129 us
    reduce_scatter x1, waiting for transfers between devices, on_device(): lax.psum_scatter(back_part, ROWS, scatter_dimension=0, tiled=True)  117 us
    pallas_call x1, Pallas kernels, run_expert_pass(): pl.pallas_call(expert_pass, grid=(chunks, local), in_specs=[pl.BlockSpec(...  115 us
    all_gather x1, waiting for transfers between devices, on_device(): lax.all_gather(jnp.concatenate([moe_in, *split_three(gates), jnp.zeros((s...  103 us
    all_gather x1, waiting for transfers between devices, on_device(): lax.all_gather(resid_grad.astype(bf16), 'tp', axis=0, tiled=True)  62.3 us
    all_gather x1, waiting for transfers between devices, on_device(): input_f = lax.all_gather(layer_input, 'tp', axis=1, tiled=True).astype(f32)  62.1 us
    reduce_scatter x1, waiting for transfers between devices, on_device(): lax.psum_scatter(out_sum, 'tp', scatter_dimension=0, tiled=True).astype(f32)  59 us
  transfers between devices with their start and end apart: 20, of which 17 were waited for; matrix products, arithmetic and copies ran while one was open for 13% of the time, Pallas kernels for 6%

profile of v1, /device:TPU:0, one launch (start us, length us, event | category | flops | bytes accessed | tf_op | source)
XLA Modules:
  0.0 1627.0 jit_solution(13193531050124749726)
XLA Ops:
  13.7 62.1 %all-gather.9.cloned.1.call-done = bf16[768,2048]{1,0:T(8,128)(2,1)} async-done(((bf16[768,512]{1,0:T(8,128)(2,1)}), bf16[768,2048]{1,0:T(8,128)(2,1)}) %all-gather.9.cloned.1.call-update) | async-done | bytes 3145744 | tf_op jit(solution)/shard_map/all_gather | solution.py:402
  75.8 2.7 multiply_reduce_fusion.2
  78.5 46.2 %all-gather.11.cloned.1.call-done = bf16[2048,1664]{1,0:T(8,128)(2,1)} async-done(((bf16[256,1664]{1,0:T(8,128)(2,1)}), bf16[2048,1664]{1,0:T(8,128)(2,1)}) %all-gather.11.cloned.1.call-update) | async-done | bytes 6815760 | tf_op jit(solution)/shard_map/all_gather | solution.py:395
  126.7 7.2 fusion.47
  153.9 47.7 %all-gather.13.cloned.1.call-done = bf16[1536,1152]{1,0:T(8,128)(2,1)} async-done(((bf16[768,1152]{1,0:T(8,128)(2,1)}), bf16[1536,1152]{1,0:T(8,128)(2,1)}) %all-gather.13.cloned.1.call-update) | async-done | bytes 3538960 | tf_op jit(solution)/shard_map/all_gather | solution.py:437
  202.7 3.2 fusion.85
  209.5 3.5 reshape.319
  213.0 2.8 copy.252
  215.8 40.9 %while.30 = (s32[]{:T(128)}, f32[4,768]{1,0:T(4,128)S(1)}, f32[4,768]{1,0:T(4,128)S(1)}, f32[4,768,128]{2,1,0:T(8,128)}, bf16[768]{0:T(1024)(128)(2,1)S(1)}, /*i...) while((s32[]{:T(128)}, f32[4,768]{1,0:T(4,128)S(1)}, ...), condition=%wide.region_9.10_spmd.clone, body=%wide.region_6.9_spmd.clone.sunk | while | flops 827341824 | bytes 50795176 | solution.py:300
  216.2 3.9 fusion.136
  220.1 4.8 fusion.137
  225.0 4.5 fusion.139
  229.8 3.9 fusion.136
  233.8 4.5 fusion.137
  238.4 4.8 fusion.139
  243.5 3.9 fusion.136
  247.4 4.5 fusion.137
  252.1 4.7 fusion.139
  256.8 3.9 copy.253
  262.3 5.3 convolution_convert_fusion.1
  269.3 27.1 %all-gather.17.cloned.1.call-done = bf16[768,2048]{1,0:T(8,128)(2,1)} async-done(((bf16[768,512]{1,0:T(8,128)(2,1)}), bf16[768,2048]{1,0:T(8,128)(2,1)}) %all-gather.17.cloned.1.call-update) | async-done | bytes 3145744 | tf_op jit(solution)/shard_map/all_gather | solution.py:411
  296.5 6.0 concatenate.47
  304.8 3.5 convert_element_type.163
  308.4 49.2 %reduce-scatter.10.cloned.1.call-done = bf16[192,2048]{1,0:T(8,128)(2,1)} async-done(((bf16[768,2048]{1,0:T(8,128)(2,1)}), bf16[192,2048]{1,0:T(8,128)(2,1)}) %reduce-scatter.10.cloned.1.call-update) | async-done | bytes 786448 | tf_op jit(solution)/shard_map/reduce_scatter | solution.py:459
  363.3 128.7 %all-gather.19.cloned.1.call-done.grad_ref = bf16[6144,2176]{1,0:T(8,128)(2,1)} async-done(((bf16[768,2176]{1,0:T(8,128)(2,1)}), bf16[6144,2176]{1,0:T(8,128)(2,1)}) %all-gather.19.cloned.1.call-update) | async-done | bytes 26738704 | tf_op jit(solution)/shard_map/all_gather | solution.py:415
  498.0 55.8 %select_grads.1 = (bf16[8,4,256,2048]{3,2,1,0:T(8,128)(2,1)}, f32[8,4,256,256]{3,2,1,0:T(8,128)}) custom-call(s32[8,4,1,768]{3,2,1,0:T(1,128)} %copy.260.rank_ref, bf16[6144,2176]{1,0:T(8,128)(2,1)} %all-gather.19.cloned.1.call-done.grad_ref, bf16[4,256,2048]{2,1,0:T(8,128)(2,1)} %down_ref.1), custom_call_target="tpu_custom_call" | custom-call | flops 34359738368 | bytes 58720256 | tf_op jit(solution)/shard_map/select_grads/pallas_call | solution.py:180
  553.8 103.4 %all-gather.21.cloned.1.call-done.token_ref = bf16[6144,2176]{1,0:T(8,128)(2,1)} async-done(((bf16[192,2176]{1,0:T(8,128)(2,1)}), bf16[6144,2176]{1,0:T(8,128)(2,1)}) %all-gather.21.cloned.1.call-update) | async-done | bytes 26738704 | tf_op jit(solution)/shard_map/all_gather | solution.py:467
  657.2 114.8 %expert_pass.1 = (bf16[8,4,256,2048]{3,2,1,0:T(8,128)(2,1)}, bf16[8,4,256,256]{3,2,1,0:T(8,128)(2,1)}, bf16[8,4,256,256]{3,2,1,0:T(8,128)(2,1)}, bf16[8,4,256,25...) custom-call(s32[1]{0:T(128)} %bitcast.8.first_ref, s32[8,4,1,768]{3,2,1,0:T(1,128)} %copy.260.rank_ref, ...), custom_call_target="tpu_custom_call" | custom-call | flops 85899345920 | bytes 83886080 | tf_op jit(solution)/shard_map/expert_pass/pallas_call | solution.py:212
  772.0 36.8 %expert_sums.1 = bf16[6144,2048]{1,0:T(8,128)(2,1)} custom-call(s32[8,768,4]{2,1,0:T(8,128)} %convert.33.column_ref, bf16[8,4,256,256]{3,2,1,0:T(8,128)(2,1)} %get-tuple-element.138.hidden_ref, bf16[1024,2048]{1,0:T(8,128)(2,1)} %bitcast.219), custom_call_target="tpu_custom_call" | custom-call | flops 28991029248 | bytes 25165824 | tf_op jit(solution)/shard_map/expert_sums/pallas_call | solution.py:255
  810.5 116.7 %reduce-scatter.16.cloned.1.call-done = bf16[768,2048]{1,0:T(8,128)(2,1)} async-done(((bf16[6144,2048]{1,0:T(8,128)(2,1)}), bf16[768,2048]{1,0:T(8,128)(2,1)}) %reduce-scatter.16.cloned.1.call-update) | async-done | bytes 3145744 | tf_op jit(solution)/shard_map/reduce_scatter | solution.py:480
  927.2 160.3 %reduce-scatter.12.cloned.1.call-done = bf16[768,2048]{1,0:T(8,128)(2,1)} async-done(((bf16[6144,2048]{1,0:T(8,128)(2,1)}), bf16[768,2048]{1,0:T(8,128)(2,1)}) %reduce-scatter.12.cloned.1.call-update) | async-done | bytes 3145744 | tf_op jit(solution)/shard_map/reduce_scatter | solution.py:522
  1087.6 37.2 %all-reduce.2.cloned.1.call-done = f32[8,4,768]{2,1,0:T(4,128)} async-done(((f32[8,4,768]{2,1,0:T(4,128)}), f32[8,4,768]{2,1,0:T(4,128)}) %all-reduce.2.cloned.1.call-update) | async-done | bytes 98320 | tf_op jit(solution)/shard_map/psum | solution.py:481
  1124.7 3.6 all-to-all-start.1
  1129.8 3.3 all-to-all-done.1
  1134.1 52.8 %reduce-scatter.18.cloned.1.call-done = bf16[192,2048]{1,0:T(8,128)(2,1)} async-done(((bf16[768,2048]{1,0:T(8,128)(2,1)}), bf16[192,2048]{1,0:T(8,128)(2,1)}) %reduce-scatter.18.cloned.1.call-update) | async-done | bytes 786448 | tf_op jit(solution)/shard_map/reduce_scatter | solution.py:515
  1187.0 3.1 multiply_reduce_fusion.5
  1190.7 59.0 %reduce-scatter.14.cloned.1.call-done = bf16[192,2048]{1,0:T(8,128)(2,1)} async-done(((bf16[768,2048]{1,0:T(8,128)(2,1)}), bf16[192,2048]{1,0:T(8,128)(2,1)}) %reduce-scatter.14.cloned.1.call-update) | async-done | bytes 786448 | tf_op jit(solution)/shard_map/reduce_scatter | solution.py:523
  1249.7 3.1 add_convert_fusion
  1254.2 62.3 %all-gather.23.cloned.1.call-done = bf16[768,2048]{1,0:T(8,128)(2,1)} async-done(((bf16[192,2048]{1,0:T(8,128)(2,1)}), bf16[768,2048]{1,0:T(8,128)(2,1)}) %all-gather.23.cloned.1.call-update) | async-done | bytes 3145744 | tf_op jit(solution)/shard_map/all_gather | solution.py:520
  1316.5 5.4 fusion.63
  1323.1 57.1 %while.31 = (s32[]{:T(128)}, f32[768,4,128]{0,2,1:T(8,128)S(1)}, bf16[3,512,4,128]{3,2,1,0:T(4,128)(2,1)}, bf16[3,512,4,128]{3,2,1,0:T(4,128)(2,1)}, bf16[3,512,...) while((s32[]{:T(128)}, f32[768,4,128]{0,2,1:T(8,128)S(1)}, ...), condition=%wide.region_24.25_spmd.clone, body=%wide.region_23.24_spmd.clone.sunk | while | flops 2031353856 | bytes 106701656 | solution.py:333
  1327.9 4.9 fusion.151
  1332.9 3.3 bitcast_add_fusion.2
  1336.8 2.6 fusion.152
  1347.0 4.9 fusion.151
  1351.9 3.3 bitcast_add_fusion.2
  1355.8 2.6 fusion.152
  1366.0 4.9 fusion.151
  1370.9 3.3 bitcast_add_fusion.2
  1384.7 3.8 fusion.52
  1396.5 30.0 %reduce-scatter.20.cloned.1.call-done = bf16[768,1024]{1,0:T(8,128)(2,1)} async-done(((bf16[1536,1024]{1,0:T(8,128)(2,1)}), bf16[768,1024]{1,0:T(8,128)(2,1)}) %reduce-scatter.20.cloned.1.call-update) | async-done | bytes 1572880 | tf_op jit(solution)/shard_map/reduce_scatter | solution.py:537
  1426.6 3.0 slice_convert_fusion.1
  1441.0 3.8 multiply_reduce_fusion.4
  1445.2 10.2 multiply_reduce_fusion
  1455.6 9.1 convolution_convert_fusion
  1466.2 19.5 %convolution_bitcast_fusion.2 = f32[4,2048,256]{2,1,0:T(8,128)} fusion(bf16[8,4,256,2048]{3,2,1,0:T(8,128)(2,1)} %get-tuple-element.145, bf16[8,4,256,256]{3,2,1,0:T(8,128)(2,1)} %get-tuple-element.146), kind=kOutput, calls=%fused_computation.65 | convolution fusion | flops 8589934592 | bytes 46137344 | tf_op jit(solution)/shard_map/gesd,gesf->edf/dot_general | solution.py:492
  1485.7 18.6 %convolution_bitcast_fusion = f32[4,256,2048]{2,1,0:T(8,128)} fusion(bf16[8,4,256,256]{3,2,1,0:T(8,128)(2,1)} %get-tuple-element.138.hidden_ref, bf16[8,4,256,2048]{3,2,1,0:T(8,128)(2,1)} %get-tuple-element.148), kind=kOutput, calls=%fused_computation.63 | convolution fusion | flops 8589934592 | bytes 46137344 | tf_op jit(solution)/shard_map/gesf,gesd->efd/dot_general | solution.py:489
  1505.2 5.1 all-to-all-start
  1510.3 19.7 %convolution_bitcast_fusion.1 = f32[4,2048,256]{2,1,0:T(8,128)} fusion(bf16[8,4,256,2048]{3,2,1,0:T(8,128)(2,1)} %get-tuple-element.145, bf16[8,4,256,256]{3,2,1,0:T(8,128)(2,1)} %get-tuple-element.147), kind=kOutput, calls=%fused_computation.64 | convolution fusion | flops 8589934592 | bytes 46137344 | tf_op jit(solution)/shard_map/gesd,gesf->edf/dot_general | solution.py:495
  1530.0 20.4 %all-to-all-done = bf16[192,4,512]{2,0,1:T(8,128)(2,1)S(1)} async-done(((bf16[192,4,512]{2,0,1:T(8,128)(2,1)}), bf16[192,4,512]{2,0,1:T(8,128)(2,1)S(1)}, u32[]{:S(2)}, u32[]{:S(2)}) %all-to-all-start) | async-done | bytes 786464 | tf_op jit(solution)/shard_map/all_to_all | solution.py:524
  1553.6 9.9 psum.22
  1563.5 38.6 %psum.23 = f32[4352]{0:T(1024)S(1)} all-reduce(f32[4352]{0:T(1024)S(1)} %pad_maximum_fusion.9), channel_id=1, replica_groups=mesh['fsdp'=4,'ctx'=2,'tp'=4] {'fsdp','ctx','tp'}, use_global_device_ids=true, to_apply=%region_37.38 | all-reduce | flops 4352 | bytes 34816 | tf_op jit(solution)/shard_map/psum | solution.py:590
  1603.3 3.1 multiply_add_fusion
  1606.4 10.2 reduce-scatter.24.cloned.1.call-done
  (333 shorter events, 119.9 us)
Async XLA Ops:
  7.2 5.3 copy-start.60
  7.2 5.4 copy-start.61
  7.2 68.6 %all-gather.9.cloned.1.call-start = ((), (), s32[]{:S(2)}) async-start(), calls=%async_computation.11 | async-start | bytes 3932160 | tf_op jit(solution)/shard_map/all_gather | solution.py:402
  7.9 116.8 %all-gather.11.cloned.1.call-start = ((), (), s32[]{:S(2)}) async-start(), calls=%async_computation.12 | async-start | bytes 7667712 | tf_op jit(solution)/shard_map/all_gather | solution.py:395
  12.5 189.1 %all-gather.13.cloned.1.call-start = ((), (), s32[]{:S(2)}) async-start(), calls=%async_computation.13 | async-start | bytes 5308416 | tf_op jit(solution)/shard_map/all_gather | solution.py:437
  13.6 135.4 %copy-start.22 = (f32[768,64]{0,1:T(8,128)}, f32[768,64]{0,1:T(8,128)S(1)}, u32[]{:S(2)}) copy-start(f32[768,64]{0,1:T(8,128)S(1)} %get-tuple-element.441) | copy-start | bytes 589828
  13.6 135.4 %copy-start.24 = (f32[768,64]{0,1:T(8,128)}, f32[768,64]{0,1:T(8,128)S(1)}, u32[]{:S(2)}) copy-start(f32[768,64]{0,1:T(8,128)S(1)} %get-tuple-element.442) | copy-start | bytes 589828
  75.8 50.9 %copy-start.12 = (bf16[768,2048]{1,0:T(8,128)(2,1)S(1)}, bf16[768,2048]{1,0:T(8,128)(2,1)}, u32[]{:S(2)}) copy-start(bf16[768,2048]{1,0:T(8,128)(2,1)} %all-gather.9.cloned.1.call-done) | copy-start | bytes 9437188
  78.5 55.4 %copy-start.51 = (f32[768]{0:T(1024)}, f32[768]{0:T(1024)S(1)}, u32[]{:S(2)}) copy-start(f32[768]{0:T(1024)S(1)} %add_rsqrt_fusion.2) | copy-start | bytes 9220
  126.7 7.3 copy-start.55
  126.7 232.8 %copy-start.40 = (f32[2048]{0:T(1024)}, f32[2048]{0:T(1024)S(1)}, u32[]{:S(2)}) copy-start(f32[2048]{0:T(1024)S(1)} %get-tuple-element.346) | copy-start | bytes 24580
  143.2 5.8 copy-start.9
  143.2 4.0 copy-start.57
  152.0 110.3 %all-gather.15.cloned.1.call-start = ((), (), s32[]{:S(2)}) async-start(), calls=%async_computation.14 | async-start | bytes 2359296 | tf_op jit(solution)/shard_map/all_gather | solution.py:396
  152.6 143.8 %all-gather.17.cloned.1.call-start = ((), (), s32[]{:S(2)}) async-start(), calls=%async_computation.16 | async-start | bytes 3932160 | tf_op jit(solution)/shard_map/all_gather | solution.py:411
  153.2 204.4 %reduce-scatter.10.cloned.1.call-start = ((), (), s32[]{:S(2)}) async-start(), calls=%async_computation.15 | async-start | bytes 3932160 | tf_op jit(solution)/shard_map/reduce_scatter | solution.py:459
  220.1 5.0 copy-start
  233.8 4.6 copy-start
  247.4 4.7 copy-start
  256.8 5.4 copy-start.3
  256.8 5.4 copy-start.6
  256.8 5.4 copy-start.27
  256.8 5.4 copy-start.29
  256.8 5.4 copy-start.36
  262.3 5.4 copy-start.33
  267.7 224.4 %all-gather.19.cloned.1.call-start = ((), (), s32[]{:S(2)}) async-start(), calls=%async_computation.17 | async-start | bytes 30081024 | tf_op jit(solution)/shard_map/all_gather | solution.py:415
  302.4 354.7 %all-gather.21.cloned.1.call-start = ((), (), s32[]{:S(2)}) async-start(), calls=%async_computation.18 | async-start | bytes 27574272 | tf_op jit(solution)/shard_map/all_gather | solution.py:467
  363.1 564.1 %reduce-scatter.16.cloned.1.call-start = ((), (), s32[]{:S(2)}) async-start(), calls=%async_computation.21 | async-start | bytes 28311552 | tf_op jit(solution)/shard_map/reduce_scatter | solution.py:480
  772.0 315.6 %reduce-scatter.12.cloned.1.call-start = ((), (), s32[]{:S(2)}) async-start(), calls=%async_computation.19 | async-start | bytes 28311552 | tf_op jit(solution)/shard_map/reduce_scatter | solution.py:522
  808.8 315.9 %all-reduce.2.cloned.1.call-start = ((), (), s32[]{:S(2)}) async-start(), calls=%async_computation.23 | async-start | bytes 196608 | tf_op jit(solution)/shard_map/psum | solution.py:481
  810.4 376.6 %reduce-scatter.18.cloned.1.call-start = ((), (), s32[]{:S(2)}) async-start(), calls=%async_computation.22 | async-start | bytes 3932160 | tf_op jit(solution)/shard_map/reduce_scatter | solution.py:515
  927.2 322.5 %reduce-scatter.14.cloned.1.call-start = ((), (), s32[]{:S(2)}) async-start(), calls=%async_computation.20 | async-start | bytes 3932160 | tf_op jit(solution)/shard_map/reduce_scatter | solution.py:523
  1124.7 8.4 all-to-all-start.1
  1128.3 188.2 %all-gather.23.cloned.1.call-start = ((), (), s32[]{:S(2)}) async-start(), calls=%async_computation.24 | async-start | bytes 3932160 | tf_op jit(solution)/shard_map/all_gather | solution.py:520
  1129.8 57.2 %copy-start.8 = (f32[192,2048]{1,0:T(8,128)S(1)}, f32[192,2048]{1,0:T(8,128)}, u32[]{:S(2)}) copy-start(f32[192,2048]{1,0:T(8,128)} %copy-done.7) | copy-start | bytes 4718596
  1129.8 57.2 %copy-start.41 = (f32[2048]{0:T(1024)S(1)}, f32[2048]{0:T(1024)}, u32[]{:S(2)}) copy-start(f32[2048]{0:T(1024)} %copy-done.40) | copy-start | bytes 24580
  1129.8 57.2 %copy-start.50 = (f32[192]{0:T(256)S(1)}, f32[192]{0:T(256)}, u32[]{:S(2)}) copy-start(f32[192]{0:T(256)} %copy-done.49) | copy-start | bytes 2308
  1252.8 173.7 %reduce-scatter.20.cloned.1.call-start = ((), (), s32[]{:S(2)}) async-start(), calls=%async_computation.25 | async-start | bytes 4718592 | tf_op jit(solution)/shard_map/reduce_scatter | solution.py:537
  1254.2 68.8 %copy-start.4 = (bf16[768,4,128]{2,0,1:T(8,128)(2,1)S(1)}, bf16[768,4,128]{2,0,1:T(8,128)(2,1)}, u32[]{:S(2)}) copy-start(bf16[768,4,128]{2,0,1:T(8,128)(2,1)} %copy-done.3) | copy-start | bytes 2359300
  1254.2 68.8 %copy-start.37 = (bf16[768]{0:T(1024)(128)(2,1)S(1)}, bf16[768]{0:T(1024)(128)(2,1)}, u32[]{:S(2)}) copy-start(bf16[768]{0:T(1024)(128)(2,1)} %copy-done.36) | copy-start | bytes 4612
  1254.2 68.8 %copy-start.39 = (bf16[3,512]{1,0:T(4,128)(2,1)S(1)}, bf16[3,512]{1,0:T(4,128)(2,1)}, u32[]{:S(2)}) copy-start(bf16[3,512]{1,0:T(4,128)(2,1)} %copy-done.38) | copy-start | bytes 9220
  1323.1 4.8 copy-start.32
  1323.1 4.8 copy-start.53
  1323.1 4.8 copy-start.54
  1342.2 4.8 copy-start.32
  1342.2 4.8 copy-start.53
  1342.2 4.8 copy-start.54
  1361.2 4.8 copy-start.32
  1361.2 4.8 copy-start.53
  1361.2 4.8 copy-start.54
  1384.4 4.1 copy-start.34
  1384.4 166.0 %reduce-scatter.26.cloned.1.call-start = ((), (), s32[]{:S(2)}) async-start(), calls=%async_computation.28 | async-start | bytes 2949120 | tf_op jit(solution)/shard_map/reduce_scatter | solution.py:579
  1392.3 210.9 %reduce-scatter.22.cloned.1.call-start = ((), (), s32[]{:S(2)}) async-start(), calls=%async_computation.26 | async-start | bytes 3932160 | tf_op jit(solution)/shard_map/reduce_scatter | solution.py:565
  1441.0 4.0 copy-start.14
  1441.0 4.2 copy-start.35
  1441.0 4.2 copy-start.52
  1441.0 4.2 copy-start.56
  1444.8 10.5 copy-start.30
  1444.9 10.5 copy-start.31
  1455.4 161.2 %reduce-scatter.24.cloned.1.call-start = ((), (), s32[]{:S(2)}) async-start(), calls=%async_computation.27 | async-start | bytes 7077888 | tf_op jit(solution)/shard_map/reduce_scatter | solution.py:587
  1485.7 18.6 %copy-start.19 = (bf16[192,2048]{1,0:T(8,128)(2,1)S(1)}, bf16[192,2048]{1,0:T(8,128)(2,1)}, u32[]{:S(2)}) copy-start(bf16[192,2048]{1,0:T(8,128)(2,1)} %get-tuple-element.426) | copy-start | bytes 2359300
  1505.2 45.2 %all-to-all-start = ((bf16[192,4,512]{2,0,1:T(8,128)(2,1)}), bf16[192,4,512]{2,0,1:T(8,128)(2,1)S(1)}, u32[]{:S(2)}, u32[]{:S(2)}) async-start(bf16[192,4,512]{2,0,1:T(8,128)(2,1)} %bitcast.150), calls=%async_computation.3 | async-start | bytes 1572864 | tf_op jit(solution)/shard_map/all_to_all | solution.py:524
  1530.0 33.6 %copy-start.47 = (f32[2048]{0:T(1024)S(1)}, f32[2048]{0:T(1024)}, u32[]{:S(2)}) copy-start(f32[2048]{0:T(1024)} %get-tuple-element.350) | copy-start | bytes 24580
  1530.0 73.3 %copy-start.21 = (bf16[768,512]{1,0:T(8,128)(2,1)S(1)}, bf16[768,512]{1,0:T(8,128)(2,1)}, u32[]{:S(2)}) copy-start(bf16[768,512]{1,0:T(8,128)(2,1)} %param.21) | copy-start | bytes 2359300
  (33 other events, 74.7 us)
Sparse Core Ops, SparseCore 0:
  9.6 66.1 all-gather.8
  78.3 46.4 all-gather.10
  152.1 49.3 all-gather.12
  203.3 28.1 all-gather.14
  232.9 63.4 all-gather.16
  298.6 58.9 reduce-scatter.9
  360.0 131.9 all-gather.18
  494.9 162.1 all-gather.20
  772.1 155.0 reduce-scatter.15
  930.6 156.8 reduce-scatter.11
  1090.4 34.2 all-reduce.1
  1127.0 59.9 reduce-scatter.17
  1189.4 60.2 reduce-scatter.13
  1253.0 63.5 all-gather.22
  1384.5 41.9 reduce-scatter.19
  1429.7 43.6 reduce-scatter.25
  1475.6 72.7 reduce-scatter.21
  1551.6 64.9 reduce-scatter.23

commit v2 on v1

v2 whole, which is shorter than its diff:
```python
import functools

import jax
import jax.numpy as jnp
from jax import lax
from jax.experimental import pallas as pl
from jax.experimental.pallas import tpu as pltpu
from jax.sharding import PartitionSpec as P

QUERY_BLOCK = 256
CHUNK = 768
SLOTS = 256
EXTRA = 128
VMEM_BYTES = 60 * 1024 * 1024


epsilon = 1e-05
rope_base = 50000.0
masked_score = -1e30
highest = lax.Precision.HIGHEST
bf16 = jnp.bfloat16
f32 = jnp.float32
ROWS = ("fsdp", "ctx")
ALL = ("fsdp", "ctx", "tp")
MESH = pl.DeviceIdType.MESH


def doc_places(order_row, length_row):
    ends = jnp.cumsum(length_row, dtype=jnp.int32)
    passed = (order_row[:, None] >= ends[None, :]).astype(jnp.int32)
    segment = jnp.sum(passed, axis=1, dtype=jnp.int32)
    start = jnp.sum(passed * length_row[None, :], axis=1, dtype=jnp.int32)
    return (segment, order_row - start)


def rope_tables(position, head_dim):
    half = head_dim // 2
    freqs = rope_base ** (-(jnp.arange(half, dtype=jnp.float32) * (2.0 / head_dim)))
    angles = position.astype(jnp.float32)[:, None] * freqs[None, :]
    cosine, sine = jnp.cos(angles), jnp.sin(angles)
    return jnp.concatenate([cosine, cosine], axis=1), jnp.concatenate([-sine, sine], axis=1)


def norm_scale(values):
    return lax.rsqrt(jnp.mean(values * values, axis=-1, keepdims=True) + epsilon)


def norm_back(incoming, values, inverse, gain):
    scaled = incoming * gain
    value_grad = inverse * (
        scaled - values * inverse * inverse * jnp.mean(scaled * values, axis=-1, keepdims=True)
    )
    return (value_grad, incoming * values * inverse)


def matmul(left, right):
    return jnp.dot(left, right, preferred_element_type=f32)


def matmul_nt(left, right):
    return lax.dot_general(left, right, (((1,), (1,)), ((), ())), preferred_element_type=f32)


def slot_rows(rank_row):
    slots = lax.broadcasted_iota(jnp.int32, (SLOTS, rank_row.shape[1]), 0)
    return slots == rank_row


def slot_columns(rank_column):
    slots = lax.broadcasted_iota(jnp.int32, (rank_column.shape[0], SLOTS), 1)
    return jnp.where(slots == rank_column, 1.0, 0.0).astype(bf16)


def as_one_hot(mask):
    return jnp.where(mask, 1.0, 0.0).astype(bf16)


def select_grads(ids_ref, rank_ref, grad_ref, down_ref, rows_ref, product_ref):
    expert = pl.program_id(1)
    rows = matmul(as_one_hot(slot_rows(rank_ref[...])), grad_ref[...]).astype(bf16)
    rows_ref[...] = rows
    product_ref[...] = matmul_nt(rows, down_ref[expert])


def expert_step(
    expert,
    named,
    rank_ref,
    tokens,
    product_ref,
    gate_ref,
    up_ref,
    await_weights,
    rows_ref,
    hidden_ref,
    gate_grad_ref,
    up_grad_ref,
    route_ref,
    held_ref,
):
    width = rows_ref.shape[1]
    mask = slot_rows(rank_ref[...])
    picked = matmul(as_one_hot(mask), tokens)
    rows = picked[:, :width].astype(bf16)
    rows_ref[...] = rows
    lane = lax.broadcasted_iota(jnp.int32, (SLOTS, EXTRA), 1)
    mine = jnp.logical_and(lax.rem(lane, 32) == named, lane < 96)
    gate = jnp.sum(jnp.where(mine, picked[:, width:], 0.0), axis=1, keepdims=True)
    await_weights()
    gate_act = matmul(rows, gate_ref[expert])
    up_act = matmul(rows, up_ref[expert])
    sigmoid_g = 1.0 / (1.0 + jnp.exp(-gate_act))
    silu_g = gate_act * sigmoid_g
    hidden = silu_g * up_act
    hidden_ref[...] = (gate * hidden).astype(bf16)
    product = product_ref[...]
    route = jnp.sum(hidden.astype(bf16).astype(f32) * product, axis=1, keepdims=True)
    route_ref[...] = jnp.sum(jnp.where(mask, route, 0.0), axis=0, keepdims=True)
    hidden_grad = gate * product
    gate_grad = (
        hidden_grad * up_act * sigmoid_g * (1.0 + gate_act * (1.0 - sigmoid_g))
    ).astype(bf16)
    up_grad = (hidden_grad * silu_g).astype(bf16)
    gate_grad_ref[...] = gate_grad
    up_grad_ref[...] = up_grad
    back = matmul_nt(gate_grad, gate_ref[expert]) + matmul_nt(up_grad, up_ref[expert])
    held_ref[pl.ds(pl.multiple_of(expert * SLOTS, SLOTS), SLOTS), :] = back.astype(bf16)


def chunk_places(column_ref):
    columns = column_ref[...]
    return jnp.concatenate(
        [slot_columns(columns[:, e : e + 1]) for e in range(columns.shape[1])], axis=1
    )


def expert_pass(
    ids_ref,
    first_ref,
    rank_ref,
    column_ref,
    near_ref,
    far_ref,
    product_ref,
    gate_in_ref,
    up_in_ref,
    *refs,
):
    (
        rows_ref,
        hidden_ref,
        gate_grad_ref,
        up_grad_ref,
        route_ref,
        near_back_ref,
        far_back_ref,
        token_ref,
        gate_ref,
        up_ref,
        held_ref,
        back_ref,
        token_sem,
        gate_sem,
        up_sem,
        back_sem,
    ) = refs[-16:]
    chunk, expert = pl.program_id(0), pl.program_id(1)
    local = gate_ref.shape[0]
    width = rows_ref.shape[1]
    tiles = back_sem.shape[1]
    tile = width // tiles
    loads = [
        pltpu.make_async_copy(source, token_ref.at[at], token_sem.at[at])
        for at, source in enumerate((near_ref, far_ref))
    ]

    def weight_load(source, held, sem, at):
        return pltpu.make_async_copy(source.at[at], held.at[at], sem.at[at])

    def back_store(to, at, step):
        columns = pl.ds(step * tile, tile)
        return pltpu.make_async_copy(
            back_ref.at[at, :, columns], to.at[:, columns], back_sem.at[at, step]
        )

    @pl.when(jnp.logical_and(chunk == 0, expert == 0))
    def _():
        loads[0].start()
        for at in range(local):
            weight_load(gate_in_ref, gate_ref, gate_sem, at).start()
            weight_load(up_in_ref, up_ref, up_sem, at).start()
        loads[1].start()
        loads[0].wait()

    @pl.when(jnp.logical_and(chunk == 1, expert == 0))
    def _():
        loads[1].wait()

    def await_weights():
        @pl.when(chunk == 0)
        def _():
            weight_load(gate_in_ref, gate_ref, gate_sem, expert).wait()
            weight_load(up_in_ref, up_ref, up_sem, expert).wait()

    expert_step(
        expert,
        first_ref[0] + expert,
        rank_ref,
        token_ref[chunk],
        product_ref,
        gate_ref,
        up_ref,
        await_weights,
        rows_ref,
        hidden_ref,
        gate_grad_ref,
        up_grad_ref,
        route_ref,
        held_ref,
    )

    @pl.when(expert == local - 1)
    def _():
        places = chunk_places(column_ref)
        for step in range(tiles):
            at = pl.ds(step * tile, tile)
            back_ref[chunk, :, at] = matmul(places, held_ref[:, at]).astype(bf16)

            @pl.when(chunk == 0)
            def _():
                back_store(near_back_ref, 0, step).start()

            @pl.when(chunk == 1)
            def _():
                back_store(far_back_ref, 1, step).start()

    @pl.when(jnp.logical_and(chunk == 1, expert == local - 1))
    def _():
        for step in range(tiles):
            back_store(near_back_ref, 0, step).wait()
            back_store(far_back_ref, 1, step).wait()


def exchange_pass(
    rank_ref,
    column_ref,
    product_ref,
    gate_in_ref,
    up_in_ref,
    down_in_ref,
    own_ref,
    sibling_ref,
    from_across_ref,
    from_other_ref,
    rows_ref,
    hidden_ref,
    gate_grad_ref,
    up_grad_ref,
    route_ref,
    sum_ref,
    out_ref,
    inbox_ref,
    landing_ref,
    token_ref,
    gate_ref,
    up_ref,
    down_ref,
    hidden_held_ref,
    held_ref,
    far_ref,
    beside_ref,
    chip_ref,
    corner_ref,
    token_sem,
    gate_sem,
    up_sem,
    pass_send,
    pass_recv,
    far_send,
    far_recv,
    link_send,
    link_recv,
    store_sem,
    down_sem,
    out_sem,
    landing_sem,
):
    step, expert = pl.program_id(0), pl.program_id(1)
    local = gate_ref.shape[0]
    rows, width = far_ref.shape
    half = rows // 2
    fsdp, ctx = lax.axis_index("fsdp"), lax.axis_index("ctx")
    beside_id = {"fsdp": fsdp + 1 - 2 * lax.rem(fsdp, 2)}
    across_id = {"fsdp": lax.rem(fsdp + 2, 4)}
    other_id = {"ctx": 1 - ctx}
    last = expert == local - 1
    low, high = pl.ds(0, half), pl.ds(half, half)
    sources = (
        inbox_ref.at[0],
        from_across_ref,
        inbox_ref.at[1],
        from_other_ref,
        inbox_ref.at[3],
        inbox_ref.at[2],
        sibling_ref,
        own_ref,
    )

    def token_load(at):
        slot = at % 2
        return pltpu.make_async_copy(sources[at], token_ref.at[slot], token_sem.at[slot])

    def weight_load(source, held, sem, at):
        return pltpu.make_async_copy(source.at[at], held.at[at], sem.at[at])

    def pass_copy(number):
        source, to, peer = (
            (from_across_ref, inbox_ref.at[0], beside_id),
            (from_other_ref, inbox_ref.at[1], beside_id),
            (from_other_ref.at[low], inbox_ref.at[2, low], across_id),
            (from_across_ref.at[high], inbox_ref.at[2, high], other_id),
            (inbox_ref.at[2], inbox_ref.at[3], beside_id),
        )[number]
        return pltpu.make_async_remote_copy(
            src_ref=source,
            dst_ref=to,
            send_sem=pass_send.at[number],
            recv_sem=pass_recv.at[number],
            device_id=peer,
            device_id_type=MESH,
        )

    def far_copy(turn):
        return pltpu.make_async_remote_copy(
            src_ref=far_ref,
            dst_ref=beside_ref.at[turn % 2],
            send_sem=far_send.at[turn],
            recv_sem=far_recv.at[turn],
            device_id=beside_id,
            device_id_type=MESH,
        )

    def link_copy(number):
        source, to, peer = (
            (chip_ref.at[0, high], landing_ref.at[0, high], across_id),
            (chip_ref.at[1, low], landing_ref.at[1, low], other_id),
            (chip_ref.at[2, low], corner_ref.at[0], other_id),
            (chip_ref.at[2, high], corner_ref.at[1], across_id),
            (chip_ref.at[1, high], landing_ref.at[1, high], other_id),
            (chip_ref.at[0, low], landing_ref.at[0, low], across_id),
        )[number]
        return pltpu.make_async_remote_copy(
            src_ref=source,
            dst_ref=to,
            send_sem=link_send.at[number],
            recv_sem=link_recv.at[number],
            device_id=peer,
            device_id_type=MESH,
        )

    @pl.when(jnp.logical_and(step == 0, expert == 0))
    def _():
        barrier = pltpu.get_barrier_semaphore()
        for peer in (beside_id, across_id, other_id):
            pl.semaphore_signal(barrier, inc=1, device_id=peer, device_id_type=MESH)
        pl.semaphore_wait(barrier, 3)
        for number in range(4):
            pass_copy(number).start()
        for at in range(local):
            weight_load(gate_in_ref, gate_ref, gate_sem, at).start()
            weight_load(up_in_ref, up_ref, up_sem, at).start()
        down_load = pltpu.make_async_copy(down_in_ref, down_ref, down_sem)
        down_load.start()
        pass_copy(0).wait_recv()
        token_load(0).start()

    @pl.when(jnp.logical_and(step == 3, expert == 0))
    def _():
        pass_copy(2).wait_recv()
        pass_copy(3).wait_recv()
        pass_copy(4).start()

    for at in range(8):

        @pl.when(jnp.logical_and(step == at, expert == 0))
        def _():
            token_load(at).wait()

        if at < 7:

            @pl.when(jnp.logical_and(step == at, last))
            def _():
                if at == 1:
                    pass_copy(1).wait_recv()
                if at == 3:
                    pass_copy(4).wait_recv()
                token_load(at + 1).start()

    def await_weights():
        @pl.when(step == 0)
        def _():
            weight_load(gate_in_ref, gate_ref, gate_sem, expert).wait()
            weight_load(up_in_ref, up_ref, up_sem, expert).wait()

    first = (fsdp * 2 + ctx) * local

    @pl.when(step < 8)
    def _():
        expert_step(
            expert,
            first + expert,
            rank_ref,
            token_ref[lax.rem(step, 2)],
            product_ref,
            gate_ref,
            up_ref,
            await_weights,
            rows_ref,
            hidden_ref,
            gate_grad_ref,
            up_grad_ref,
            route_ref,
            held_ref,
        )
        hidden_held_ref[step, expert] = hidden_ref[...]

    tile = 512

    def tiles():
        for at in range(0, width, tile):
            yield pl.ds(at, tile)

    def add_half(turn, part, landed):
        total = chip_ref[turn, part, :].astype(f32) + corner_ref[landed].astype(f32)
        chip_ref[turn, part, :] = total.astype(bf16)

    for turn in range(4):

        @pl.when(jnp.logical_and(step == 2 * turn, last))
        def _():
            if turn > 0:
                far_copy(turn - 1).wait_send()
            places = chunk_places(column_ref)
            for at in tiles():
                far_ref[:, at] = matmul(places, held_ref[:, at]).astype(bf16)
            far_copy(turn).start()

        @pl.when(jnp.logical_and(step == 2 * turn + 1, last))
        def _():
            far_copy(turn).wait_recv()
            if turn == 3:
                far_copy(3).wait_send()
            places = chunk_places(column_ref)
            for at in tiles():
                total = matmul(places, held_ref[:, at]) + beside_ref[turn % 2, :, at].astype(f32)
                if turn < 3:
                    chip_ref[turn, :, at] = total.astype(bf16)
                else:
                    far_ref[:, at] = total.astype(bf16)
            if turn < 2:
                link_copy(turn).start()
            if turn == 2:
                link_copy(2).start()
                link_copy(3).start()


    number = step - 8
    turn = number // 2
    chip = lax.rem(fsdp + 2 * (1 - lax.rem(turn, 2)), 4)
    core = chip + (1 - lax.rem(number, 2)) * (1 - 2 * lax.rem(fsdp, 2))
    line = lax.rem(ctx + lax.rem((turn + 1) // 2, 2), 2)
    places_at = (core * 2 + line) * rows
    slot = lax.rem(step, 2)
    columns_of = width // local
    hidden = gate_ref.shape[2]

    def out_store(at, which):
        columns = pl.ds(pl.multiple_of(which * columns_of, columns_of), columns_of)
        return pltpu.make_async_copy(
            token_ref.at[slot, :, columns],
            out_ref.at[pl.ds(pl.multiple_of(at, rows), rows), columns],
            out_sem.at[slot, which],
        )

    @pl.when(step >= 8)
    def _():
        @pl.when(jnp.logical_and(step == 8, expert == 0))
        def _():
            pltpu.make_async_copy(down_in_ref, down_ref, down_sem).wait()

        @pl.when(expert == 0)
        def _():
            columns = column_ref[...]
            for e in range(local):
                held_ref[pl.ds(0, rows), pl.ds(e * hidden, hidden)] = matmul(
                    slot_columns(columns[:, e : e + 1]), hidden_held_ref[number, e]
                ).astype(bf16)

        @pl.when(step >= 10)
        def _():
            out_store(places_at, expert).wait()

        at = pl.ds(pl.multiple_of(expert * columns_of, columns_of), columns_of)
        token_ref[slot, :, at] = matmul(
            held_ref[pl.ds(0, rows), pl.ds(0, local * hidden)], down_ref[:, at]
        ).astype(bf16)
        out_store(places_at, expert).start()

    @pl.when(jnp.logical_and(step == 9, expert == 1))
    def _():
        link_copy(3).wait_recv()
        add_half(1, high, 1)
        link_copy(4).start()
        link_copy(2).wait_recv()
        add_half(0, low, 0)
        link_copy(5).start()

    @pl.when(jnp.logical_and(step == 15, last))
    def _():
        landing = []
        for way, numbers in enumerate(((0, 5), (1, 4))):
            for number in numbers:
                link_copy(number).wait_recv()
            copy = pltpu.make_async_copy(
                landing_ref.at[way], beside_ref.at[way], landing_sem.at[way]
            )
            copy.start()
            landing.append(copy)
        for copy in landing:
            copy.wait()
        for part in (low, high):
            held_ref[part, :] = (
                far_ref[part, :].astype(f32)
                + beside_ref[0, part, :].astype(f32)
                + beside_ref[1, part, :].astype(f32)
            ).astype(bf16)
        store = pltpu.make_async_copy(held_ref.at[pl.ds(0, rows)], sum_ref, store_sem)
        store.start()
        for number in range(5):
            pass_copy(number).wait_send()
        for number in range(6):
            link_copy(number).wait_send()
        for other_slot in (0, 1):
            for which in range(local):
                columns = pl.ds(which * columns_of, columns_of)
                pltpu.make_async_copy(
                    token_ref.at[other_slot, :, columns],
                    out_ref.at[pl.ds(0, rows), columns],
                    out_sem.at[other_slot, which],
                ).wait()
        store.wait()


def expert_sums(ids_ref, column_ref, hidden_ref, down_ref, out_ref):
    columns = column_ref[...]
    dense = [
        matmul(slot_columns(columns[:, e : e + 1]), hidden_ref[e]).astype(bf16)
        for e in range(columns.shape[1])
    ]
    out_ref[...] = matmul(jnp.concatenate(dense, axis=1), down_ref[...]).astype(bf16)


def params(dims):
    return pltpu.CompilerParams(
        dimension_semantics=("arbitrary",) * dims, vmem_limit_bytes=VMEM_BYTES
    )


def once(shape):
    return pl.BlockSpec(
        shape, lambda *ids: (0,) * len(shape), pipeline_mode=pl.Buffered(1)
    )


def run_select_grads(ids, rank_rows, grad_all, down_weight):
    chunks, local = rank_rows.shape[:2]
    hidden, width = down_weight.shape[1:]
    slots = chunks * local * SLOTS
    place = lambda g, e, ids: (g, e, 0, 0)
    return pl.pallas_call(
        select_grads,
        grid_spec=pltpu.PrefetchScalarGridSpec(
            num_scalar_prefetch=1,
            grid=(chunks, local),
            in_specs=[
                pl.BlockSpec((None, None, 1, CHUNK), place),
                pl.BlockSpec((CHUNK, width), lambda g, e, ids: (ids[g], 0)),
                once(down_weight.shape),
            ],
            out_specs=[
                pl.BlockSpec((None, None, SLOTS, width), place),
                pl.BlockSpec((None, None, SLOTS, hidden), place),
            ],
        ),
        out_shape=[
            jax.ShapeDtypeStruct((chunks, local, SLOTS, width), bf16),
            jax.ShapeDtypeStruct((chunks, local, SLOTS, hidden), f32),
        ],
        compiler_params=params(2),
        cost_estimate=pl.CostEstimate(
            flops=2 * slots * width * (CHUNK + hidden),
            bytes_accessed=2 * (chunks * CHUNK + slots) * width,
            transcendentals=0,
        ),
        name="select_grads",
    )(ids, rank_rows, grad_all, down_weight)


def run_exchange_pass(rank_rows, rank_columns, product, weights, sources):
    gate_weight, up_weight, down_weight = weights
    chunks, local = rank_rows.shape[:2]
    width, hidden = gate_weight.shape[1:]
    slots = chunks * local * SLOTS
    flat_down = down_weight.reshape(local * hidden, width)

    def per_expert(g, e):
        return (jnp.minimum(g, chunks - 1), jnp.where(g < chunks, e, local - 1), 0, 0)

    narrow = pl.BlockSpec((None, None, SLOTS, hidden), per_expert)
    anywhere = pl.BlockSpec(memory_space=pl.ANY)
    half = (2, CHUNK // 2, width)
    narrow_shape = jax.ShapeDtypeStruct((chunks, local, SLOTS, hidden), bf16)
    outs = pl.pallas_call(
        exchange_pass,
        grid=(2 * chunks, local),
        in_specs=[
            pl.BlockSpec((None, None, 1, CHUNK), per_expert),
            pl.BlockSpec((None, CHUNK, local), lambda g, e: (lax.rem(g, chunks), 0, 0)),
            narrow,
            *[anywhere] * 7,
        ],
        out_specs=[
            pl.BlockSpec((None, None, SLOTS, width), per_expert),
            narrow,
            narrow,
            narrow,
            pl.BlockSpec((None, None, 1, CHUNK), per_expert),
            *[anywhere] * 4,
        ],
        out_shape=[
            jax.ShapeDtypeStruct((chunks, local, SLOTS, width), bf16),
            narrow_shape,
            narrow_shape,
            narrow_shape,
            jax.ShapeDtypeStruct((chunks, local, 1, CHUNK), f32),
            jax.ShapeDtypeStruct((CHUNK, width), bf16),
            jax.ShapeDtypeStruct((chunks * CHUNK, width), bf16),
            jax.ShapeDtypeStruct((4, *sources[0].shape), bf16),
            jax.ShapeDtypeStruct((2, CHUNK, width), bf16),
        ],
        scratch_shapes=[
            pltpu.VMEM((2, CHUNK, width + EXTRA), bf16),
            pltpu.VMEM(gate_weight.shape, bf16),
            pltpu.VMEM(up_weight.shape, bf16),
            pltpu.VMEM(flat_down.shape, bf16),
            pltpu.VMEM((chunks, local, SLOTS, hidden), bf16),
            pltpu.VMEM((local * SLOTS, width), bf16),
            pltpu.VMEM((CHUNK, width), bf16),
            pltpu.VMEM((2, CHUNK, width), bf16),
            pltpu.VMEM((3, CHUNK, width), bf16),
            pltpu.VMEM(half, bf16),
            pltpu.SemaphoreType.DMA((2,)),
            pltpu.SemaphoreType.DMA((local,)),
            pltpu.SemaphoreType.DMA((local,)),
            pltpu.SemaphoreType.DMA((5,)),
            pltpu.SemaphoreType.DMA((5,)),
            pltpu.SemaphoreType.DMA((4,)),
            pltpu.SemaphoreType.DMA((4,)),
            pltpu.SemaphoreType.DMA((6,)),
            pltpu.SemaphoreType.DMA((6,)),
            pltpu.SemaphoreType.DMA,
            pltpu.SemaphoreType.DMA,
            pltpu.SemaphoreType.DMA((2, local)),
            pltpu.SemaphoreType.DMA((2,)),
        ],
        compiler_params=pltpu.CompilerParams(
            dimension_semantics=("arbitrary",) * 2,
            collective_id=9,
            has_side_effects=True,
            vmem_limit_bytes=VMEM_BYTES,
        ),
        cost_estimate=pl.CostEstimate(
            flops=2 * slots * width * (2 * CHUNK + 4 * hidden),
            bytes_accessed=2 * (12 * CHUNK + slots) * width,
            transcendentals=slots * hidden,
        ),
        name="exchange_pass",
    )(rank_rows, rank_columns, product, gate_weight, up_weight, flat_down, *sources)
    return outs[:5], outs[5], outs[6]


def run_expert_pass(
    ids, first, rank_rows, rank_columns, near, far, product, gate_weight, up_weight, kept
):
    chunks, local = rank_rows.shape[:2]
    width, hidden = gate_weight.shape[1:]
    slots = 2 * local * SLOTS
    per_expert = lambda g, e, ids: (ids[g], e, 0, 0)
    narrow = pl.BlockSpec((None, None, SLOTS, hidden), per_expert)
    in_specs = [
        pl.BlockSpec(memory_space=pltpu.SMEM),
        pl.BlockSpec((None, None, 1, CHUNK), per_expert),
        pl.BlockSpec((None, CHUNK, local), lambda g, e, ids: (ids[g], 0, 0)),
        pl.BlockSpec(memory_space=pl.ANY),
        pl.BlockSpec(memory_space=pl.ANY),
        narrow,
        pl.BlockSpec(memory_space=pl.ANY),
        pl.BlockSpec(memory_space=pl.ANY),
    ]
    kept_shapes = [
        jax.ShapeDtypeStruct((chunks, local, SLOTS, width), bf16),
        jax.ShapeDtypeStruct((chunks, local, SLOTS, hidden), bf16),
        jax.ShapeDtypeStruct((chunks, local, SLOTS, hidden), bf16),
        jax.ShapeDtypeStruct((chunks, local, SLOTS, hidden), bf16),
        jax.ShapeDtypeStruct((chunks, local, 1, CHUNK), f32),
    ]
    outs = pl.pallas_call(
        expert_pass,
        grid_spec=pltpu.PrefetchScalarGridSpec(
            num_scalar_prefetch=1,
            grid=(2, local),
            in_specs=in_specs + [pl.BlockSpec(memory_space=pl.ANY)] * len(kept),
            out_specs=[
                pl.BlockSpec((None, None, SLOTS, width), per_expert),
                narrow,
                narrow,
                narrow,
                pl.BlockSpec((None, None, 1, CHUNK), per_expert),
                pl.BlockSpec(memory_space=pl.ANY),
                pl.BlockSpec(memory_space=pl.ANY),
            ],
            scratch_shapes=[
                pltpu.VMEM((2, CHUNK, width + EXTRA), bf16),
                pltpu.VMEM(gate_weight.shape, bf16),
                pltpu.VMEM(up_weight.shape, bf16),
                pltpu.VMEM((local * SLOTS, width), bf16),
                pltpu.VMEM((2, CHUNK, width), bf16),
                pltpu.SemaphoreType.DMA((2,)),
                pltpu.SemaphoreType.DMA((local,)),
                pltpu.SemaphoreType.DMA((local,)),
                pltpu.SemaphoreType.DMA((2, 4)),
            ],
        ),
        out_shape=kept_shapes + [jax.ShapeDtypeStruct((CHUNK, width), bf16)] * 2,
        input_output_aliases={9 + at: at for at in range(len(kept))},
        compiler_params=params(2),
        cost_estimate=pl.CostEstimate(
            flops=2 * slots * width * (2 * CHUNK + 4 * hidden),
            bytes_accessed=2 * (4 * CHUNK + slots) * width,
            transcendentals=slots * hidden,
        ),
        name="expert_pass",
    )(ids, first, rank_rows, rank_columns, near, far, product, gate_weight, up_weight, *kept)
    return outs[:5], outs[5], outs[6]


def run_expert_sums(ids, rank_columns, hidden_rows, down_weight):
    chunks, local, unused, hidden = hidden_rows.shape
    width = down_weight.shape[2]
    flat = down_weight.reshape(local * hidden, width)
    return pl.pallas_call(
        expert_sums,
        grid_spec=pltpu.PrefetchScalarGridSpec(
            num_scalar_prefetch=1,
            grid=(chunks,),
            in_specs=[
                pl.BlockSpec((None, CHUNK, local), lambda g, ids: (g, 0, 0)),
                pl.BlockSpec((None, local, SLOTS, hidden), lambda g, ids: (g, 0, 0, 0)),
                once(flat.shape),
            ],
            out_specs=pl.BlockSpec((CHUNK, width), lambda g, ids: (ids[g], 0)),
        ),
        out_shape=jax.ShapeDtypeStruct((chunks * CHUNK, width), bf16),
        compiler_params=params(1),
        cost_estimate=pl.CostEstimate(
            flops=2 * chunks * CHUNK * local * hidden * (width + SLOTS),
            bytes_accessed=2 * chunks * CHUNK * width,
            transcendentals=0,
        ),
        name="expert_sums",
    )(ids, rank_columns, hidden_rows, flat)


def line_barrier(size):
    place = lax.axis_index("tp")
    barrier = pltpu.get_barrier_semaphore()

    @pl.when(place > 0)
    def _():
        pl.semaphore_signal(barrier, inc=1, device_id={"tp": place - 1}, device_id_type=MESH)

    @pl.when(place < size - 1)
    def _():
        pl.semaphore_signal(barrier, inc=1, device_id={"tp": place + 1}, device_id_type=MESH)

    has_left = jnp.where(place > 0, 1, 0)
    has_right = jnp.where(place < size - 1, 1, 0)
    pl.semaphore_wait(barrier, has_left + has_right)


def line_gather(size, columns, in_ref, out_ref, own_sem, send_sem, recv_sem):
    place = lax.axis_index("tp")
    extent = in_ref.shape[1] if columns else in_ref.shape[0]

    def block(index):
        at = pl.ds(pl.multiple_of(index * extent, extent), extent)
        return out_ref.at[:, at] if columns else out_ref.at[at, :]

    line_barrier(size)
    own = pltpu.make_async_copy(in_ref, block(place), own_sem)
    own.start()

    def sending(way, step):
        source = place - step if way == 0 else place + step
        to = place + 1 if way == 0 else place - 1
        return pltpu.make_async_remote_copy(
            src_ref=in_ref if step == 0 else block(source),
            dst_ref=block(source),
            send_sem=send_sem.at[way, step],
            recv_sem=recv_sem.at[way, step],
            device_id={"tp": to},
            device_id_type=MESH,
        )

    def sends(way, step):
        if way == 0:
            return jnp.logical_and(place >= step, place < size - 1)
        return jnp.logical_and(place + step < size, place > 0)

    def receiving(way, step):
        source = place - 1 - step if way == 0 else place + 1 + step
        origin = place - 1 if way == 0 else place + 1
        return pltpu.make_async_remote_copy(
            src_ref=block(source),
            dst_ref=block(source),
            send_sem=send_sem.at[way, step],
            recv_sem=recv_sem.at[way, step],
            device_id={"tp": origin},
            device_id_type=MESH,
        )

    def receives(way, step):
        return place > step if way == 0 else place + 1 + step < size

    for step in range(size - 1):
        for way in (0, 1):

            @pl.when(sends(way, step))
            def _():
                sending(way, step).start()

        for way in (0, 1):

            @pl.when(receives(way, step))
            def _():
                receiving(way, step).wait_recv()

    for step in range(size - 1):
        for way in (0, 1):

            @pl.when(sends(way, step))
            def _():
                sending(way, step).wait_send()

    own.wait()


def line_scatter(
    size, columns, in_ref, out_ref, staged_ref, landed_ref, send_sem, recv_sem, stages=()
):
    place = lax.axis_index("tp")
    extent = out_ref.shape[1] if columns else out_ref.shape[0]

    def block(index):
        at = pl.ds(pl.multiple_of(index * extent, extent), extent)
        values = in_ref[:, at] if columns else in_ref[at, :]
        return values.astype(f32)

    if not stages:
        line_barrier(size)

    def copying(way, step, to):
        return pltpu.make_async_remote_copy(
            src_ref=staged_ref.at[way, step],
            dst_ref=landed_ref.at[way, step],
            send_sem=send_sem.at[way, step],
            recv_sem=recv_sem.at[way, step],
            device_id={"tp": to},
            device_id_type=MESH,
        )

    for step in range(size - 1):
        for way in (0, 1):
            rank = place if way == 0 else size - 1 - place
            target = size - 1 - step + place if way == 0 else place - (size - 1 - step)
            to = place + 1 if way == 0 else place - 1
            active = jnp.logical_and(rank <= step, rank < size - 1)

            @pl.when(active)
            def _():
                values = block(target)
                if step == 0:
                    staged_ref[way, step] = values.astype(bf16)
                else:

                    @pl.when(rank == 0)
                    def _():
                        staged_ref[way, step] = values.astype(bf16)

                    @pl.when(rank > 0)
                    def _():
                        landed = landed_ref[way, step - 1].astype(f32)
                        staged_ref[way, step] = (values + landed).astype(bf16)

                copying(way, step, to).start()

        if step < len(stages):
            stages[step]()

        for way in (0, 1):
            rank = place if way == 0 else size - 1 - place
            origin = place - 1 if way == 0 else place + 1

            @pl.when(jnp.logical_and(rank > 0, rank - 1 <= step))
            def _():
                copying(way, step, origin).wait_recv()

    for stage in stages[size - 1 :]:
        stage()
    out_ref[...] = block(place)
    for way in (0, 1):
        rank = place if way == 0 else size - 1 - place

        @pl.when(rank > 0)
        def _():
            out_ref[...] += landed_ref[way, size - 2].astype(f32)

    for step in range(size - 1):
        for way in (0, 1):
            rank = place if way == 0 else size - 1 - place
            to = place + 1 if way == 0 else place - 1

            @pl.when(jnp.logical_and(rank <= step, rank < size - 1))
            def _():
                copying(way, step, to).wait_send()


def closing_sums(
    sizes,
    narrow,
    in_ref,
    small_ref,
    out_ref,
    every_ref,
    line_ref,
    staged_ref,
    landed_ref,
    total_ref,
    small_tp_ref,
    small_ctx_ref,
    small_fsdp_ref,
    send_sem,
    recv_sem,
    small_send_sem,
    small_recv_sem,
):
    axes = ("tp", "ctx", "fsdp")
    barrier = pltpu.get_barrier_semaphore()
    for axis, size in zip(axes, sizes):
        place = lax.axis_index(axis)
        for offset in range(1, size):
            peer = lax.rem(place + offset, size)
            pl.semaphore_signal(barrier, inc=1, device_id={axis: peer}, device_id_type=MESH)
    pl.semaphore_wait(barrier, sum(sizes) - len(sizes))
    landings = (small_tp_ref, small_ctx_ref, small_fsdp_ref)

    def copying(axis, offset, peer):
        return pltpu.make_async_remote_copy(
            src_ref=small_ref if axis == 0 else total_ref.at[axis - 1],
            dst_ref=landings[axis].at[offset - 1],
            send_sem=small_send_sem.at[axis, offset - 1],
            recv_sem=small_recv_sem.at[axis, offset - 1],
            device_id={axes[axis]: peer},
            device_id_type=MESH,
        )

    def each(axis):
        size, place = sizes[axis], lax.axis_index(axes[axis])
        for offset in range(1, size):
            yield (
                offset,
                lax.rem(place + offset, size),
                lax.rem(place + size - offset, size),
            )

    def start(axis):
        for offset, to, origin in each(axis):
            copying(axis, offset, to).start()

    def finish(axis):
        total = small_ref[...] if axis == 0 else total_ref[axis - 1]
        for offset, to, origin in each(axis):
            copying(axis, offset, origin).wait_recv()
            total = total + landings[axis][offset - 1]
        for offset, to, origin in each(axis):
            copying(axis, offset, to).wait_send()
        return total

    def first():
        start(0)

    def second():
        total = finish(0)
        total_ref[0] = total
        line_ref[...] = total[:, narrow:]
        start(1)

    def third():
        total_ref[1] = finish(1)
        start(2)

    def last():
        every_ref[...] = finish(2)[:, :narrow]

    line_scatter(
        sizes[0],
        True,
        in_ref,
        out_ref,
        staged_ref,
        landed_ref,
        send_sem,
        recv_sem,
        stages=(first, second, third, last),
    )


def peer_barrier(axis, size):
    place = lax.axis_index(axis)
    barrier = pltpu.get_barrier_semaphore()
    for offset in range(1, size):
        peer = lax.rem(place + offset, size)
        pl.semaphore_signal(barrier, inc=1, device_id={axis: peer}, device_id_type=MESH)
    pl.semaphore_wait(barrier, size - 1)


def peer_gather(size, in_ref, out_ref, own_sem, send_sem, recv_sem):
    place = lax.axis_index("ctx")
    rows = in_ref.shape[0]

    def block(index):
        return out_ref.at[pl.ds(pl.multiple_of(index * rows, rows), rows), :]

    def copying(offset, source, peer):
        return pltpu.make_async_remote_copy(
            src_ref=in_ref,
            dst_ref=block(source),
            send_sem=send_sem.at[offset - 1],
            recv_sem=recv_sem.at[offset - 1],
            device_id={"ctx": peer},
            device_id_type=MESH,
        )

    peer_barrier("ctx", size)
    own = pltpu.make_async_copy(in_ref, block(place), own_sem)
    own.start()
    for offset in range(1, size):
        copying(offset, place, lax.rem(place + offset, size)).start()
    for offset in range(1, size):
        origin = lax.rem(place + size - offset, size)
        copying(offset, origin, origin).wait_recv()
    for offset in range(1, size):
        copying(offset, place, lax.rem(place + offset, size)).wait_send()
    own.wait()


def peer_scatter(size, in_ref, out_ref, landed_ref, send_sem, recv_sem):
    place = lax.axis_index("ctx")
    rows = out_ref.shape[0]

    def at(index):
        return pl.ds(pl.multiple_of(index * rows, rows), rows)

    def copying(offset, peer):
        return pltpu.make_async_remote_copy(
            src_ref=in_ref.at[at(peer), :],
            dst_ref=landed_ref.at[offset - 1],
            send_sem=send_sem.at[offset - 1],
            recv_sem=recv_sem.at[offset - 1],
            device_id={"ctx": peer},
            device_id_type=MESH,
        )

    peer_barrier("ctx", size)
    for offset in range(1, size):
        copying(offset, lax.rem(place + offset, size)).start()
    total = in_ref[at(place), :].astype(f32)
    for offset in range(1, size):
        origin = lax.rem(place + size - offset, size)
        copying(offset, origin).wait_recv()
        total = total + landed_ref[offset - 1].astype(f32)
    out_ref[...] = total.astype(bf16)
    for offset in range(1, size):
        copying(offset, lax.rem(place + offset, size)).wait_send()


def remote_params(number):
    return pltpu.CompilerParams(
        collective_id=number, has_side_effects=True, vmem_limit_bytes=VMEM_BYTES
    )


def gather_tp(values, columns, number):
    size = lax.axis_size("tp")
    rows, width = values.shape
    shape = (rows, size * width) if columns else (size * rows, width)
    return pl.pallas_call(
        functools.partial(line_gather, size, columns),
        in_specs=[pl.BlockSpec(memory_space=pl.ANY)],
        out_specs=pl.BlockSpec(memory_space=pl.ANY),
        out_shape=jax.ShapeDtypeStruct(shape, values.dtype),
        scratch_shapes=[
            pltpu.SemaphoreType.DMA,
            pltpu.SemaphoreType.DMA((2, size - 1)),
            pltpu.SemaphoreType.DMA((2, size - 1)),
        ],
        compiler_params=remote_params(number),
        cost_estimate=pl.CostEstimate(flops=0, bytes_accessed=150_000_000, transcendentals=0),
        name="gather_tp",
    )(values)


def scatter_tp(values, columns, number):
    size = lax.axis_size("tp")
    rows, width = values.shape
    shape = (rows, width // size) if columns else (rows // size, width)
    return pl.pallas_call(
        functools.partial(line_scatter, size, columns),
        in_specs=[pl.BlockSpec(memory_space=pltpu.VMEM)],
        out_specs=pl.BlockSpec(memory_space=pltpu.VMEM),
        out_shape=jax.ShapeDtypeStruct(shape, f32),
        scratch_shapes=[
            pltpu.VMEM((2, size - 1, *shape), bf16),
            pltpu.VMEM((2, size - 1, *shape), bf16),
            pltpu.SemaphoreType.DMA((2, size - 1)),
            pltpu.SemaphoreType.DMA((2, size - 1)),
        ],
        compiler_params=remote_params(number),
        cost_estimate=pl.CostEstimate(flops=0, bytes_accessed=150_000_000, transcendentals=0),
        name="scatter_tp",
    )(values)


def close_tp(values, gains, along, number):
    sizes = tuple(lax.axis_size(axis) for axis in ("tp", "ctx", "fsdp"))
    rows, width = values.shape
    shape = (rows, width // sizes[0])
    pad = lambda row: jnp.pad(row, (0, -row.shape[0] % 1024)).reshape(8, -1)
    gains_b, along_b = pad(gains), pad(along)
    narrow, wide = gains_b.shape[1], along_b.shape[1]
    small = jnp.concatenate([gains_b, along_b], axis=1)
    peers = max(sizes) - 1
    out, every, line = pl.pallas_call(
        functools.partial(closing_sums, sizes, narrow),
        in_specs=[pl.BlockSpec(memory_space=pltpu.VMEM)] * 2,
        out_specs=[pl.BlockSpec(memory_space=pltpu.VMEM)] * 3,
        out_shape=[
            jax.ShapeDtypeStruct(shape, f32),
            jax.ShapeDtypeStruct((8, narrow), f32),
            jax.ShapeDtypeStruct((8, wide), f32),
        ],
        scratch_shapes=[
            pltpu.VMEM((2, sizes[0] - 1, *shape), bf16),
            pltpu.VMEM((2, sizes[0] - 1, *shape), bf16),
            pltpu.VMEM((2, *small.shape), f32),
            *[pltpu.VMEM((size - 1, *small.shape), f32) for size in sizes],
            pltpu.SemaphoreType.DMA((2, sizes[0] - 1)),
            pltpu.SemaphoreType.DMA((2, sizes[0] - 1)),
            pltpu.SemaphoreType.DMA((3, peers)),
            pltpu.SemaphoreType.DMA((3, peers)),
        ],
        compiler_params=remote_params(number),
        cost_estimate=pl.CostEstimate(flops=0, bytes_accessed=150_000_000, transcendentals=0),
        name="close_tp",
    )(values, small)
    return out, every.reshape(-1)[: gains.shape[0]], line.reshape(-1)[: along.shape[0]]


def gather_ctx(values, number):
    size = lax.axis_size("ctx")
    rows, width = values.shape
    return pl.pallas_call(
        functools.partial(peer_gather, size),
        in_specs=[pl.BlockSpec(memory_space=pl.ANY)],
        out_specs=pl.BlockSpec(memory_space=pl.ANY),
        out_shape=jax.ShapeDtypeStruct((size * rows, width), values.dtype),
        scratch_shapes=[
            pltpu.SemaphoreType.DMA,
            pltpu.SemaphoreType.DMA((size - 1,)),
            pltpu.SemaphoreType.DMA((size - 1,)),
        ],
        compiler_params=remote_params(number),
        cost_estimate=pl.CostEstimate(flops=0, bytes_accessed=100_000_000, transcendentals=0),
        name="gather_ctx",
    )(values)


def scatter_ctx(values, number):
    size = lax.axis_size("ctx")
    rows, width = values.shape
    shape = (rows // size, width)
    return pl.pallas_call(
        functools.partial(peer_scatter, size),
        in_specs=[pl.BlockSpec(memory_space=pltpu.VMEM)],
        out_specs=pl.BlockSpec(memory_space=pltpu.VMEM),
        out_shape=jax.ShapeDtypeStruct(shape, values.dtype),
        scratch_shapes=[
            pltpu.VMEM((size - 1, *shape), bf16),
            pltpu.SemaphoreType.DMA((size - 1,)),
            pltpu.SemaphoreType.DMA((size - 1,)),
        ],
        compiler_params=remote_params(number),
        cost_estimate=pl.CostEstimate(flops=0, bytes_accessed=100_000_000, transcendentals=0),
        name="scatter_ctx",
    )(values)


def attend(scale, query_ref, key_ref, value_ref, seg_row_ref, seg_column_ref, out_ref, total_ref):
    scores = matmul_nt(key_ref[...], query_ref[...]) * scale
    scores = jnp.where(seg_column_ref[...] == seg_row_ref[...], scores, masked_score)
    most = jnp.max(scores, axis=0, keepdims=True)
    probs = jnp.exp(scores - most)
    total = jnp.sum(probs, axis=0, keepdims=True)
    mixed = matmul(value_ref[...].T, probs.astype(bf16)) / total
    out_ref[...] = mixed.T.astype(bf16)
    total_ref[...] = most + jnp.log(total)


def attend_back(
    scale,
    query_ref,
    key_ref,
    value_ref,
    seg_row_ref,
    seg_column_ref,
    out_ref,
    total_ref,
    grad_ref,
    query_grad_ref,
    key_grad_ref,
    value_grad_ref,
    key_sum_ref,
    value_sum_ref,
):
    step = pl.program_id(1)
    query, key, grad = query_ref[...], key_ref[...], grad_ref[...]
    scores = matmul_nt(key, query) * scale
    scores = jnp.where(seg_column_ref[...] == seg_row_ref[...], scores, masked_score)
    probs = jnp.exp(scores - total_ref[...])
    products = grad.astype(f32) * out_ref[...].astype(f32)
    delta = jnp.sum(products.T, axis=0, keepdims=True)
    score_grad = (probs * (matmul_nt(value_ref[...], grad) - delta)).astype(bf16)
    query_grad_ref[...] = (matmul(key.T, score_grad) * scale).T
    key_part = matmul(score_grad, query) * scale
    value_part = matmul(probs.astype(bf16), grad)

    @pl.when(step == 0)
    def _():
        key_sum_ref[...] = key_part
        value_sum_ref[...] = value_part

    @pl.when(step > 0)
    def _():
        key_sum_ref[...] += key_part
        value_sum_ref[...] += value_part

    @pl.when(step == pl.num_programs(1) - 1)
    def _():
        key_grad_ref[...] = key_sum_ref[...].astype(bf16)
        value_grad_ref[...] = value_sum_ref[...].astype(bf16)


def attention_specs(rows, keys, heads, head_dim):
    block = min(rows, QUERY_BLOCK)
    query = pl.BlockSpec((block, head_dim), lambda h, i: (i, h))
    return (
        (heads, rows // block),
        [
            query,
            pl.BlockSpec((keys, head_dim), lambda h, i: (0, h)),
            pl.BlockSpec((keys, head_dim), lambda h, i: (0, h + heads)),
            pl.BlockSpec((None, 1, block), lambda h, i: (i, 0, 0)),
            pl.BlockSpec((keys, 1), lambda h, i: (0, 0)),
        ],
        query,
        pl.BlockSpec((None, None, 1, block), lambda h, i: (h, i, 0, 0)),
        pl.BlockSpec((keys, head_dim), lambda h, i: (0, h)),
    )


def run_attend(query_b, group, seg_rows, seg_columns, heads, scale):
    rows, keys = query_b.shape[0], group.shape[0]
    head_dim = query_b.shape[1] // heads
    grid, specs, query, total, unused = attention_specs(rows, keys, heads, head_dim)
    work = heads * rows * keys
    return pl.pallas_call(
        functools.partial(attend, scale),
        grid=grid,
        in_specs=specs,
        out_specs=[query, total],
        out_shape=[
            jax.ShapeDtypeStruct(query_b.shape, bf16),
            jax.ShapeDtypeStruct((*grid, 1, rows // grid[1]), f32),
        ],
        compiler_params=params(2),
        cost_estimate=pl.CostEstimate(
            flops=4 * work * head_dim, bytes_accessed=8 * query_b.size, transcendentals=work
        ),
        name="attend",
    )(query_b, group, group, seg_rows, seg_columns)


def run_attend_back(query_b, group, seg_rows, seg_columns, out_b, total, grad_b, heads, scale):
    rows, keys = query_b.shape[0], group.shape[0]
    head_dim = query_b.shape[1] // heads
    grid, specs, query, total_spec, key = attention_specs(rows, keys, heads, head_dim)
    work = heads * rows * keys
    return pl.pallas_call(
        functools.partial(attend_back, scale),
        grid=grid,
        in_specs=[*specs, query, total_spec, query],
        out_specs=[query, key, key],
        out_shape=[
            jax.ShapeDtypeStruct(query_b.shape, f32),
            jax.ShapeDtypeStruct((keys, query_b.shape[1]), bf16),
            jax.ShapeDtypeStruct((keys, query_b.shape[1]), bf16),
        ],
        scratch_shapes=[pltpu.VMEM((keys, head_dim), f32)] * 2,
        compiler_params=params(2),
        cost_estimate=pl.CostEstimate(
            flops=10 * work * head_dim, bytes_accessed=16 * query_b.size, transcendentals=work
        ),
        name="attend_back",
    )(query_b, group, group, seg_rows, seg_columns, out_b, total, grad_b)


def beside(values):
    return lax.ppermute(values, "fsdp", [(0, 1), (1, 0), (2, 3), (3, 2)])


def across(values):
    return lax.ppermute(values, "fsdp", [(0, 2), (1, 3), (2, 0), (3, 1)])


def other(values):
    return lax.ppermute(values, "ctx", [(0, 1), (1, 0)])


def added(*values):
    total = values[0].astype(f32)
    for value in values[1:]:
        total = total + value.astype(f32)
    return total.astype(bf16)


def then(first, *values):
    return lax.optimization_barrier((first, *values))[1:]


def weight_grad(left, right):
    return jnp.einsum("gesa,gesb->eab", left, right, preferred_element_type=f32)


def by_chips():
    return lax.axis_size("fsdp") == 4 and lax.axis_size("ctx") == 2


def chunk_order(chunks):
    if not by_chips():
        return jnp.arange(chunks, dtype=jnp.int32)
    fsdp, ctx = lax.axis_index("fsdp"), lax.axis_index("ctx")
    sibling = fsdp + 1 - 2 * lax.rem(fsdp, 2)
    flip = lambda core: lax.rem(core + 2, 4)
    places = (
        (flip(sibling), ctx),
        (flip(fsdp), ctx),
        (sibling, 1 - ctx),
        (fsdp, 1 - ctx),
        (flip(sibling), 1 - ctx),
        (flip(fsdp), 1 - ctx),
        (sibling, ctx),
        (fsdp, ctx),
    )
    return jnp.stack([jnp.asarray(2 * f + c, jnp.int32) for f, c in places])


def expert_steps(ids, own_tokens, grad_all, rank_rows, rank_columns, first, weights):
    gate_weight, up_weight, down_weight = weights
    chunks = rank_rows.shape[0]

    def one_pass(at, near, far, product, kept):
        return run_expert_pass(
            jnp.array([at, at + 1], jnp.int32),
            first,
            rank_rows,
            rank_columns,
            near,
            far,
            product,
            gate_weight,
            up_weight,
            kept,
        )

    if not by_chips():
        token_all = lax.all_gather(own_tokens, ROWS, axis=0, tiled=True)
        blocks = token_all.reshape(chunks, CHUNK, -1)
        grad_slots, product = run_select_grads(ids, rank_rows, grad_all, down_weight)
        kept, backs = (), []
        for at in range(0, chunks, 2):
            kept, near, far = one_pass(at, blocks[at], blocks[at + 1], product, kept)
            backs += [near, far]
        back_sum = lax.psum_scatter(
            jnp.concatenate(backs), ROWS, scatter_dimension=0, tiled=True
        )
        out_part = run_expert_sums(ids, rank_columns, kept[1], down_weight)
        return kept, grad_slots, back_sum, out_part

    from_across, from_other = across(own_tokens), other(own_tokens)
    from_beside = beside(own_tokens)
    grad_slots, product = run_select_grads(ids, rank_rows, grad_all, down_weight)
    from_across, from_other = then(product, from_across, from_other)
    kept, back_sum, out_part = run_exchange_pass(
        rank_rows,
        rank_columns,
        product,
        weights,
        (own_tokens, from_beside, from_across, from_other),
    )
    return kept, grad_slots, back_sum, out_part


def rotated_sum(values):
    size = lax.axis_size("tp")
    total = values
    for offset in range(1, size):
        pairs = [(at, (at + offset) % size) for at in range(size)]
        total = total + lax.ppermute(values, "tp", pairs)
    return total


def scatter_line(values, beside_steps):
    size, place = lax.axis_size("tp"), lax.axis_index("tp")
    rows = values.shape[0] // size
    block = lambda at: lax.dynamic_slice_in_dim(
        values, jnp.clip(at, 0, size - 1) * rows, rows, 0
    )
    right, left, made = None, None, []
    for step in range(size - 1):
        to_right = block(size - 1 - step + place)
        to_left = block(place - (size - 1 - step))
        if step > 0:
            to_right, to_left = added(to_right, right), added(to_left, left)
        right = lax.ppermute(
            to_right, "tp", [(at, at + 1) for at in range(size - 1) if at <= step]
        )
        left = lax.ppermute(
            to_left, "tp", [(at, at - 1) for at in range(1, size) if size - 1 - at <= step]
        )
        if step < len(beside_steps):
            made.append(beside_steps[step]())
            right, left = then(made[-1], right, left)
    total = block(place).astype(f32) + right.astype(f32) + left.astype(f32)
    return total, made


def head_blocks(width, head_dim):
    for at in range(0, width, head_dim):
        yield slice(at, at + head_dim)


def project(
    input_ref,
    gain_ref,
    weight_ref,
    cosine_ref,
    sine_ref,
    head_gain_ref,
    segment_ref,
    normed_ref,
    inverse_ref,
    pre_ref,
    query_ref,
    group_ref,
):
    values = input_ref[...].astype(f32)
    inverse = norm_scale(values)
    normed = (values * inverse * gain_ref[...]).astype(bf16)
    normed_ref[...] = normed
    inverse_ref[...] = inverse
    qkv = matmul(normed, weight_ref[...])
    width = query_ref.shape[1]
    head_dim = cosine_ref.shape[1]
    pre_ref[...] = qkv[:, : 2 * width]
    cosine, sine = cosine_ref[...], sine_ref[...]
    for which in (0, 1):
        gain = head_gain_ref[which : which + 1, :]
        for at in head_blocks(width, head_dim):
            head = qkv[:, which * width + at.start : which * width + at.stop]
            head = head * norm_scale(head) * gain
            turned = head * cosine + pltpu.roll(head, head_dim // 2, 1) * sine
            to_ref = query_ref if which == 0 else group_ref
            to_ref[:, at] = turned.astype(bf16)
    group_ref[:, width : 2 * width] = qkv[:, 2 * width :].astype(bf16)
    rest = group_ref.shape[1] - 2 * width
    group_ref[:, 2 * width :] = jnp.broadcast_to(
        segment_ref[...], (segment_ref.shape[0], rest)
    ).astype(bf16)


def project_back(
    query_grad_ref,
    group_grad_ref,
    pre_ref,
    cosine_ref,
    sine_ref,
    head_gain_ref,
    weight_ref,
    input_ref,
    inverse_ref,
    gain_ref,
    grad_ref,
    part_ref,
    along_ref,
    terms_ref,
    head_terms_ref,
):
    width = query_grad_ref.shape[1]
    head_dim = cosine_ref.shape[1]
    cosine, sine = cosine_ref[...], sine_ref[...]

    @pl.when(pl.program_id(0) == 0)
    def _():
        terms_ref[...] = jnp.zeros_like(terms_ref)
        head_terms_ref[...] = jnp.zeros_like(head_terms_ref)

    for which in (0, 1):
        gain = head_gain_ref[which : which + 1, :]
        from_ref = query_grad_ref if which == 0 else group_grad_ref
        for at in head_blocks(width, head_dim):
            own = slice(which * width + at.start, which * width + at.stop)
            grad = from_ref[:, at].astype(f32)
            incoming = grad * cosine - pltpu.roll(grad, head_dim // 2, 1) * sine
            head = pre_ref[:, own]
            value_grad, gain_terms = norm_back(incoming, head, norm_scale(head), gain)
            grad_ref[:, own] = value_grad.astype(bf16)
            head_terms_ref[which : which + 1, :] += jnp.sum(gain_terms, axis=0, keepdims=True)
    grad_ref[:, 2 * width :] = group_grad_ref[:, width:]
    part = matmul_nt(grad_ref[...], weight_ref[...])
    part_ref[...] = part.astype(bf16)
    product = part * input_ref[...].astype(f32)
    terms_ref[...] += jnp.sum(product * inverse_ref[...], axis=0, keepdims=True)
    along_ref[...] = jnp.sum(product * gain_ref[...], axis=1, keepdims=True)


def run_project(input_b, gain, full, cosine, sine, head_gains, segment, width):
    rows, depth = input_b.shape
    head_dim = cosine.shape[1]
    block = min(rows, QUERY_BLOCK)
    by_rows = lambda columns: pl.BlockSpec((block, columns), lambda i: (i, 0))
    return pl.pallas_call(
        project,
        grid=(rows // block,),
        in_specs=[
            by_rows(depth),
            once((1, depth)),
            once((depth, 3 * width)),
            by_rows(head_dim),
            by_rows(head_dim),
            once((2, head_dim)),
            by_rows(1),
        ],
        out_specs=[
            by_rows(depth),
            by_rows(1),
            by_rows(2 * width),
            by_rows(width),
            by_rows(2 * width + EXTRA),
        ],
        out_shape=[
            jax.ShapeDtypeStruct((rows, depth), bf16),
            jax.ShapeDtypeStruct((rows, 1), f32),
            jax.ShapeDtypeStruct((rows, 2 * width), f32),
            jax.ShapeDtypeStruct((rows, width), bf16),
            jax.ShapeDtypeStruct((rows, 2 * width + EXTRA), bf16),
        ],
        compiler_params=params(1),
        cost_estimate=pl.CostEstimate(
            flops=6 * rows * depth * width, bytes_accessed=6 * depth * width, transcendentals=0
        ),
        name="project",
    )(input_b, gain, full, cosine, sine, head_gains, segment)


def run_project_back(
    query_grad, group_grad, pre, cosine, sine, head_gains, full, input_b, inverse, gain
):
    rows, depth = input_b.shape
    width = query_grad.shape[1]
    head_dim = cosine.shape[1]
    block = min(rows, QUERY_BLOCK)
    by_rows = lambda columns: pl.BlockSpec((block, columns), lambda i: (i, 0))
    whole = lambda shape: pl.BlockSpec(shape, lambda i: (0, 0))
    return pl.pallas_call(
        project_back,
        grid=(rows // block,),
        in_specs=[
            by_rows(width),
            by_rows(2 * width),
            by_rows(2 * width),
            by_rows(head_dim),
            by_rows(head_dim),
            once((2, head_dim)),
            once((depth, 3 * width)),
            by_rows(depth),
            by_rows(1),
            once((1, depth)),
        ],
        out_specs=[
            by_rows(3 * width),
            by_rows(depth),
            by_rows(1),
            whole((1, depth)),
            whole((2, head_dim)),
        ],
        out_shape=[
            jax.ShapeDtypeStruct((rows, 3 * width), bf16),
            jax.ShapeDtypeStruct((rows, depth), bf16),
            jax.ShapeDtypeStruct((rows, 1), f32),
            jax.ShapeDtypeStruct((1, depth), f32),
            jax.ShapeDtypeStruct((2, head_dim), f32),
        ],
        compiler_params=params(1),
        cost_estimate=pl.CostEstimate(
            flops=6 * rows * depth * width, bytes_accessed=8 * depth * width, transcendentals=0
        ),
        name="project_back",
    )(query_grad, group_grad, pre, cosine, sine, head_gains, full, input_b, inverse, gain)


def split_three(values):
    high = values.astype(bf16)
    rest = values - high.astype(f32)
    middle = rest.astype(bf16)
    return (high, middle, (rest - middle.astype(f32)).astype(bf16))


def on_device(
    layer_input,
    token_order,
    doc_lengths,
    expert_routes,
    attn_gain,
    query_weight,
    key_weight,
    value_weight,
    query_gain,
    key_gain,
    out_weight,
    moe_gain,
    router_weight,
    gate_weight,
    up_weight,
    down_weight,
    out_grad,
):
    tp_index = lax.axis_index("tp")
    ctx_size = lax.axis_size("ctx")
    fc_size = lax.axis_size("fsdp") * ctx_size
    fc_index = lax.axis_index("fsdp") * ctx_size + lax.axis_index("ctx")
    tok_count, quarter = layer_input.shape
    share = tok_count // lax.axis_size("tp")
    head_dim = query_gain.shape[0]
    head_width = query_weight.shape[1]
    heads = head_width // head_dim
    scale = head_dim ** (-0.5)
    experts = router_weight.shape[1]
    top = expert_routes.shape[1]
    local_experts = gate_weight.shape[0]
    capacity = tok_count * top * 5 // (4 * experts)
    own_rows = lambda values: lax.dynamic_slice_in_dim(values, tp_index * share, share, 0)
    own_width = lambda values: lax.dynamic_slice_in_dim(values, tp_index * quarter, quarter, 1)

    packed = jnp.concatenate(
        [
            query_weight,
            key_weight,
            value_weight,
            out_weight.T,
            router_weight,
            attn_gain[:, None],
            moe_gain[:, None],
            jnp.zeros((attn_gain.shape[0], EXTRA - experts - 2), bf16),
        ],
        axis=1,
    )
    full = lax.all_gather(packed, ROWS, axis=0, tiled=True)
    expert_ids = jnp.arange(experts, dtype=jnp.int32)
    named = jnp.any(expert_routes[:, :, None] == expert_ids[None, None, :], axis=1)
    earlier = jnp.tri(tok_count, tok_count, -1, dtype=bf16)
    before = matmul(earlier, named.astype(bf16))
    first_slot = (lax.rem(fc_index, CHUNK // tok_count) * capacity).astype(f32)
    ranks = jnp.where(named, before + first_slot, -1.0).astype(bf16)
    input_b = gather_tp(layer_input, True, 0)
    out_grad, full, input_b = lax.optimization_barrier((out_grad, full, input_b))
    grad_rows_b = lax.all_gather(out_grad, "tp", axis=1, tiled=True)
    side = 3 * head_width
    qkv_weight = full[:, :side]
    full_out = full[:, side : side + head_width]
    side = side + head_width
    full_router = full[:, side : side + experts]
    attn_gain_f = full[:, side + experts].astype(f32)
    moe_gain_f = full[:, side + experts + 1].astype(f32)
    width = input_b.shape[1]
    segment, position = doc_places(token_order[0], doc_lengths[0])
    cosine, sine = rope_tables(position, head_dim)
    head_gains = jnp.stack([query_gain, key_gain])
    attn_gain_row = attn_gain_f[None, :]
    normed, inverse_one, heads_pre, query_rows, group_part = run_project(
        input_b,
        attn_gain_row,
        full,
        cosine,
        sine,
        head_gains,
        segment.astype(f32)[:, None],
        head_width,
    )
    group = gather_ctx(group_part, 1)
    after_group, group = lax.optimization_barrier((grad_rows_b, group))
    grad_packed = jnp.concatenate(
        [after_group, ranks, jnp.zeros((tok_count, EXTRA - experts), bf16)], axis=1
    )
    grad_all = lax.all_gather(grad_packed, ROWS, axis=0, tiled=True)
    chunks = grad_all.shape[0] // CHUNK
    first_expert = fc_index * local_experts
    local_ranks = lax.dynamic_slice_in_dim(
        grad_all[:, width:], first_expert, local_experts, 1
    ).astype(jnp.int32)
    ids = chunk_order(chunks)
    rank_columns = jnp.stack(
        [
            lax.dynamic_slice_in_dim(local_ranks, ids[at] * CHUNK, CHUNK, 0)
            for at in range(chunks)
        ]
    )
    rank_rows = jnp.transpose(rank_columns, (0, 2, 1))[:, :, None, :]

    seg_rows = segment.astype(f32).reshape(-1, 1, min(tok_count, QUERY_BLOCK))
    seg_columns = group[:, 2 * head_width : 2 * head_width + 1].astype(f32)
    attn_b, log_total = run_attend(query_rows, group, seg_rows, seg_columns, heads, scale)
    attn_part = matmul_nt(attn_b, full_out).astype(bf16)
    attn_out = scatter_tp(attn_part, False, 2)
    resid = own_rows(input_b).astype(f32) + attn_out
    inverse_two = norm_scale(resid)
    moe_in = (resid * inverse_two * moe_gain_f).astype(bf16)
    logits = matmul(moe_in, full_router)
    own_named = own_rows(named)
    chosen = jnp.where(own_named, logits, -jnp.inf)
    gates = jax.nn.softmax(chosen, axis=-1)
    own_tokens = gather_tp(
        jnp.concatenate(
            [moe_in, *split_three(gates), jnp.zeros((share, EXTRA - 3 * experts), bf16)], axis=1
        ),
        False,
        3,
    )
    kept, grad_slots, back_sum, out_part = expert_steps(
        ids,
        own_tokens,
        grad_all,
        rank_rows,
        rank_columns,
        first_expert.reshape(1),
        (gate_weight, up_weight, down_weight),
    )
    token_slots, hidden_rows, gate_act_grad, up_act_grad, route_part = kept
    hit = jnp.arange(chunks, dtype=jnp.int32)[:, None] == ids[None, :]
    route_all = jnp.sum(
        jnp.where(hit[:, :, None, None], route_part[None, :, :, 0, :], 0.0), axis=1
    )
    route_all = jnp.transpose(route_all, (1, 0, 2)).reshape(
        local_experts, fc_size, tok_count
    )
    route_all = lax.all_to_all(
        jnp.transpose(route_all, (1, 0, 2)), ROWS, split_axis=0, concat_axis=0, tiled=True
    ).reshape(experts, tok_count)

    back_rows, ((grad_gate, gate_grad), grad_up, grad_down) = scatter_line(
        back_sum,
        (
            lambda: (weight_grad(token_slots, gate_act_grad), rotated_sum(route_all)),
            lambda: weight_grad(token_slots, up_act_grad),
            lambda: weight_grad(hidden_rows, grad_slots),
        ),
    )
    parts = own_tokens[:, width : width + 3 * experts].astype(f32)
    all_gates = parts[:, :experts] + parts[:, experts : 2 * experts] + parts[:, 2 * experts :]
    gate_grad = gate_grad.T
    logit_grad = all_gates * (
        gate_grad - jnp.sum(all_gates * gate_grad, axis=-1, keepdims=True)
    )
    grad_router = lax.dot_general(
        own_tokens[:, :width].astype(f32),
        logit_grad,
        (((0,), (0,)), ((), ())),
        precision=highest,
    )
    own_logit_grad = own_rows(logit_grad)
    router_back = lax.dot_general(
        own_logit_grad, full_router.astype(f32), (((1,), (1,)), ((), ())), precision=highest
    )
    moe_in_grad = (
        back_rows + router_back
    )
    resid_norm_grad, gain_terms = norm_back(moe_in_grad, resid, inverse_two, moe_gain_f)
    grad_moe_gain = jnp.sum(gain_terms, axis=0)
    resid_grad = own_rows(grad_rows_b).astype(f32) + resid_norm_grad
    resid_grad_b = gather_tp(resid_grad.astype(bf16), False, 5)

    out_sum = lax.psum_scatter(out_part, ROWS, scatter_dimension=0, tiled=True)

    grad_out = lax.dot_general(
        resid_grad_b, attn_b, (((0,), (0,)), ((), ())), preferred_element_type=f32
    )
    attn_grad = matmul(resid_grad_b, full_out).astype(bf16)
    query_rot_grad, key_part, value_part = run_attend_back(
        query_rows, group, seg_rows, seg_columns, attn_b, log_total, attn_grad, heads, scale
    )
    out_sum, key_part = lax.optimization_barrier((out_sum, key_part))
    out_sum = lax.psum_scatter(out_sum, "tp", scatter_dimension=0, tiled=True).astype(f32)
    group_grad = scatter_ctx(jnp.concatenate([key_part, value_part], axis=1), 6)
    qkv_grad, normed_part, along, attn_terms, head_terms = run_project_back(
        query_rot_grad,
        group_grad,
        heads_pre,
        cosine,
        sine,
        head_gains,
        full,
        input_b,
        inverse_one,
        attn_gain_row,
    )
    along = along[:, 0]
    gains = jnp.concatenate([attn_terms[0], grad_moe_gain, head_terms[0], head_terms[1]])
    normed_grad, gains, along = close_tp(normed_part, gains, along, 7)
    along = along[:, None] / width
    normed_grad, out_sum = lax.optimization_barrier((normed_grad, out_sum))
    layer_sum = resid + out_sum
    layer_output = lax.all_to_all(
        layer_sum.astype(bf16), "tp", split_axis=1, concat_axis=0, tiled=True
    )
    input_quarter = layer_input.astype(f32)
    gain_quarter = lax.dynamic_slice_in_dim(attn_gain_f, tp_index * quarter, quarter, 0)
    grad_input = own_width(resid_grad_b).astype(f32) + inverse_one * (
        normed_grad * gain_quarter - input_quarter * inverse_one * inverse_one * along
    )
    grad_qkv = lax.dot_general(
        normed, qkv_grad, (((0,), (0,)), ((), ())), preferred_element_type=f32
    )
    owned_out = lax.psum_scatter(
        jnp.concatenate(
            [grad_out, grad_router, jnp.zeros((width, EXTRA - experts), f32)], axis=1
        ).astype(bf16),
        ROWS,
        scatter_dimension=0,
        tiled=True,
    )
    (owned_out,) = then(normed_grad, owned_out)
    owned_out = owned_out.astype(f32)
    owned_qkv = lax.psum_scatter(
        grad_qkv.astype(bf16), ROWS, scatter_dimension=0, tiled=True
    ).astype(f32)
    owned_gain = attn_gain.shape[0]
    own_gain = lambda at: lax.dynamic_slice_in_dim(
        gains, at * width + fc_index * owned_gain, owned_gain, 0
    )
    return (
        layer_output,
        grad_input,
        own_gain(0),
        owned_qkv[:, :head_width],
        owned_qkv[:, head_width : 2 * head_width],
        owned_qkv[:, 2 * head_width :],
        gains[2 * width : 2 * width + head_dim],
        gains[2 * width + head_dim :],
        owned_out[:, :head_width].T,
        own_gain(1),
        owned_out[:, head_width : head_width + experts],
        grad_gate,
        grad_up,
        grad_down,
    )


def solution(mesh):
    in_specs = (
        P(("fsdp", "ctx"), "tp"),
        P("fsdp", "ctx"),
        P("fsdp", None),
        P(("fsdp", "ctx"), None),
        P(("fsdp", "ctx")),
        P(("fsdp", "ctx"), "tp"),
        P(("fsdp", "ctx"), "tp"),
        P(("fsdp", "ctx"), "tp"),
        P(),
        P(),
        P("tp", ("fsdp", "ctx")),
        P(("fsdp", "ctx")),
        P(("fsdp", "ctx"), None),
        P(("fsdp", "ctx"), None, "tp"),
        P(("fsdp", "ctx"), None, "tp"),
        P(("fsdp", "ctx"), "tp", None),
        P(("fsdp", "ctx"), "tp"),
    )
    out_specs = (
        P(("fsdp", "ctx"), "tp"),
        P(("fsdp", "ctx"), "tp"),
        P(("fsdp", "ctx")),
        P(("fsdp", "ctx"), "tp"),
        P(("fsdp", "ctx"), "tp"),
        P(("fsdp", "ctx"), "tp"),
        P(),
        P(),
        P("tp", ("fsdp", "ctx")),
        P(("fsdp", "ctx")),
        P(("fsdp", "ctx"), None),
        P(("fsdp", "ctx"), None, "tp"),
        P(("fsdp", "ctx"), None, "tp"),
        P(("fsdp", "ctx"), "tp", None),
    )
    return jax.shard_map(
        on_device, mesh=mesh, in_specs=in_specs, out_specs=out_specs, check_vma=False
    )
```

time: 1640 us -> 952 us (0.58)
  waiting for transfers between devices: 1020 us -> 42 us
  Pallas kernels: 207 us -> 706 us
  matrix products: 173 us -> 95.3 us
  local copies, waits for them, and re-layouts: 87.6 us -> 33.1 us
  blocking collectives: 48.5 us -> 0 us
  other arithmetic: 64.9 us -> 31.8 us
    pallas_call x3 -> x13, Pallas kernels: 207 us -> 706 us  [the longest x1 201 us: run_exchange_pass(): pl.pallas_call(exchange_pass, grid=(2 * chunks, local), in_specs=[pl.Bloc...]
    all_gather x5 -> x0, waiting for transfers between devices: 275 us -> none  [the longest x1 103 us: on_device(): lax.all_gather(jnp.concatenate([moe_in, *split_three(gates), jnp.zeros((s...]
    reduce_scatter x5 -> x0, waiting for transfers between devices: 249 us -> none  [the longest x1 117 us: on_device(): lax.psum_scatter(back_part, ROWS, scatter_dimension=0, tiled=True)]
    reduce_scatter x1, waiting for transfers between devices: 160 us -> 0.01 us  [on_device(): out_sum = lax.psum_scatter(out_part, ROWS, scatter_dimension=0, tiled=True)]
    all_gather x1, waiting for transfers between devices: 129 us -> 0.01 us  [on_device(): grad_all = lax.all_gather(grad_packed, ROWS, axis=0, tiled=True)]
    dot_general x24 -> x3, matrix products: 125 us -> 64.6 us  [weight_grad(): return jnp.einsum('gesa,gesb->eab', left, right, preferred_element_type=f32)]
    reduce_scatter x1, waiting for transfers between devices: 59 us -> 0.02 us  [on_device(): lax.psum_scatter(out_sum, 'tp', scatter_dimension=0, tiled=True).astype(f32)]
    psum x2 -> x0, blocking collectives: 48.5 us -> none  [the longest x1 38.6 us: on_device(): lax.psum(jnp.concatenate([attn_terms, grad_moe_gain, jnp.sum(query_gain_t...]
  transfers between devices with their start and end apart: 20 -> 21, of which waited for: 17 -> 9; matrix products, arithmetic and copies ran while one was open for 13% -> 15% of each run, Pallas kernels for 6% -> 53%
where the time goes in v2:
time: 952 us; the launch traced here: 950 us
  Pallas kernels  706 us (74%)
  matrix products  95.3 us (10%)
  waiting for transfers between devices  42 us (4%)
  local copies, waits for them, and re-layouts  33.1 us (3%)
  other arithmetic  31.8 us (3%)
  starting transfers between devices  26.5 us (3%)
  between operations  15.2 us (2%)
    pallas_call x1, Pallas kernels, run_exchange_pass(): pl.pallas_call(exchange_pass, grid=(2 * chunks, local), in_specs=[pl.Bloc...  201 us
    pallas_call x3, Pallas kernels, gather_tp(): pl.pallas_call(functools.partial(line_gather, size, columns), in_specs=[p...  168 us
    dot_general x3, matrix products, weight_grad(): return jnp.einsum('gesa,gesb->eab', left, right, preferred_element_type=f32)  64.6 us
    pallas_call x1, Pallas kernels, close_tp(): pl.pallas_call(functools.partial(closing_sums, sizes, narrow), in_specs=[...  61 us
    pallas_call x1, Pallas kernels, scatter_tp(): pl.pallas_call(functools.partial(line_scatter, size, columns), in_specs=[...  59.3 us
    pallas_call x1, Pallas kernels, run_select_grads(): pl.pallas_call(select_grads, grid_spec=pltpu.PrefetchScalarGridSpec(num_s...  56.3 us
    pallas_call x1, Pallas kernels, gather_ctx(): pl.pallas_call(functools.partial(peer_gather, size), in_specs=[pl.BlockSp...  55.8 us
    pallas_call x1, Pallas kernels, scatter_ctx(): pl.pallas_call(functools.partial(peer_scatter, size), in_specs=[pl.BlockS...  37.2 us
  transfers between devices with their start and end apart: 21, of which 9 were waited for; matrix products, arithmetic and copies ran while one was open for 15% of the time, Pallas kernels for 53%

profile of v2, /device:TPU:0, one launch (start us, length us, event | category | flops | bytes accessed | tf_op | source)
XLA Modules:
  0.0 950.2 jit_solution(7824708801607121341)
XLA Ops:
  7.2 1.1 copy.154
  10.7 3.0 concatenate.28
  13.9 57.8 %gather_tp.3.input_ref = bf16[768,2048]{1,0:T(8,128)(2,1)} custom-call(bf16[768,512]{1,0:T(8,128)(2,1)} %in_ref.1), custom_call_target="tpu_custom_call" | custom-call | bytes 150000000 | tf_op jit(solution)/shard_map/gather_tp/pallas_call | solution.py:1117
  71.6 1.6 all-gather.4.cloned.1.call-done.weight_ref
  75.5 1.4 fusion.22
  76.9 1.2 pad_maximum_fusion.1
  78.7 2.6 convert_reduce_fusion
  81.3 11.0 %project.1 = (bf16[768,2048]{1,0:T(8,128)(2,1)}, f32[768,1]{1,0:T(8,128)}, f32[768,1024]{1,0:T(8,128)}, bf16[768,512]{1,0:T(8,128)(2,1)}, bf16[768,1152]{1,0:T(8,128)(2,1)}) custom-call(bf16[768,2048]{1,0:T(8,128)(2,1)} %gather_tp.3.input_ref, f32[1,2048]{1,0:T(1,128)} %bitcast.90, bf16[2048,2176]{1,0:T(8,128)(2,1)} %all-gather.4.cloned.1.call-done.weight_ref, ...), custom_call_target="tpu_custom_call" | custom-call | flops 4831838208 | bytes 6291456 | tf_op jit(solution)/shard_map/project/pallas_call | solution.py:1571
  92.3 55.8 %gather_ctx.1.key_ref.value_ref = bf16[1536,1152]{1,0:T(8,128)(2,1)} custom-call(bf16[768,1152]{1,0:T(8,128)(2,1)} %get-tuple-element.63.in_ref), custom_call_target="tpu_custom_call" | custom-call | bytes 100000000 | tf_op jit(solution)/shard_map/gather_ctx/pallas_call | solution.py:1192
  148.2 6.0 concatenate.31
  155.4 2.0 slice_convert_fusion.1.seg_column_ref
  157.4 15.9 %attend.1 = (bf16[768,512]{1,0:T(8,128)(2,1)}, f32[4,3,1,256]{3,2,1,0:T(1,128)}) custom-call(bf16[768,512]{1,0:T(8,128)(2,1)} %get-tuple-element.61.query_ref, bf16[1536,1152]{1,0:T(8,128)(2,1)} %gather_ctx.1.key_ref.value_ref, bf16[1536,1152]{1,0:T(8,128)(2,1)} %gather_ctx.1.key_ref.value_ref, f32[3,1,256]{2,1,0:T(1,128)} %convert_element_type.188.seg_row_ref, ...), custom_call_target="tpu_custom_call" | custom-call | flops 2415919104 | bytes 3145728 | tf_op jit(solution)/shard_map/attend/pallas_call | solution.py:1306
  173.3 5.3 convolution_convert_fusion.1.in_ref
  178.6 59.3 %scatter_tp.1 = f32[192,2048]{1,0:T(8,128)} custom-call(bf16[768,2048]{1,0:T(8,128)(2,1)} %convolution_convert_fusion.1.in_ref), custom_call_target="tpu_custom_call" | custom-call | bytes 150000000 | tf_op jit(solution)/shard_map/scatter_tp/pallas_call | solution.py:1137
  238.0 1.9 multiply_reduce_fusion.2
  239.9 1.1 copy-done
  241.2 1.5 fusion.38
  243.1 1.1 concatenate.32.in_ref
  244.2 54.6 %gather_tp.4.own_ref = bf16[768,2176]{1,0:T(8,128)(2,1)} custom-call(bf16[192,2176]{1,0:T(8,128)(2,1)} %concatenate.32.in_ref), custom_call_target="tpu_custom_call" | custom-call | bytes 150000000 | tf_op jit(solution)/shard_map/gather_tp/pallas_call | solution.py:1117
  299.6 1.4 collective-permute-start.2
  301.1 1.5 slice-done
  303.5 1.8 copy.181.rank_ref
  305.3 56.3 %select_grads.1 = (bf16[8,4,256,2048]{3,2,1,0:T(8,128)(2,1)}, f32[8,4,256,256]{3,2,1,0:T(8,128)}) custom-call(s32[8]{0:T(128)} %stack.83.ids_ref, s32[8,4,1,768]{3,2,1,0:T(1,128)} %copy.181.rank_ref, bf16[6144,2176]{1,0:T(8,128)(2,1)} %all-gather.8.cloned.1.call-done.grad_ref, bf16[4,256,2048]{2,1,0:T(8,128)(2,1)} %down_ref.1), custom_call_target="tpu_custom_call" | custom-call | flops 34359738368 | bytes 58720256 | tf_op jit(solution)/shard_map/select_grads/pallas_call | solution.py:580
  361.6 8.8 collective-permute-done.1.from_across_ref
  371.2 200.8 %exchange_pass.1 = (bf16[8,4,256,2048]{3,2,1,0:T(8,128)(2,1)}, bf16[8,4,256,256]{3,2,1,0:T(8,128)(2,1)}, bf16[8,4,256,256]{3,2,1,0:T(8,128)(2,1)}, bf16[8,4,256,...) custom-call(s32[8,4,1,768]{3,2,1,0:T(1,128)} %copy.181.rank_ref, ...), custom_call_target="tpu_custom_call" | custom-call | flops 85899345920 | bytes 71303168 | tf_op jit(solution)/shard_map/exchange_pass/pallas_call | solution.py:623
  572.6 1.0 slice_convert_fusion.2
  573.6 0.9 select_reduce_fusion
  574.6 3.4 all-to-all-start
  578.0 3.1 constant_dynamic-slice_fusion
  581.0 1.6 collective-permute-start.6
  583.6 2.4 collective-permute-start.4
  586.0 1.4 collective-permute-start.5
  587.5 24.6 %convolution_bitcast_fusion = f32[4,2048,256]{2,1,0:T(8,128)} fusion(bf16[8,4,256,2048]{3,2,1,0:T(8,128)(2,1)} %get-tuple-element.74, bf16[8,4,256,256]{3,2,1,0:T(8,128)(2,1)} %get-tuple-element.76), kind=kOutput, calls=%fused_computation.1 | convolution fusion | flops 8589934592 | bytes 46137344 | tf_op jit(solution)/shard_map/gesa,gesb->eab/dot_general | solution.py:1371
  612.2 5.3 collective-permute-done.4
  617.5 7.9 collective-permute-done.5
  626.5 1.3 collective-permute-start.8
  628.5 20.5 %convolution_bitcast_fusion.1 = f32[4,2048,256]{2,1,0:T(8,128)} fusion(bf16[8,4,256,2048]{3,2,1,0:T(8,128)(2,1)} %get-tuple-element.74, bf16[8,4,256,256]{3,2,1,0:T(8,128)(2,1)} %get-tuple-element.75), kind=kOutput, calls=%fused_computation.2 | convolution fusion | flops 8589934592 | bytes 46137344 | tf_op jit(solution)/shard_map/gesa,gesb->eab/dot_general | solution.py:1371
  649.1 1.9 add_convert_fusion.2
  650.9 7.3 collective-permute-start.10
  658.2 1.3 collective-permute-start.11
  659.5 19.6 %convolution_bitcast_fusion.2 = f32[4,256,2048]{2,1,0:T(8,128)} fusion(bf16[8,4,256,256]{3,2,1,0:T(8,128)(2,1)} %get-tuple-element.72, bf16[8,4,256,2048]{3,2,1,0:T(8,128)(2,1)} %get-tuple-element.73), kind=kOutput, calls=%fused_computation.3 | convolution fusion | flops 8589934592 | bytes 46137344 | tf_op jit(solution)/shard_map/gesa,gesb->eab/dot_general | solution.py:1371
  679.6 3.1 multiply_reduce_fusion
  682.7 2.6 add_convert_fusion.1.in_ref
  685.3 55.7 %gather_tp.5 = bf16[768,2048]{1,0:T(8,128)(2,1)} custom-call(bf16[192,2048]{1,0:T(8,128)(2,1)} %add_convert_fusion.1.in_ref), custom_call_target="tpu_custom_call" | custom-call | bytes 150000000 | tf_op jit(solution)/shard_map/gather_tp/pallas_call | solution.py:1117
  741.0 5.2 fusion.9.grad_ref
  746.2 22.0 %attend_back.1 = (f32[768,512]{1,0:T(8,128)}, bf16[1536,512]{1,0:T(8,128)(2,1)}, bf16[1536,512]{1,0:T(8,128)(2,1)}) custom-call(bf16[768,512]{1,0:T(8,128)(2,1)} %get-tuple-element.61.query_ref, bf16[1536,1152]{1,0:T(8,128)(2,1)} %gather_ctx.1.key_ref.value_ref, bf16[1536,1152]{1,0:T(8,128)(2,1)} %gather_ctx.1.key_ref.value_ref, ...), custom_call_target="tpu_custom_call" | custom-call | flops 6039797760 | bytes 6291456 | tf_op jit(solution)/shard_map/attend_back/pallas_call | solution.py:1328
  768.6 3.8 fusion.3
  772.4 1.9 convolution_convert_fusion.2
  774.3 1.9 maximum_maximum_fusion
  776.3 3.5 pad_maximum_fusion.in_ref
  779.8 37.2 %scatter_ctx.1.group_grad_ref = bf16[768,1024]{1,0:T(8,128)(2,1)} custom-call(bf16[1536,1024]{1,0:T(8,128)(2,1)} %pad_maximum_fusion.in_ref), custom_call_target="tpu_custom_call" | custom-call | bytes 100000000 | tf_op jit(solution)/shard_map/scatter_ctx/pallas_call | solution.py:1212
  817.0 18.8 %project_back.1 = (bf16[768,1536]{1,0:T(8,128)(2,1)}, bf16[768,2048]{1,0:T(8,128)(2,1)}, f32[768,1]{1,0:T(8,128)}, f32[1,2048]{1,0:T(1,128)}, f32[2,128]{1,0:T(2,128)}) custom-call(f32[768,512]{1,0:T(8,128)} %get-tuple-element.84.query_grad_ref, bf16[768,1024]{1,0:T(8,128)(2,1)} %scatter_ctx.1.group_grad_ref, f32[768,1024]{1,0:T(8,128)} %get-tuple-element.89.pre_ref, ...), custom_call_target="tpu_custom_call" | custom-call | flops 4831838208 | bytes 8388608 | tf_op jit(solution)/shard_map/project_back/pallas_call | solution.py:1614
  835.8 9.3 convolution_convert_fusion
  846.9 61.0 %close_tp.1 = (f32[768,512]{1,0:T(8,128)}, f32[8,640]{1,0:T(8,128)}, f32[8,128]{1,0:T(8,128)}) custom-call(bf16[768,2048]{1,0:T(8,128)(2,1)} %get-tuple-element.91.in_ref, f32[8,768]{1,0:T(8,128)} %pad_maximum_fusion.3.small_ref), custom_call_target="tpu_custom_call" | custom-call | bytes 150000000 | tf_op jit(solution)/shard_map/close_tp/pallas_call | solution.py:1163
  907.9 1.3 convert_element_type.220
  909.5 0.9 copy.208
  910.4 3.6 all-to-all-start.1
  914.1 1.3 slice_convert_fusion
  916.9 1.0 convert_element_type.227
  917.9 1.3 slice.102
  920.1 2.8 multiply_add_fusion
  922.9 10.3 %all-to-all-done.1 = bf16[192,4,512]{2,0,1:T(8,128)(2,1)S(1)} async-done(((bf16[192,4,512]{2,0,1:T(8,128)(2,1)}), bf16[192,4,512]{2,0,1:T(8,128)(2,1)S(1)}, u32[]{:S(2)}, u32[]{:S(2)}) %all-to-all-start.1) | async-done | bytes 786464 | tf_op jit(solution)/shard_map/all_to_all | solution.py:1861
  933.2 6.7 reduce-scatter.9.cloned.1.call-done
  939.9 2.3 fusion.35
  (144 shorter events, 19.2 us)
Async XLA Ops:
  7.2 66.1 %all-gather.4.cloned.1.call-start = ((), (), s32[]{:S(2)}) async-start(), calls=%async_computation.6 | async-start | bytes 10027008 | tf_op jit(solution)/shard_map/all_gather | solution.py:1707
  13.7 59.6 %copy-start.19 = (s32[1,768]{1,0:T(1,128)S(1)}, s32[1,768]{1,0:T(1,128)}, u32[]{:S(2)}) copy-start(s32[1,768]{1,0:T(1,128)} %param.18) | copy-start | bytes 9220
  13.7 59.6 %copy-start.24 = (s32[1,3]{1,0:T(1,128)S(1)}, s32[1,3]{1,0:T(1,128)}, u32[]{:S(2)}) copy-start(s32[1,3]{1,0:T(1,128)} %param.19) | copy-start | bytes 40
  13.7 60.8 %copy-start.13 = (s32[768,8]{0,1:T(8,128)S(1)}, s32[768,8]{0,1:T(8,128)}, u32[]{:S(2)}) copy-start(s32[768,8]{0,1:T(8,128)} %param.20) | copy-start | bytes 73732
  13.8 61.1 %copy-start.22 = (f32[128]{0:T(128)S(1)}, f32[128]{0:T(128)}, u32[]{:S(2)}) copy-start(f32[128]{0:T(128)} %param.26) | copy-start | bytes 1540
  13.8 61.1 %copy-start.23 = (f32[128]{0:T(128)S(1)}, f32[128]{0:T(128)}, u32[]{:S(2)}) copy-start(f32[128]{0:T(128)} %param.25) | copy-start | bytes 1540
  13.8 134.3 %all-gather.6.cloned.1.call-start = ((), (), s32[]{:S(2)}) async-start(), calls=%async_computation.7 | async-start | bytes 3932160 | tf_op jit(solution)/shard_map/all_gather | solution.py:1716
  73.3 227.8 %all-gather.8.cloned.1.call-start = ((), (), s32[]{:S(2)}) async-start(), calls=%async_computation.8 | async-start | bytes 30081024 | tf_op jit(solution)/shard_map/all_gather | solution.py:1744
  81.3 158.6 %copy-start.10 = (f32[2048]{0:T(1024)}, f32[2048]{0:T(1024)S(1)}, u32[]{:S(2)}) copy-start(f32[2048]{0:T(1024)S(1)} %get-tuple-element.104) | copy-start | bytes 24580
  154.1 614.0 %reduce-scatter.5.cloned.1.call-start = ((), (), s32[]{:S(2)}) async-start(), calls=%async_computation.9 | async-start | bytes 28311552 | tf_op jit(solution)/shard_map/reduce_scatter | solution.py:1831
  239.9 1.1 copy-start
  239.9 3.2 copy-start.15
  298.8 71.6 %collective-permute-start.1 = (bf16[768,2176]{1,0:T(8,128)(2,1)}, bf16[768,2176]{1,0:T(8,128)(2,1)}, u32[]{:S(2)}, u32[]{:S(2)}) collective-permute-start(bf16[768,2176]{1,0:T(8,128)(2,1)} %gather_tp.4.own_ref), channel_id=1, source_target_pairs={{0,16},{8,24},{16,0},{24,8},{1,17},{9,25},{17,1},{25,9},{2,18},{10... | collective-permute-start | bytes 10027016 | tf_op jit(solution)/shard_map/ppermute | solution.py:1352
  299.6 71.6 %collective-permute-start.2 = (bf16[768,2176]{1,0:T(8,128)(2,1)}, bf16[768,2176]{1,0:T(8,128)(2,1)}, u32[]{:S(2)}, u32[]{:S(2)}) collective-permute-start(bf16[768,2176]{1,0:T(8,128)(2,1)} %gather_tp.4.own_ref), channel_id=1, source_target_pairs={{0,4},{4,0},{1,5},{5,1},{2,6},{6,2},{3,7},{7,3},{8,12},{12,8},{9,1... | collective-permute-start | bytes 10027016 | tf_op jit(solution)/shard_map/ppermute | solution.py:1356
  301.1 70.2 %collective-permute-start = (bf16[768,2176]{1,0:T(8,128)(2,1)}, bf16[768,2176]{1,0:T(8,128)(2,1)}, u32[]{:S(2)}, u32[]{:S(2)}) collective-permute-start(bf16[768,2176]{1,0:T(8,128)(2,1)} %gather_tp.4.own_ref), channel_id=1, source_target_pairs={{0,8},{8,0},{16,24},{24,16},{1,9},{9,1},{17,25},{25,17},{2,10},{10... | collective-permute-start | bytes 10027016 | tf_op jit(solution)/shard_map/ppermute | solution.py:1348
  301.1 1.5 slice-start
  303.5 58.1 %copy-start.4 = (s32[8,768,4]{2,1,0:T(8,128)}, s32[8,768,4]{2,1,0:T(8,128)S(1)}, u32[]{:S(2)}) copy-start(s32[8,768,4]{2,1,0:T(8,128)S(1)} %bitcast_dynamic-update-slice_fusion.column_ref) | copy-start | bytes 294916
  572.0 0.6 copy-start.21
  572.0 1.5 copy-start.12
  574.6 8.8 all-to-all-start
  577.9 330.0 %reduce-scatter.7.cloned.1.call-start = ((), (), s32[]{:S(2)}) async-start(), calls=%async_computation.10 | async-start | bytes 3932160 | tf_op jit(solution)/shard_map/reduce_scatter | solution.py:1841
  581.0 44.8 %collective-permute-start.6 = (bf16[192,2048]{1,0:T(8,128)(2,1)}, bf16[192,2048]{1,0:T(8,128)(2,1)S(1)}, u32[]{:S(2)}, u32[]{:S(2)}) collective-permute-start(bf16[192,2048]{1,0:T(8,128)(2,1)} %get-tuple-element.119), channel_id=1, source_target_pairs={{0,1},{4,5},{8,9},{12,13},{16,17},{20,21},{24,25},{28,29}} | collective-permute-start | bytes 2359304 | tf_op jit(solution)/shard_map/ppermute | solution.py:1464
  582.6 43.2 %collective-permute-start.7 = (bf16[192,2048]{1,0:T(8,128)(2,1)}, bf16[192,2048]{1,0:T(8,128)(2,1)S(1)}, u32[]{:S(2)}, u32[]{:S(2)}) collective-permute-start(bf16[192,2048]{1,0:T(8,128)(2,1)} %get-tuple-element.118), channel_id=1, source_target_pairs={{3,2},{7,6},{11,10},{15,14},{19,18},{23,22},{27,26},{31,30}} | collective-permute-start | bytes 2359304 | tf_op jit(solution)/shard_map/ppermute | solution.py:1467
  583.6 28.6 %collective-permute-start.3 = (f32[32,768]{0,1:T(8,128)S(1)}, f32[32,768]{0,1:T(8,128)S(1)}, u32[]{:S(2)}, u32[]{:S(2)}) collective-permute-start(f32[32,768]{0,1:T(8,128)S(1)} %copy.187), channel_id=1, source_target_pairs={{0,1},{1,2},{2,3},{3,0},{4,5},{5,6},{6,7},{7,4},{8,9},{9,10},{10,1... | collective-permute-start | bytes 294920 | tf_op jit(solution)/shard_map/ppermute | solution.py:1448
  583.6 33.9 %collective-permute-start.4 = (f32[32,768]{0,1:T(8,128)S(1)}, f32[32,768]{0,1:T(8,128)S(1)}, u32[]{:S(2)}, u32[]{:S(2)}) collective-permute-start(f32[32,768]{0,1:T(8,128)S(1)} %copy.187), channel_id=1, source_target_pairs={{0,2},{1,3},{2,0},{3,1},{4,6},{5,7},{6,4},{7,5},{8,10},{9,11},{10,... | collective-permute-start | bytes 294920 | tf_op jit(solution)/shard_map/ppermute | solution.py:1448
  586.0 39.4 %collective-permute-start.5 = (f32[32,768]{0,1:T(8,128)S(1)}, f32[32,768]{0,1:T(8,128)S(1)}, u32[]{:S(2)}, u32[]{:S(2)}) collective-permute-start(f32[32,768]{0,1:T(8,128)S(1)} %copy.187), channel_id=1, source_target_pairs={{0,3},{1,0},{2,1},{3,2},{4,7},{5,4},{6,5},{7,6},{8,11},{9,8},{10,9... | collective-permute-start | bytes 294920 | tf_op jit(solution)/shard_map/ppermute | solution.py:1448
  612.0 13.8 %copy-start.2 = (bf16[768,2048]{1,0:T(8,128)(2,1)S(1)}, bf16[768,2048]{1,0:T(8,128)(2,1)}, u32[]{:S(2)}) copy-start(bf16[768,2048]{1,0:T(8,128)(2,1)} %get-tuple-element.71) | copy-start | bytes 9437188
  626.5 22.6 %collective-permute-start.8 = (bf16[192,2048]{1,0:T(8,128)(2,1)S(1)}, bf16[192,2048]{1,0:T(8,128)(2,1)S(1)}, u32[]{:S(2)}, u32[]{:S(2)}) collective-permute-start(bf16[192,2048]{1,0:T(8,128)(2,1)S(1)} %get-tuple-element.117), channel_id=1, source_target_pairs={{0,1},{1,2},{4,5},{5,6},{8,9},{9,10},{12,13},{13,14},{16,17},{17,1... | collective-permute-start | bytes 2359304 | tf_op jit(solution)/shard_map/ppermute | solution.py:1464
  627.8 21.2 %collective-permute-start.9 = (bf16[192,2048]{1,0:T(8,128)(2,1)S(1)}, bf16[192,2048]{1,0:T(8,128)(2,1)S(1)}, u32[]{:S(2)}, u32[]{:S(2)}) collective-permute-start(bf16[192,2048]{1,0:T(8,128)(2,1)S(1)} %get-tuple-element.116), channel_id=1, source_target_pairs={{2,1},{3,2},{6,5},{7,6},{10,9},{11,10},{14,13},{15,14},{18,17},{19... | collective-permute-start | bytes 2359304 | tf_op jit(solution)/shard_map/ppermute | solution.py:1467
  650.9 28.6 %collective-permute-start.10 = (bf16[192,2048]{1,0:T(8,128)(2,1)}, bf16[192,2048]{1,0:T(8,128)(2,1)S(1)}, u32[]{:S(2)}, u32[]{:S(2)}) collective-permute-start(bf16[192,2048]{1,0:T(8,128)(2,1)} %get-tuple-element.115), channel_id=1, source_target_pairs={{0,1},{1,2},{2,3},{4,5},{5,6},{6,7},{8,9},{9,10},{10,11},{12,13},{... | collective-permute-start | bytes 2359304 | tf_op jit(solution)/shard_map/ppermute | solution.py:1464
  658.2 21.3 %collective-permute-start.11 = (bf16[192,2048]{1,0:T(8,128)(2,1)}, bf16[192,2048]{1,0:T(8,128)(2,1)}, u32[]{:S(2)}, u32[]{:S(2)}) collective-permute-start(bf16[192,2048]{1,0:T(8,128)(2,1)} %get-tuple-element.114), channel_id=1, source_target_pairs={{1,0},{2,1},{3,2},{5,4},{6,5},{7,6},{9,8},{10,9},{11,10},{13,12},{... | collective-permute-start | bytes 2359304 | tf_op jit(solution)/shard_map/ppermute | solution.py:1467
  659.5 20.0 %copy-start.1 = (f32[192,2048]{1,0:T(8,128)S(1)}, f32[192,2048]{1,0:T(8,128)}, u32[]{:S(2)}) copy-start(f32[192,2048]{1,0:T(8,128)} %copy-done) | copy-start | bytes 4718596
  659.5 20.0 %copy-start.11 = (f32[2048]{0:T(1024)S(1)}, f32[2048]{0:T(1024)}, u32[]{:S(2)}) copy-start(f32[2048]{0:T(1024)} %copy-done.10) | copy-start | bytes 24580
  679.5 3.2 copy-start.16
  768.2 4.2 copy-start.25
  768.2 148.7 %reduce-scatter.11.cloned.1.call-start = ((), (), s32[]{:S(2)}) async-start(), calls=%async_computation.12 | async-start | bytes 2949120 | tf_op jit(solution)/shard_map/reduce_scatter | solution.py:1872
  768.5 3.9 copy-start.3
  774.3 2.0 copy-start.7
  776.2 163.7 %reduce-scatter.9.cloned.1.call-start = ((), (), s32[]{:S(2)}) async-start(), calls=%async_computation.11 | async-start | bytes 7077888 | tf_op jit(solution)/shard_map/reduce_scatter | solution.py:1882
  845.0 0.7 copy-start.20
  845.0 0.7 copy-start.17
  845.1 1.0 copy-start.9
  909.5 5.9 copy-start.8
  909.5 6.2 copy-start.14
  909.5 7.4 copy-start.18
  910.4 9.7 %copy-start.5 = (bf16[768,512]{1,0:T(8,128)(2,1)S(1)}, bf16[768,512]{1,0:T(8,128)(2,1)}, u32[]{:S(2)}) copy-start(bf16[768,512]{1,0:T(8,128)(2,1)} %in_ref.1) | copy-start | bytes 2359300
  910.4 22.8 %all-to-all-start.1 = ((bf16[192,4,512]{2,0,1:T(8,128)(2,1)}), bf16[192,4,512]{2,0,1:T(8,128)(2,1)S(1)}, u32[]{:S(2)}, u32[]{:S(2)}) async-start(bf16[192,4,512]{2,0,1:T(8,128)(2,1)} %bitcast.82), calls=%async_computation.3 | async-start | bytes 1572864 | tf_op jit(solution)/shard_map/all_to_all | solution.py:1861
  915.7 4.4 copy-start.6
Sparse Core Ops, SparseCore 0:
  13.9 59.2 all-gather.3
  74.8 63.4 all-gather.5
  154.3 132.3 all-gather.7
  572.2 155.3 reduce-scatter.4
  768.3 59.0 reduce-scatter.6
  830.6 43.8 reduce-scatter.10
  877.9 62.0 reduce-scatter.8

commit v3 on v2

--- a/solution.py
+++ b/solution.py
@@ -1468,7 +1468,7 @@
             to_left, "tp", [(at, at - 1) for at in range(1, size) if size - 1 - at <= step]
         )
         if step < len(beside_steps):
-            made.append(beside_steps[step]())
+            made.append(beside_steps[step](made))
             right, left = then(made[-1], right, left)
     total = block(place).astype(f32) + right.astype(f32) + left.astype(f32)
     return total, made
@@ -1486,7 +1486,6 @@
     cosine_ref,
     sine_ref,
     head_gain_ref,
-    segment_ref,
     normed_ref,
     inverse_ref,
     pre_ref,
@@ -1512,10 +1511,6 @@
             to_ref = query_ref if which == 0 else group_ref
             to_ref[:, at] = turned.astype(bf16)
     group_ref[:, width : 2 * width] = qkv[:, 2 * width :].astype(bf16)
-    rest = group_ref.shape[1] - 2 * width
-    group_ref[:, 2 * width :] = jnp.broadcast_to(
-        segment_ref[...], (segment_ref.shape[0], rest)
-    ).astype(bf16)
 
 
 def project_back(
@@ -1563,7 +1558,7 @@
     along_ref[...] = jnp.sum(product * gain_ref[...], axis=1, keepdims=True)
 
 
-def run_project(input_b, gain, full, cosine, sine, head_gains, segment, width):
+def run_project(input_b, gain, full, cosine, sine, head_gains, width):
     rows, depth = input_b.shape
     head_dim = cosine.shape[1]
     block = min(rows, QUERY_BLOCK)
@@ -1578,28 +1573,27 @@
             by_rows(head_dim),
             by_rows(head_dim),
             once((2, head_dim)),
-            by_rows(1),
         ],
         out_specs=[
             by_rows(depth),
             by_rows(1),
             by_rows(2 * width),
             by_rows(width),
-            by_rows(2 * width + EXTRA),
+            by_rows(2 * width),
         ],
         out_shape=[
             jax.ShapeDtypeStruct((rows, depth), bf16),
             jax.ShapeDtypeStruct((rows, 1), f32),
             jax.ShapeDtypeStruct((rows, 2 * width), f32),
             jax.ShapeDtypeStruct((rows, width), bf16),
-            jax.ShapeDtypeStruct((rows, 2 * width + EXTRA), bf16),
+            jax.ShapeDtypeStruct((rows, 2 * width), bf16),
         ],
         compiler_params=params(1),
         cost_estimate=pl.CostEstimate(
             flops=6 * rows * depth * width, bytes_accessed=6 * depth * width, transcendentals=0
         ),
         name="project",
-    )(input_b, gain, full, cosine, sine, head_gains, segment)
+    )(input_b, gain, full, cosine, sine, head_gains)
 
 
 def run_project_back(
@@ -1712,7 +1706,19 @@
     first_slot = (lax.rem(fc_index, CHUNK // tok_count) * capacity).astype(f32)
     ranks = jnp.where(named, before + first_slot, -1.0).astype(bf16)
     input_b = gather_tp(layer_input, True, 0)
-    out_grad, full, input_b = lax.optimization_barrier((out_grad, full, input_b))
+    segment, position = doc_places(token_order[0], doc_lengths[0])
+    ctx_index = lax.axis_index("ctx")
+    seg_columns = jnp.zeros((ctx_size, tok_count), f32)
+    for offset in range(ctx_size):
+        piece = segment.astype(f32)[None, :]
+        if offset > 0:
+            pairs = [(at, (at + offset) % ctx_size) for at in range(ctx_size)]
+            piece = lax.ppermute(piece, "ctx", pairs)
+        origin = lax.rem(ctx_index + ctx_size - offset, ctx_size)
+        seg_columns = lax.dynamic_update_slice_in_dim(seg_columns, piece, origin, 0)
+    out_grad, full, input_b, seg_columns = lax.optimization_barrier(
+        (out_grad, full, input_b, seg_columns)
+    )
     grad_rows_b = lax.all_gather(out_grad, "tp", axis=1, tiled=True)
     side = 3 * head_width
     qkv_weight = full[:, :side]
@@ -1722,7 +1728,6 @@
     attn_gain_f = full[:, side + experts].astype(f32)
     moe_gain_f = full[:, side + experts + 1].astype(f32)
     width = input_b.shape[1]
-    segment, position = doc_places(token_order[0], doc_lengths[0])
     cosine, sine = rope_tables(position, head_dim)
     head_gains = jnp.stack([query_gain, key_gain])
     attn_gain_row = attn_gain_f[None, :]
@@ -1733,7 +1738,6 @@
         cosine,
         sine,
         head_gains,
-        segment.astype(f32)[:, None],
         head_width,
     )
     group = gather_ctx(group_part, 1)
@@ -1757,7 +1761,7 @@
     rank_rows = jnp.transpose(rank_columns, (0, 2, 1))[:, :, None, :]
 
     seg_rows = segment.astype(f32).reshape(-1, 1, min(tok_count, QUERY_BLOCK))
-    seg_columns = group[:, 2 * head_width : 2 * head_width + 1].astype(f32)
+    seg_columns = seg_columns.reshape(-1, 1)
     attn_b, log_total = run_attend(query_rows, group, seg_rows, seg_columns, heads, scale)
     attn_part = matmul_nt(attn_b, full_out).astype(bf16)
     attn_out = scatter_tp(attn_part, False, 2)
@@ -1796,12 +1800,12 @@
         jnp.transpose(route_all, (1, 0, 2)), ROWS, split_axis=0, concat_axis=0, tiled=True
     ).reshape(experts, tok_count)
 
-    back_rows, ((grad_gate, gate_grad), grad_up, grad_down) = scatter_line(
+    back_rows, ((grad_gate, route_all), (grad_up, gate_grad), grad_down) = scatter_line(
         back_sum,
         (
-            lambda: (weight_grad(token_slots, gate_act_grad), rotated_sum(route_all)),
-            lambda: weight_grad(token_slots, up_act_grad),
-            lambda: weight_grad(hidden_rows, grad_slots),
+            lambda made: (weight_grad(token_slots, gate_act_grad), route_all),
+            lambda made: (weight_grad(token_slots, up_act_grad), rotated_sum(made[0][1])),
+            lambda made: weight_grad(hidden_rows, grad_slots),
         ),
     )
     parts = own_tokens[:, width : width + 3 * experts].astype(f32)

time: 952 us -> 953 us (level)
  starting transfers between devices: 26.5 us -> 38.7 us
    ppermute x3, waiting for transfers between devices: 13.4 us -> 0.01 us  [rotated_sum(): total = total + lax.ppermute(values, 'tp', pairs)]
    ppermute x3, waiting for transfers between devices: 0.01 us -> 12 us  [scatter_line(): lax.ppermute(to_right, 'tp', [(at, at + 1) for at in range(size - 1) if a...]
  transfers between devices with their start and end apart: 21 -> 22, of which waited for: 9 -> 6; matrix products, arithmetic and copies ran while one was open for 15% -> 15% of each run, Pallas kernels for 53% -> 52%
where the time goes in v3:
time: 953 us; the launch traced here: 951 us
  Pallas kernels  697 us (73%)
  matrix products  96.2 us (10%)
  waiting for transfers between devices  39.3 us (4%)
  starting transfers between devices  38.7 us (4%)
  local copies, waits for them, and re-layouts  32.9 us (3%)
  other arithmetic  31.7 us (3%)
  between operations  15.3 us (2%)
    pallas_call x1, Pallas kernels, run_exchange_pass(): pl.pallas_call(exchange_pass, grid=(2 * chunks, local), in_specs=[pl.Bloc...  201 us
    pallas_call x3, Pallas kernels, gather_tp(): pl.pallas_call(functools.partial(line_gather, size, columns), in_specs=[p...  164 us
    dot_general x3, matrix products, weight_grad(): return jnp.einsum('gesa,gesb->eab', left, right, preferred_element_type=f32)  65 us
    pallas_call x1, Pallas kernels, close_tp(): pl.pallas_call(functools.partial(closing_sums, sizes, narrow), in_specs=[...  61.6 us
    pallas_call x1, Pallas kernels, scatter_tp(): pl.pallas_call(functools.partial(line_scatter, size, columns), in_specs=[...  59 us
    pallas_call x1, Pallas kernels, run_select_grads(): pl.pallas_call(select_grads, grid_spec=pltpu.PrefetchScalarGridSpec(num_s...  56.3 us
    pallas_call x1, Pallas kernels, gather_ctx(): pl.pallas_call(functools.partial(peer_gather, size), in_specs=[pl.BlockSp...  49.7 us
    pallas_call x1, Pallas kernels, scatter_ctx(): pl.pallas_call(functools.partial(peer_scatter, size), in_specs=[pl.BlockS...  37.5 us
  transfers between devices with their start and end apart: 22, of which 6 were waited for; matrix products, arithmetic and copies ran while one was open for 15% of the time, Pallas kernels for 52%

profile of v3, /device:TPU:0, one launch (start us, length us, event | category | flops | bytes accessed | tf_op | source)
XLA Modules:
  0.0 951.0 jit_solution(5512936934002660662)
XLA Ops:
  7.2 1.1 copy.158
  10.7 3.0 concatenate.28
  14.2 3.0 collective-permute-start
  17.2 55.7 %gather_tp.3.input_ref = bf16[768,2048]{1,0:T(8,128)(2,1)} custom-call(bf16[768,512]{1,0:T(8,128)(2,1)} %in_ref.1), custom_call_target="tpu_custom_call" | custom-call | bytes 150000000 | tf_op jit(solution)/shard_map/gather_tp/pallas_call | solution.py:1117
  74.2 1.4 fusion.24
  75.7 1.2 pad_maximum_fusion.1
  77.4 2.7 convert_reduce_fusion
  80.2 11.3 %project.1 = (bf16[768,2048]{1,0:T(8,128)(2,1)}, f32[768,1]{1,0:T(8,128)}, f32[768,1024]{1,0:T(8,128)}, bf16[768,512]{1,0:T(8,128)(2,1)}, bf16[768,1024]{1,0:T(8,128)(2,1)}) custom-call(bf16[768,2048]{1,0:T(8,128)(2,1)} %gather_tp.3.input_ref, f32[1,2048]{1,0:T(1,128)} %bitcast.96, bf16[2048,2176]{1,0:T(8,128)(2,1)} %all-gather.4.cloned.1.call-done.weight_ref, ...), custom_call_target="tpu_custom_call" | custom-call | flops 4831838208 | bytes 6291456 | tf_op jit(solution)/shard_map/project/pallas_call | solution.py:1566
  91.5 49.7 %gather_ctx.1.key_ref.value_ref = bf16[1536,1024]{1,0:T(8,128)(2,1)} custom-call(bf16[768,1024]{1,0:T(8,128)(2,1)} %get-tuple-element.64.in_ref), custom_call_target="tpu_custom_call" | custom-call | bytes 100000000 | tf_op jit(solution)/shard_map/gather_ctx/pallas_call | solution.py:1192
  141.3 6.0 concatenate.31
  148.6 1.2 copy.212
  149.8 16.0 %attend.1 = (bf16[768,512]{1,0:T(8,128)(2,1)}, f32[4,3,1,256]{3,2,1,0:T(1,128)}) custom-call(bf16[768,512]{1,0:T(8,128)(2,1)} %get-tuple-element.62.query_ref, bf16[1536,1024]{1,0:T(8,128)(2,1)} %gather_ctx.1.key_ref.value_ref, bf16[1536,1024]{1,0:T(8,128)(2,1)} %gather_ctx.1.key_ref.value_ref, f32[3,1,256]{2,1,0:T(1,128)} %convert_element_type.186.seg_row_ref, ...), custom_call_target="tpu_custom_call" | custom-call | flops 2415919104 | bytes 3145728 | tf_op jit(solution)/shard_map/attend/pallas_call | solution.py:1306
  165.8 5.3 convolution_convert_fusion.1.in_ref
  171.2 59.0 %scatter_tp.1 = f32[192,2048]{1,0:T(8,128)} custom-call(bf16[768,2048]{1,0:T(8,128)(2,1)} %convolution_convert_fusion.1.in_ref), custom_call_target="tpu_custom_call" | custom-call | bytes 150000000 | tf_op jit(solution)/shard_map/scatter_tp/pallas_call | solution.py:1137
  230.2 1.9 multiply_reduce_fusion.2
  232.1 1.1 copy-done
  233.4 1.5 fusion.36
  235.3 1.1 concatenate.32.in_ref
  236.4 54.7 %gather_tp.4.own_ref = bf16[768,2176]{1,0:T(8,128)(2,1)} custom-call(bf16[192,2176]{1,0:T(8,128)(2,1)} %concatenate.32.in_ref), custom_call_target="tpu_custom_call" | custom-call | bytes 150000000 | tf_op jit(solution)/shard_map/gather_tp/pallas_call | solution.py:1117
  291.8 1.6 collective-permute-start.3
  293.4 1.4 slice-done
  295.8 1.8 copy.185.rank_ref
  297.6 56.3 %select_grads.1 = (bf16[8,4,256,2048]{3,2,1,0:T(8,128)(2,1)}, f32[8,4,256,256]{3,2,1,0:T(8,128)}) custom-call(s32[8]{0:T(128)} %stack.83.ids_ref, s32[8,4,1,768]{3,2,1,0:T(1,128)} %copy.185.rank_ref, bf16[6144,2176]{1,0:T(8,128)(2,1)} %all-gather.8.cloned.1.call-done.grad_ref, bf16[4,256,2048]{2,1,0:T(8,128)(2,1)} %down_ref.1), custom_call_target="tpu_custom_call" | custom-call | flops 34359738368 | bytes 58720256 | tf_op jit(solution)/shard_map/select_grads/pallas_call | solution.py:580
  353.9 8.9 collective-permute-done.2.from_across_ref
  363.3 201.0 %exchange_pass.1 = (bf16[8,4,256,2048]{3,2,1,0:T(8,128)(2,1)}, bf16[8,4,256,256]{3,2,1,0:T(8,128)(2,1)}, bf16[8,4,256,256]{3,2,1,0:T(8,128)(2,1)}, bf16[8,4,256,...) custom-call(s32[8,4,1,768]{3,2,1,0:T(1,128)} %copy.185.rank_ref, ...), custom_call_target="tpu_custom_call" | custom-call | flops 85899345920 | bytes 71303168 | tf_op jit(solution)/shard_map/exchange_pass/pallas_call | solution.py:623
  565.0 1.0 slice_convert_fusion.1
  565.9 2.4 constant_dynamic-slice_fusion
  568.3 1.5 collective-permute-start.7
  570.6 0.9 select_reduce_fusion
  571.5 3.4 all-to-all-start
  574.9 26.0 %convolution_bitcast_fusion = f32[4,2048,256]{2,1,0:T(8,128)} fusion(bf16[8,4,256,2048]{3,2,1,0:T(8,128)(2,1)} %get-tuple-element.76, bf16[8,4,256,256]{3,2,1,0:T(8,128)(2,1)} %get-tuple-element.79), kind=kOutput, calls=%fused_computation.1 | convolution fusion | flops 8589934592 | bytes 46137344 | tf_op jit(solution)/shard_map/gesa,gesb->eab/dot_general | solution.py:1371
  601.7 2.5 collective-permute-start.5
  605.0 2.4 add_convert_fusion.4
  608.2 3.7 collective-permute-start.9
  611.9 20.0 %convolution_bitcast_fusion.1 = f32[4,2048,256]{2,1,0:T(8,128)} fusion(bf16[8,4,256,2048]{3,2,1,0:T(8,128)(2,1)} %get-tuple-element.76, bf16[8,4,256,256]{3,2,1,0:T(8,128)(2,1)S(1)} %copy-done.26), kind=kOutput, calls=%fused_computation.2 | convolution fusion | flops 8589934592 | bytes 46137344 | tf_op jit(solution)/shard_map/gesa,gesb->eab/dot_general | solution.py:1371
  632.3 12.0 %collective-permute-done.9 = bf16[192,2048]{1,0:T(8,128)(2,1)S(1)} collective-permute-done((bf16[192,2048]{1,0:T(8,128)(2,1)S(1)}, bf16[192,2048]{1,0:T(8,128)(2,1)S(1)}, u32[]{:S(2)}, u32[]{:S(2)}) %collective-permute-start.9) | collective-permute-done | bytes 786464 | tf_op jit(solution)/shard_map/ppermute | solution.py:1464
  644.4 1.8 add_convert_fusion.2
  646.1 14.1 %collective-permute-start.11 = (bf16[192,2048]{1,0:T(8,128)(2,1)}, bf16[192,2048]{1,0:T(8,128)(2,1)S(1)}, u32[]{:S(2)}, u32[]{:S(2)}) collective-permute-start(bf16[192,2048]{1,0:T(8,128)(2,1)} %get-tuple-element.117), channel_id=1, source_target_pairs={{0,1},{1,2},{2,3},{4,5},{5,6},{6,7},{8,9},{9,10},{10,11},{12,13},{... | collective-permute-start | bytes 2359304 | tf_op jit(solution)/shard_map/ppermute | solution.py:1464
  660.2 1.3 collective-permute-start.12
  661.5 19.0 %convolution_bitcast_fusion.2 = f32[4,256,2048]{2,1,0:T(8,128)} fusion(bf16[8,4,256,256]{3,2,1,0:T(8,128)(2,1)} %get-tuple-element.74, bf16[8,4,256,2048]{3,2,1,0:T(8,128)(2,1)} %get-tuple-element.75), kind=kOutput, calls=%fused_computation.3 | convolution fusion | flops 8589934592 | bytes 46137344 | tf_op jit(solution)/shard_map/gesa,gesb->eab/dot_general | solution.py:1371
  681.0 3.5 multiply_reduce_fusion
  684.6 2.6 add_convert_fusion.1.in_ref
  687.1 53.6 %gather_tp.5 = bf16[768,2048]{1,0:T(8,128)(2,1)} custom-call(bf16[192,2048]{1,0:T(8,128)(2,1)} %add_convert_fusion.1.in_ref), custom_call_target="tpu_custom_call" | custom-call | bytes 150000000 | tf_op jit(solution)/shard_map/gather_tp/pallas_call | solution.py:1117
  740.8 5.2 fusion.9.grad_ref
  746.0 22.0 %attend_back.1 = (f32[768,512]{1,0:T(8,128)}, bf16[1536,512]{1,0:T(8,128)(2,1)}, bf16[1536,512]{1,0:T(8,128)(2,1)}) custom-call(bf16[768,512]{1,0:T(8,128)(2,1)} %get-tuple-element.62.query_ref, bf16[1536,1024]{1,0:T(8,128)(2,1)} %gather_ctx.1.key_ref.value_ref, bf16[1536,1024]{1,0:T(8,128)(2,1)} %gather_ctx.1.key_ref.value_ref, ...), custom_call_target="tpu_custom_call" | custom-call | flops 6039797760 | bytes 6291456 | tf_op jit(solution)/shard_map/attend_back/pallas_call | solution.py:1328
  768.4 3.8 fusion.3
  772.2 1.9 convolution_convert_fusion.2
  774.1 1.9 maximum_maximum_fusion
  776.1 3.4 pad_maximum_fusion.in_ref
  779.6 37.5 %scatter_ctx.1.group_grad_ref = bf16[768,1024]{1,0:T(8,128)(2,1)} custom-call(bf16[1536,1024]{1,0:T(8,128)(2,1)} %pad_maximum_fusion.in_ref), custom_call_target="tpu_custom_call" | custom-call | bytes 100000000 | tf_op jit(solution)/shard_map/scatter_ctx/pallas_call | solution.py:1212
  817.0 18.5 %project_back.1 = (bf16[768,1536]{1,0:T(8,128)(2,1)}, bf16[768,2048]{1,0:T(8,128)(2,1)}, f32[768,1]{1,0:T(8,128)}, f32[1,2048]{1,0:T(1,128)}, f32[2,128]{1,0:T(2,128)}) custom-call(f32[768,512]{1,0:T(8,128)} %get-tuple-element.86.query_grad_ref, bf16[768,1024]{1,0:T(8,128)(2,1)} %scatter_ctx.1.group_grad_ref, f32[768,1024]{1,0:T(8,128)} %get-tuple-element.91.pre_ref, ...), custom_call_target="tpu_custom_call" | custom-call | flops 4831838208 | bytes 8388608 | tf_op jit(solution)/shard_map/project_back/pallas_call | solution.py:1608
  835.6 9.4 convolution_convert_fusion
  846.8 61.6 %close_tp.1 = (f32[768,512]{1,0:T(8,128)}, f32[8,640]{1,0:T(8,128)}, f32[8,128]{1,0:T(8,128)}) custom-call(bf16[768,2048]{1,0:T(8,128)(2,1)} %get-tuple-element.93.in_ref, f32[8,768]{1,0:T(8,128)} %pad_maximum_fusion.3.small_ref), custom_call_target="tpu_custom_call" | custom-call | bytes 150000000 | tf_op jit(solution)/shard_map/close_tp/pallas_call | solution.py:1163
  908.4 1.3 convert_element_type.217
  910.0 0.9 copy.215
  910.9 3.6 all-to-all-start.1
  914.6 1.3 slice_convert_fusion
  917.4 1.0 convert_element_type.224
  918.4 1.3 slice.98
  920.6 2.8 multiply_add_fusion
  923.4 10.2 %all-to-all-done.1 = bf16[192,4,512]{2,0,1:T(8,128)(2,1)S(1)} async-done(((bf16[192,4,512]{2,0,1:T(8,128)(2,1)}), bf16[192,4,512]{2,0,1:T(8,128)(2,1)S(1)}, u32[]{:S(2)}, u32[]{:S(2)}) %all-to-all-start.1) | async-done | bytes 786464 | tf_op jit(solution)/shard_map/all_to_all | solution.py:1865
  933.6 7.2 reduce-scatter.9.cloned.1.call-done
  940.8 2.3 fusion.33
  943.1 0.9 copy.229
  (152 shorter events, 17.9 us)
Async XLA Ops:
  7.2 6.7 copy-start.19
  7.2 6.7 copy-start.24
  7.2 66.1 %all-gather.4.cloned.1.call-start = ((), (), s32[]{:S(2)}) async-start(), calls=%async_computation.6 | async-start | bytes 10027008 | tf_op jit(solution)/shard_map/all_gather | solution.py:1701
  13.8 59.6 %copy-start.13 = (s32[768,8]{0,1:T(8,128)S(1)}, s32[768,8]{0,1:T(8,128)}, u32[]{:S(2)}) copy-start(s32[768,8]{0,1:T(8,128)} %param.20) | copy-start | bytes 73732
  13.8 59.9 %copy-start.22 = (f32[128]{0:T(128)S(1)}, f32[128]{0:T(128)}, u32[]{:S(2)}) copy-start(f32[128]{0:T(128)} %param.26) | copy-start | bytes 1540
  13.8 59.9 %copy-start.23 = (f32[128]{0:T(128)S(1)}, f32[128]{0:T(128)}, u32[]{:S(2)}) copy-start(f32[128]{0:T(128)} %param.25) | copy-start | bytes 1540
  13.8 127.4 %all-gather.6.cloned.1.call-start = ((), (), s32[]{:S(2)}) async-start(), calls=%async_computation.7 | async-start | bytes 3932160 | tf_op jit(solution)/shard_map/all_gather | solution.py:1722
  14.2 58.8 %collective-permute-start = (f32[1,768]{1,0:T(1,128)S(1)}, f32[1,768]{1,0:T(1,128)S(1)}, u32[]{:S(2)}, u32[]{:S(2)}) collective-permute-start(f32[1,768]{1,0:T(1,128)S(1)} %convert_element_type.181), channel_id=1, source_target_pairs={{0,4},{4,0},{1,5},{5,1},{2,6},{6,2},{3,7},{7,3},{8,12},{12,8},{9,1... | collective-permute-start | bytes 9224 | tf_op jit(solution)/shard_map/ppermute | solution.py:1716
  73.3 220.1 %all-gather.8.cloned.1.call-start = ((), (), s32[]{:S(2)}) async-start(), calls=%async_computation.8 | async-start | bytes 30081024 | tf_op jit(solution)/shard_map/all_gather | solution.py:1748
  80.2 151.9 %copy-start.10 = (f32[2048]{0:T(1024)}, f32[2048]{0:T(1024)S(1)}, u32[]{:S(2)}) copy-start(f32[2048]{0:T(1024)S(1)} %get-tuple-element.106) | copy-start | bytes 24580
  147.2 620.8 %reduce-scatter.5.cloned.1.call-start = ((), (), s32[]{:S(2)}) async-start(), calls=%async_computation.9 | async-start | bytes 28311552 | tf_op jit(solution)/shard_map/reduce_scatter | solution.py:1835
  232.1 1.1 copy-start
  232.1 3.2 copy-start.15
  291.1 71.7 %collective-permute-start.2 = (bf16[768,2176]{1,0:T(8,128)(2,1)}, bf16[768,2176]{1,0:T(8,128)(2,1)}, u32[]{:S(2)}, u32[]{:S(2)}) collective-permute-start(bf16[768,2176]{1,0:T(8,128)(2,1)} %gather_tp.4.own_ref), channel_id=1, source_target_pairs={{0,16},{8,24},{16,0},{24,8},{1,17},{9,25},{17,1},{25,9},{2,18},{10... | collective-permute-start | bytes 10027016 | tf_op jit(solution)/shard_map/ppermute | solution.py:1352
  291.8 71.5 %collective-permute-start.3 = (bf16[768,2176]{1,0:T(8,128)(2,1)}, bf16[768,2176]{1,0:T(8,128)(2,1)}, u32[]{:S(2)}, u32[]{:S(2)}) collective-permute-start(bf16[768,2176]{1,0:T(8,128)(2,1)} %gather_tp.4.own_ref), channel_id=1, source_target_pairs={{0,4},{4,0},{1,5},{5,1},{2,6},{6,2},{3,7},{7,3},{8,12},{12,8},{9,1... | collective-permute-start | bytes 10027016 | tf_op jit(solution)/shard_map/ppermute | solution.py:1356
  293.4 69.9 %collective-permute-start.1 = (bf16[768,2176]{1,0:T(8,128)(2,1)}, bf16[768,2176]{1,0:T(8,128)(2,1)}, u32[]{:S(2)}, u32[]{:S(2)}) collective-permute-start(bf16[768,2176]{1,0:T(8,128)(2,1)} %gather_tp.4.own_ref), channel_id=1, source_target_pairs={{0,8},{8,0},{16,24},{24,16},{1,9},{9,1},{17,25},{25,17},{2,10},{10... | collective-permute-start | bytes 10027016 | tf_op jit(solution)/shard_map/ppermute | solution.py:1348
  293.4 1.4 slice-start
  295.8 58.1 %copy-start.4 = (s32[8,768,4]{2,1,0:T(8,128)}, s32[8,768,4]{2,1,0:T(8,128)S(1)}, u32[]{:S(2)}) copy-start(s32[8,768,4]{2,1,0:T(8,128)S(1)} %bitcast_dynamic-update-slice_fusion.column_ref) | copy-start | bytes 294916
  564.3 0.6 copy-start.21
  564.3 6.2 copy-start.12
  568.3 36.7 %collective-permute-start.7 = (bf16[192,2048]{1,0:T(8,128)(2,1)}, bf16[192,2048]{1,0:T(8,128)(2,1)S(1)}, u32[]{:S(2)}, u32[]{:S(2)}) collective-permute-start(bf16[192,2048]{1,0:T(8,128)(2,1)} %get-tuple-element.121), channel_id=1, source_target_pairs={{0,1},{4,5},{8,9},{12,13},{16,17},{20,21},{24,25},{28,29}} | collective-permute-start | bytes 2359304 | tf_op jit(solution)/shard_map/ppermute | solution.py:1464
  569.8 35.2 %collective-permute-start.8 = (bf16[192,2048]{1,0:T(8,128)(2,1)S(1)}, bf16[192,2048]{1,0:T(8,128)(2,1)S(1)}, u32[]{:S(2)}, u32[]{:S(2)}) collective-permute-start(bf16[192,2048]{1,0:T(8,128)(2,1)S(1)} %get-tuple-element.120), channel_id=1, source_target_pairs={{3,2},{7,6},{11,10},{15,14},{19,18},{23,22},{27,26},{31,30}} | collective-permute-start | bytes 2359304 | tf_op jit(solution)/shard_map/ppermute | solution.py:1467
  571.5 29.4 %all-to-all-start = ((f32[8,4,768]{2,1,0:T(4,128)}), f32[8,4,768]{2,1,0:T(4,128)S(1)}, u32[]{:S(2)}, u32[]{:S(2)}) async-start(f32[8,4,768]{2,1,0:T(4,128)} %select_reduce_fusion), calls=%async_computation | async-start | bytes 196608 | tf_op jit(solution)/shard_map/all_to_all | solution.py:1799
  574.9 333.5 %reduce-scatter.7.cloned.1.call-start = ((), (), s32[]{:S(2)}) async-start(), calls=%async_computation.10 | async-start | bytes 3932160 | tf_op jit(solution)/shard_map/reduce_scatter | solution.py:1845
  601.1 10.8 %copy-start.26 = (bf16[8,4,256,256]{3,2,1,0:T(8,128)(2,1)S(1)}, bf16[8,4,256,256]{3,2,1,0:T(8,128)(2,1)}, u32[]{:S(2)}) copy-start(bf16[8,4,256,256]{3,2,1,0:T(8,128)(2,1)} %get-tuple-element.77) | copy-start | bytes 12582916
  601.1 30.8 %collective-permute-start.4 = (f32[32,768]{0,1:T(8,128)S(1)}, f32[32,768]{0,1:T(8,128)S(1)}, u32[]{:S(2)}, u32[]{:S(2)}) collective-permute-start(f32[32,768]{0,1:T(8,128)S(1)} %copy.190), channel_id=1, source_target_pairs={{0,1},{1,2},{2,3},{3,0},{4,5},{5,6},{6,7},{7,4},{8,9},{9,10},{10,1... | collective-permute-start | bytes 294920 | tf_op jit(solution)/shard_map/ppermute | solution.py:1448
  601.7 30.2 %collective-permute-start.5 = (f32[32,768]{0,1:T(8,128)S(1)}, f32[32,768]{0,1:T(8,128)S(1)}, u32[]{:S(2)}, u32[]{:S(2)}) collective-permute-start(f32[32,768]{0,1:T(8,128)S(1)} %copy.190), channel_id=1, source_target_pairs={{0,2},{1,3},{2,0},{3,1},{4,6},{5,7},{6,4},{7,5},{8,10},{9,11},{10,... | collective-permute-start | bytes 294920 | tf_op jit(solution)/shard_map/ppermute | solution.py:1448
  604.2 27.7 %collective-permute-start.6 = (f32[32,768]{0,1:T(8,128)S(1)}, f32[32,768]{0,1:T(8,128)S(1)}, u32[]{:S(2)}, u32[]{:S(2)}) collective-permute-start(f32[32,768]{0,1:T(8,128)S(1)} %copy.190), channel_id=1, source_target_pairs={{0,3},{1,0},{2,1},{3,2},{4,7},{5,4},{6,5},{7,6},{8,11},{9,8},{10,9... | collective-permute-start | bytes 294920 | tf_op jit(solution)/shard_map/ppermute | solution.py:1448
  607.4 24.9 %collective-permute-start.10 = (bf16[192,2048]{1,0:T(8,128)(2,1)S(1)}, bf16[192,2048]{1,0:T(8,128)(2,1)S(1)}, u32[]{:S(2)}, u32[]{:S(2)}) collective-permute-start(bf16[192,2048]{1,0:T(8,128)(2,1)S(1)} %get-tuple-element.118), channel_id=1, source_target_pairs={{2,1},{3,2},{6,5},{7,6},{10,9},{11,10},{14,13},{15,14},{18,17},{19... | collective-permute-start | bytes 2359304 | tf_op jit(solution)/shard_map/ppermute | solution.py:1467
  608.2 36.2 %collective-permute-start.9 = (bf16[192,2048]{1,0:T(8,128)(2,1)S(1)}, bf16[192,2048]{1,0:T(8,128)(2,1)S(1)}, u32[]{:S(2)}, u32[]{:S(2)}) collective-permute-start(bf16[192,2048]{1,0:T(8,128)(2,1)S(1)} %get-tuple-element.119), channel_id=1, source_target_pairs={{0,1},{1,2},{4,5},{5,6},{8,9},{9,10},{12,13},{13,14},{16,17},{17,1... | collective-permute-start | bytes 2359304 | tf_op jit(solution)/shard_map/ppermute | solution.py:1464
  631.9 12.5 %copy-start.2 = (bf16[768,2048]{1,0:T(8,128)(2,1)S(1)}, bf16[768,2048]{1,0:T(8,128)(2,1)}, u32[]{:S(2)}) copy-start(bf16[768,2048]{1,0:T(8,128)(2,1)} %get-tuple-element.73) | copy-start | bytes 9437188
  646.1 34.8 %collective-permute-start.11 = (bf16[192,2048]{1,0:T(8,128)(2,1)}, bf16[192,2048]{1,0:T(8,128)(2,1)S(1)}, u32[]{:S(2)}, u32[]{:S(2)}) collective-permute-start(bf16[192,2048]{1,0:T(8,128)(2,1)} %get-tuple-element.117), channel_id=1, source_target_pairs={{0,1},{1,2},{2,3},{4,5},{5,6},{6,7},{8,9},{9,10},{10,11},{12,13},{... | collective-permute-start | bytes 2359304 | tf_op jit(solution)/shard_map/ppermute | solution.py:1464
  660.2 20.8 %collective-permute-start.12 = (bf16[192,2048]{1,0:T(8,128)(2,1)}, bf16[192,2048]{1,0:T(8,128)(2,1)}, u32[]{:S(2)}, u32[]{:S(2)}) collective-permute-start(bf16[192,2048]{1,0:T(8,128)(2,1)} %get-tuple-element.116), channel_id=1, source_target_pairs={{1,0},{2,1},{3,2},{5,4},{6,5},{7,6},{9,8},{10,9},{11,10},{13,12},{... | collective-permute-start | bytes 2359304 | tf_op jit(solution)/shard_map/ppermute | solution.py:1467
  661.5 19.5 %copy-start.1 = (f32[192,2048]{1,0:T(8,128)S(1)}, f32[192,2048]{1,0:T(8,128)}, u32[]{:S(2)}) copy-start(f32[192,2048]{1,0:T(8,128)} %copy-done) | copy-start | bytes 4718596
  661.5 19.5 %copy-start.11 = (f32[2048]{0:T(1024)S(1)}, f32[2048]{0:T(1024)}, u32[]{:S(2)}) copy-start(f32[2048]{0:T(1024)} %copy-done.10) | copy-start | bytes 24580
  680.9 3.6 copy-start.16
  768.0 4.2 copy-start.25
  768.0 149.3 %reduce-scatter.11.cloned.1.call-start = ((), (), s32[]{:S(2)}) async-start(), calls=%async_computation.12 | async-start | bytes 2949120 | tf_op jit(solution)/shard_map/reduce_scatter | solution.py:1876
  768.3 3.9 copy-start.3
  774.1 2.0 copy-start.7
  776.1 164.7 %reduce-scatter.9.cloned.1.call-start = ((), (), s32[]{:S(2)}) async-start(), calls=%async_computation.11 | async-start | bytes 7077888 | tf_op jit(solution)/shard_map/reduce_scatter | solution.py:1886
  845.0 0.7 copy-start.20
  845.0 0.7 copy-start.17
  845.0 1.0 copy-start.9
  909.9 5.9 copy-start.8
  910.0 6.2 copy-start.14
  910.0 7.4 copy-start.18
  910.9 9.7 %copy-start.5 = (bf16[768,512]{1,0:T(8,128)(2,1)S(1)}, bf16[768,512]{1,0:T(8,128)(2,1)}, u32[]{:S(2)}) copy-start(bf16[768,512]{1,0:T(8,128)(2,1)} %in_ref.1) | copy-start | bytes 2359300
  910.9 22.7 %all-to-all-start.1 = ((bf16[192,4,512]{2,0,1:T(8,128)(2,1)}), bf16[192,4,512]{2,0,1:T(8,128)(2,1)S(1)}, u32[]{:S(2)}, u32[]{:S(2)}) async-start(bf16[192,4,512]{2,0,1:T(8,128)(2,1)} %bitcast.86), calls=%async_computation.3 | async-start | bytes 1572864 | tf_op jit(solution)/shard_map/all_to_all | solution.py:1865
  916.2 4.4 copy-start.6
Sparse Core Ops, SparseCore 0:
  13.9 59.2 all-gather.3
  74.8 63.4 all-gather.5
  147.4 132.4 all-gather.7
  564.5 155.1 reduce-scatter.4
  768.2 59.9 reduce-scatter.6
  831.4 44.1 reduce-scatter.10
  879.0 61.7 reduce-scatter.8

commit v4 on v3

--- a/solution.py
+++ b/solution.py
@@ -1367,10 +1367,6 @@
     return lax.optimization_barrier((first, *values))[1:]
 
 
-def weight_grad(left, right):
-    return jnp.einsum("gesa,gesb->eab", left, right, preferred_element_type=f32)
-
-
 def by_chips():
     return lax.axis_size("fsdp") == 4 and lax.axis_size("ctx") == 2
 
@@ -1438,40 +1434,6 @@
         (own_tokens, from_beside, from_across, from_other),
     )
     return kept, grad_slots, back_sum, out_part
-
-
-def rotated_sum(values):
-    size = lax.axis_size("tp")
-    total = values
-    for offset in range(1, size):
-        pairs = [(at, (at + offset) % size) for at in range(size)]
-        total = total + lax.ppermute(values, "tp", pairs)
-    return total
-
-
-def scatter_line(values, beside_steps):
-    size, place = lax.axis_size("tp"), lax.axis_index("tp")
-    rows = values.shape[0] // size
-    block = lambda at: lax.dynamic_slice_in_dim(
-        values, jnp.clip(at, 0, size - 1) * rows, rows, 0
-    )
-    right, left, made = None, None, []
-    for step in range(size - 1):
-        to_right = block(size - 1 - step + place)
-        to_left = block(place - (size - 1 - step))
-        if step > 0:
-            to_right, to_left = added(to_right, right), added(to_left, left)
-        right = lax.ppermute(
-            to_right, "tp", [(at, at + 1) for at in range(size - 1) if at <= step]
-        )
-        left = lax.ppermute(
-            to_left, "tp", [(at, at - 1) for at in range(1, size) if size - 1 - at <= step]
-        )
-        if step < len(beside_steps):
-            made.append(beside_steps[step](made))
-            right, left = then(made[-1], right, left)
-    total = block(place).astype(f32) + right.astype(f32) + left.astype(f32)
-    return total, made
 
 
 def head_blocks(width, head_dim):
@@ -1640,6 +1602,227 @@
         ),
         name="project_back",
     )(query_grad, group_grad, pre, cosine, sine, head_gains, full, input_b, inverse, gain)
+
+
+def grads_scatter(
+    size,
+    local,
+    in_ref,
+    small_ref,
+    rows_ref,
+    grad_rows_ref,
+    gate_grad_ref,
+    up_grad_ref,
+    hidden_ref,
+    out_ref,
+    total_ref,
+    gate_out_ref,
+    up_out_ref,
+    down_out_ref,
+    staged_ref,
+    landed_ref,
+    small_landed_ref,
+    first_ref,
+    second_ref,
+    send_sem,
+    recv_sem,
+    small_send_sem,
+    small_recv_sem,
+):
+    step, part = pl.program_id(0), pl.program_id(1)
+    place = lax.axis_index("tp")
+    extent = out_ref.shape[0]
+
+    def block(index):
+        return in_ref[pl.ds(pl.multiple_of(index * extent, extent), extent), :].astype(f32)
+
+    def copying(way, stage, to):
+        return pltpu.make_async_remote_copy(
+            src_ref=staged_ref.at[way, stage],
+            dst_ref=landed_ref.at[way, stage],
+            send_sem=send_sem.at[way, stage],
+            recv_sem=recv_sem.at[way, stage],
+            device_id={"tp": to},
+            device_id_type=MESH,
+        )
+
+    def small_copy(offset, peer):
+        return pltpu.make_async_remote_copy(
+            src_ref=small_ref,
+            dst_ref=small_landed_ref.at[offset - 1],
+            send_sem=small_send_sem.at[offset - 1],
+            recv_sem=small_recv_sem.at[offset - 1],
+            device_id={"tp": peer},
+            device_id_type=MESH,
+        )
+
+    def ways():
+        yield 0, place, place + 1, place - 1
+        yield 1, size - 1 - place, place - 1, place + 1
+
+    def send(stage):
+        for way, rank, to, origin in ways():
+            target = size - 1 - stage + place if way == 0 else place - (size - 1 - stage)
+
+            @pl.when(jnp.logical_and(rank <= stage, rank < size - 1))
+            def _():
+                values = block(target)
+                if stage == 0:
+                    staged_ref[way, stage] = values.astype(bf16)
+                else:
+
+                    @pl.when(rank == 0)
+                    def _():
+                        staged_ref[way, stage] = values.astype(bf16)
+
+                    @pl.when(rank > 0)
+                    def _():
+                        landed = landed_ref[way, stage - 1].astype(f32)
+                        staged_ref[way, stage] = (values + landed).astype(bf16)
+
+                copying(way, stage, to).start()
+
+    def receive(stage):
+        for way, rank, to, origin in ways():
+
+            @pl.when(jnp.logical_and(rank > 0, rank - 1 <= stage))
+            def _():
+                copying(way, stage, origin).wait_recv()
+
+    @pl.when(jnp.logical_and(step == 0, part == 0))
+    def _():
+        peer_barrier("tp", size)
+        for offset in range(1, size):
+            small_copy(offset, lax.rem(place + offset, size)).start()
+        send(0)
+
+    for stage in range(1, size - 1):
+
+        @pl.when(jnp.logical_and(step == min(2 * stage, 2 * local - 1), part == 0))
+        def _():
+            receive(stage - 1)
+            send(stage)
+
+    def flat(ref):
+        return ref[...].reshape(ref.shape[0] * ref.shape[1], ref.shape[2])
+
+    def collect(sum_ref, values):
+        @pl.when(part == 0)
+        def _():
+            sum_ref[...] = values
+
+        @pl.when(part == 1)
+        def _():
+            sum_ref[...] += values
+
+    @pl.when(step < local)
+    def _():
+        rows = flat(rows_ref)
+        collect(first_ref, matmul(flat(gate_grad_ref).T, rows))
+        collect(second_ref, matmul(flat(up_grad_ref).T, rows))
+
+        @pl.when(part == 1)
+        def _():
+            gate_out_ref[...] = first_ref[...].T
+            up_out_ref[...] = second_ref[...].T
+
+    @pl.when(step >= local)
+    def _():
+        collect(down_out_ref, matmul(flat(hidden_ref).T, flat(grad_rows_ref)))
+
+    @pl.when(jnp.logical_and(step == 2 * local - 1, part == 1))
+    def _():
+        total = small_ref[...]
+        for offset in range(1, size):
+            small_copy(offset, lax.rem(place + size - offset, size)).wait_recv()
+            total = total + small_landed_ref[offset - 1]
+        total_ref[...] = total
+        receive(size - 2)
+        out_ref[...] = block(place)
+        for way, rank, to, origin in ways():
+
+            @pl.when(rank > 0)
+            def _():
+                out_ref[...] += landed_ref[way, size - 2].astype(f32)
+
+        for offset in range(1, size):
+            small_copy(offset, lax.rem(place + offset, size)).wait_send()
+        for stage in range(size - 1):
+            for way, rank, to, origin in ways():
+
+                @pl.when(jnp.logical_and(rank <= stage, rank < size - 1))
+                def _():
+                    copying(way, stage, to).wait_send()
+
+
+def run_grads_scatter(values, small, token_slots, grad_slots, gate_grad, up_grad, hidden_rows):
+    size = lax.axis_size("tp")
+    rows, width = values.shape
+    shape = (rows // size, width)
+    chunks, local, slots, hidden = hidden_rows.shape
+    half = chunks // 2
+    early = lambda i, k: jnp.minimum(i, local - 1)
+    late = lambda i, k: jnp.maximum(i - local, 0)
+    early_part = lambda i, k: jnp.where(i < local, k, 1)
+    late_part = lambda i, k: jnp.where(i < local, 0, k)
+    wide = lambda at, part: pl.BlockSpec(
+        (half, None, slots, width), lambda i, k: (part(i, k), at(i, k), 0, 0)
+    )
+    thin = lambda at, part: pl.BlockSpec(
+        (half, None, slots, hidden), lambda i, k: (part(i, k), at(i, k), 0, 0)
+    )
+    tall = pl.BlockSpec((None, width, hidden), lambda i, k: (early(i, k), 0, 0))
+    fixed = lambda form: pl.BlockSpec(form, lambda i, k: (0,) * len(form))
+    return pl.pallas_call(
+        functools.partial(grads_scatter, size, local),
+        grid=(2 * local, 2),
+        in_specs=[
+            once(values.shape),
+            once(small.shape),
+            wide(early, early_part),
+            wide(late, late_part),
+            thin(early, early_part),
+            thin(early, early_part),
+            thin(late, late_part),
+        ],
+        out_specs=[
+            fixed(shape),
+            fixed(small.shape),
+            tall,
+            tall,
+            pl.BlockSpec((None, hidden, width), lambda i, k: (late(i, k), 0, 0)),
+        ],
+        out_shape=[
+            jax.ShapeDtypeStruct(shape, f32),
+            jax.ShapeDtypeStruct(small.shape, f32),
+            jax.ShapeDtypeStruct((local, width, hidden), f32),
+            jax.ShapeDtypeStruct((local, width, hidden), f32),
+            jax.ShapeDtypeStruct((local, hidden, width), f32),
+        ],
+        scratch_shapes=[
+            pltpu.VMEM((2, size - 1, *shape), bf16),
+            pltpu.VMEM((2, size - 1, *shape), bf16),
+            pltpu.VMEM((size - 1, *small.shape), f32),
+            pltpu.VMEM((hidden, width), f32),
+            pltpu.VMEM((hidden, width), f32),
+            pltpu.SemaphoreType.DMA((2, size - 1)),
+            pltpu.SemaphoreType.DMA((2, size - 1)),
+            pltpu.SemaphoreType.DMA((size - 1,)),
+            pltpu.SemaphoreType.DMA((size - 1,)),
+        ],
+        compiler_params=pltpu.CompilerParams(
+            dimension_semantics=("arbitrary",) * 2,
+            collective_id=10,
+            has_side_effects=True,
+            vmem_limit_bytes=VMEM_BYTES,
+        ),
+        cost_estimate=pl.CostEstimate(
+            flops=6 * chunks * local * slots * width * hidden,
+            bytes_accessed=150_000_000,
+            transcendentals=0,
+        ),
+        name="grads_scatter",
+    )(values, small, token_slots, grad_slots, gate_grad, up_grad, hidden_rows)
 
 
 def split_three(values):
@@ -1800,13 +1983,8 @@
         jnp.transpose(route_all, (1, 0, 2)), ROWS, split_axis=0, concat_axis=0, tiled=True
     ).reshape(experts, tok_count)
 
-    back_rows, ((grad_gate, route_all), (grad_up, gate_grad), grad_down) = scatter_line(
-        back_sum,
-        (
-            lambda made: (weight_grad(token_slots, gate_act_grad), route_all),
-            lambda made: (weight_grad(token_slots, up_act_grad), rotated_sum(made[0][1])),
-            lambda made: weight_grad(hidden_rows, grad_slots),
-        ),
+    back_rows, gate_grad, grad_gate, grad_up, grad_down = run_grads_scatter(
+        back_sum, route_all, token_slots, grad_slots, gate_act_grad, up_act_grad, hidden_rows
     )
     parts = own_tokens[:, width : width + 3 * experts].astype(f32)
     all_gates = parts[:, :experts] + parts[:, experts : 2 * experts] + parts[:, 2 * experts :]

time: 953 us -> 932 us (0.978)
  matrix products: 96.2 us -> 30.5 us
  Pallas kernels: 697 us -> 752 us
  starting transfers between devices: 38.7 us -> 12.9 us
  local copies, waits for them, and re-layouts: 32.9 us -> 48.9 us
    pallas_call x0 -> x1, Pallas kernels: none -> 74.5 us  [run_grads_scatter(): pl.pallas_call(functools.partial(grads_scatter, size, local), grid=(2 * l...]
    dot_general x3 -> x0, matrix products: 65 us -> none  [weight_grad(): return jnp.einsum('gesa,gesb->eab', left, right, preferred_element_type=f32)]
    ppermute x9 -> x0, starting transfers between devices: 25.8 us -> none  [the longest x3 19.2 us: scatter_line(): lax.ppermute(to_right, 'tp', [(at, at + 1) for at in range(size - 1) if a...]
    unnamed x66 -> x76, local copies, waits for them, and re-layouts: 7.03 us -> 23.8 us
    pallas_call x1, Pallas kernels: 201 us -> 185 us  [run_exchange_pass(): pl.pallas_call(exchange_pass, grid=(2 * chunks, local), in_specs=[pl.Bloc...]
    ppermute x9 -> x0, waiting for transfers between devices: 12.1 us -> none  [the longest x3 12 us: scatter_line(): lax.ppermute(to_right, 'tp', [(at, at + 1) for at in range(size - 1) if a...]
  transfers between devices with their start and end apart: 22 -> 13, of which waited for: 6 -> 6; matrix products, arithmetic and copies ran while one was open for 15% -> 8% of each run, Pallas kernels for 52% -> 61%
where the time goes in v4:
time: 932 us; the launch traced here: 923 us
  Pallas kernels  752 us (81%)
  local copies, waits for them, and re-layouts  48.9 us (5%)
  waiting for transfers between devices  35.4 us (4%)
  matrix products  30.5 us (3%)
  other arithmetic  28 us (3%)
  between operations  15.1 us (2%)
  starting transfers between devices  12.9 us (1%)
    pallas_call x1, Pallas kernels, run_exchange_pass(): pl.pallas_call(exchange_pass, grid=(2 * chunks, local), in_specs=[pl.Bloc...  185 us
    pallas_call x3, Pallas kernels, gather_tp(): pl.pallas_call(functools.partial(line_gather, size, columns), in_specs=[p...  162 us
    pallas_call x1, Pallas kernels, run_grads_scatter(): pl.pallas_call(functools.partial(grads_scatter, size, local), grid=(2 * l...  74.5 us
    pallas_call x1, Pallas kernels, close_tp(): pl.pallas_call(functools.partial(closing_sums, sizes, narrow), in_specs=[...  59.7 us
    pallas_call x1, Pallas kernels, scatter_tp(): pl.pallas_call(functools.partial(line_scatter, size, columns), in_specs=[...  59.2 us
    pallas_call x1, Pallas kernels, run_select_grads(): pl.pallas_call(select_grads, grid_spec=pltpu.PrefetchScalarGridSpec(num_s...  56.3 us
    pallas_call x1, Pallas kernels, gather_ctx(): pl.pallas_call(functools.partial(peer_gather, size), in_specs=[pl.BlockSp...  49.7 us
    pallas_call x1, Pallas kernels, scatter_ctx(): pl.pallas_call(functools.partial(peer_scatter, size), in_specs=[pl.BlockS...  36.9 us
  transfers between devices with their start and end apart: 13, of which 6 were waited for; matrix products, arithmetic and copies ran while one was open for 8% of the time, Pallas kernels for 61%

profile of v4, /device:TPU:0, one launch (start us, length us, event | category | flops | bytes accessed | tf_op | source)
XLA Modules:
  0.0 922.8 jit_solution(15325988214147894594)
XLA Ops:
  7.2 1.1 copy.126
  8.3 0.8 copy.127
  9.2 0.8 broadcast_in_dim.88
  9.9 0.8 broadcast_in_dim.89
  10.7 3.0 concatenate.28
  14.2 3.0 collective-permute-start
  17.2 55.7 %gather_tp.3.input_ref = bf16[768,2048]{1,0:T(8,128)(2,1)} custom-call(bf16[768,512]{1,0:T(8,128)(2,1)} %in_ref.1), custom_call_target="tpu_custom_call" | custom-call | bytes 150000000 | tf_op jit(solution)/shard_map/gather_tp/pallas_call | solution.py:1117
  74.3 1.4 fusion.20
  75.7 1.2 pad_maximum_fusion.1
  77.4 2.8 convert_reduce_fusion
  80.3 11.3 %project.1 = (bf16[768,2048]{1,0:T(8,128)(2,1)}, f32[768,1]{1,0:T(8,128)}, f32[768,1024]{1,0:T(8,128)}, bf16[768,512]{1,0:T(8,128)(2,1)}, bf16[768,1024]{1,0:T(8,128)(2,1)}) custom-call(bf16[768,2048]{1,0:T(8,128)(2,1)} %gather_tp.3.input_ref, f32[1,2048]{1,0:T(1,128)} %bitcast.88, bf16[2048,2176]{1,0:T(8,128)(2,1)} %all-gather.4.cloned.1.call-done.weight_ref, ...), custom_call_target="tpu_custom_call" | custom-call | flops 4831838208 | bytes 6291456 | tf_op jit(solution)/shard_map/project/pallas_call | solution.py:1528
  91.6 49.7 %gather_ctx.1.key_ref.value_ref = bf16[1536,1024]{1,0:T(8,128)(2,1)} custom-call(bf16[768,1024]{1,0:T(8,128)(2,1)} %get-tuple-element.63.in_ref), custom_call_target="tpu_custom_call" | custom-call | bytes 100000000 | tf_op jit(solution)/shard_map/gather_ctx/pallas_call | solution.py:1192
  141.4 6.0 concatenate.31
  148.6 1.2 copy.172
  149.9 16.1 %attend.1 = (bf16[768,512]{1,0:T(8,128)(2,1)}, f32[4,3,1,256]{3,2,1,0:T(1,128)}) custom-call(bf16[768,512]{1,0:T(8,128)(2,1)} %get-tuple-element.61.query_ref, bf16[1536,1024]{1,0:T(8,128)(2,1)} %gather_ctx.1.key_ref.value_ref, bf16[1536,1024]{1,0:T(8,128)(2,1)} %gather_ctx.1.key_ref.value_ref, f32[3,1,256]{2,1,0:T(1,128)} %convert_element_type.141.seg_row_ref, ...), custom_call_target="tpu_custom_call" | custom-call | flops 2415919104 | bytes 3145728 | tf_op jit(solution)/shard_map/attend/pallas_call | solution.py:1306
  165.9 5.3 convolution_convert_fusion.1.in_ref
  171.3 59.2 %scatter_tp.1 = f32[192,2048]{1,0:T(8,128)} custom-call(bf16[768,2048]{1,0:T(8,128)(2,1)} %convolution_convert_fusion.1.in_ref), custom_call_target="tpu_custom_call" | custom-call | bytes 150000000 | tf_op jit(solution)/shard_map/scatter_tp/pallas_call | solution.py:1137
  230.5 1.9 multiply_reduce_fusion.2
  232.5 1.1 copy-done
  233.8 1.5 fusion.34
  235.6 1.1 concatenate.32.in_ref
  236.8 54.8 %gather_tp.4.own_ref = bf16[768,2176]{1,0:T(8,128)(2,1)} custom-call(bf16[192,2176]{1,0:T(8,128)(2,1)} %concatenate.32.in_ref), custom_call_target="tpu_custom_call" | custom-call | bytes 150000000 | tf_op jit(solution)/shard_map/gather_tp/pallas_call | solution.py:1117
  292.3 1.6 collective-permute-start.3
  293.9 1.4 slice-done.4
  296.3 1.8 copy.153.rank_ref
  298.1 56.3 %select_grads.1 = (bf16[8,4,256,2048]{3,2,1,0:T(8,128)(2,1)}, f32[8,4,256,256]{3,2,1,0:T(8,128)}) custom-call(s32[8]{0:T(128)} %stack.83.ids_ref, s32[8,4,1,768]{3,2,1,0:T(1,128)} %copy.153.rank_ref, bf16[6144,2176]{1,0:T(8,128)(2,1)} %all-gather.8.cloned.1.call-done.grad_ref, bf16[4,256,2048]{2,1,0:T(8,128)(2,1)} %down_ref.1), custom_call_target="tpu_custom_call" | custom-call | flops 34359738368 | bytes 58720256 | tf_op jit(solution)/shard_map/select_grads/pallas_call | solution.py:580
  354.4 12.3 %collective-permute-done.2.from_across_ref = bf16[768,2176]{1,0:T(8,128)(2,1)} collective-permute-done((bf16[768,2176]{1,0:T(8,128)(2,1)}, bf16[768,2176]{1,0:T(8,128)(2,1)}, u32[]{:S(2)}, u32[]{:S(2)}) %collective-permute-start.2) | collective-permute-done | bytes 3342368 | tf_op jit(solution)/shard_map/ppermute | solution.py:1352
  367.0 185.4 %exchange_pass.1 = (bf16[8,4,256,2048]{3,2,1,0:T(8,128)(2,1)}, bf16[8,4,256,256]{3,2,1,0:T(8,128)(2,1)}, bf16[8,4,256,256]{3,2,1,0:T(8,128)(2,1)}, bf16[8,4,256,...) custom-call(s32[8,4,1,768]{3,2,1,0:T(1,128)} %copy.153.rank_ref, ...), custom_call_target="tpu_custom_call" | custom-call | flops 85899345920 | bytes 71303168 | tf_op jit(solution)/shard_map/exchange_pass/pallas_call | solution.py:623
  553.4 0.9 select_reduce_fusion
  554.3 3.4 all-to-all-start
  557.7 0.9 slice.71
  558.9 3.6 all-to-all-done
  563.1 74.5 %grads_scatter.1 = (f32[192,2048]{1,0:T(8,128)}, f32[32,768]{1,0:T(8,128)}, f32[4,2048,256]{2,1,0:T(8,128)}, f32[4,2048,256]{2,1,0:T(8,128)}, f32[4,256,2048]{2,1,0:T(8,128)}) custom-call(bf16[768,2048]{1,0:T(8,128)(2,1)} %get-tuple-element.72.in_ref, f32[32,768]{1,0:T(8,128)} %reshape.181.small_ref, bf16[8,4,256,2048]{3,2,1,0:T(8,128)(2,1)} %get-tuple-element.74.rows_ref, ...), custom_call_target="tpu_custom_call" | custom-call | flops 25769803776 | bytes 150000000 | tf_op jit(solution)/shard_map/grads_scatter/pallas_call | solution.py:1776
  637.6 1.0 fusion.21
  638.6 0.9 fusion.22
  639.6 3.1 multiply_reduce_fusion
  642.7 2.6 add_convert_fusion.1.in_ref
  645.3 51.8 %gather_tp.5 = bf16[768,2048]{1,0:T(8,128)(2,1)} custom-call(bf16[192,2048]{1,0:T(8,128)(2,1)} %add_convert_fusion.1.in_ref), custom_call_target="tpu_custom_call" | custom-call | bytes 150000000 | tf_op jit(solution)/shard_map/gather_tp/pallas_call | solution.py:1117
  697.1 5.2 fusion.9.grad_ref
  702.4 22.0 %attend_back.1 = (f32[768,512]{1,0:T(8,128)}, bf16[1536,512]{1,0:T(8,128)(2,1)}, bf16[1536,512]{1,0:T(8,128)(2,1)}) custom-call(bf16[768,512]{1,0:T(8,128)(2,1)} %get-tuple-element.61.query_ref, bf16[1536,1024]{1,0:T(8,128)(2,1)} %gather_ctx.1.key_ref.value_ref, bf16[1536,1024]{1,0:T(8,128)(2,1)} %gather_ctx.1.key_ref.value_ref, ...), custom_call_target="tpu_custom_call" | custom-call | flops 6039797760 | bytes 6291456 | tf_op jit(solution)/shard_map/attend_back/pallas_call | solution.py:1328
  724.7 3.7 fusion.3
  728.4 1.9 convolution_convert_fusion.2
  730.4 1.9 maximum_maximum_fusion
  732.4 3.5 pad_maximum_fusion.in_ref
  735.9 36.9 %scatter_ctx.1.group_grad_ref = bf16[768,1024]{1,0:T(8,128)(2,1)} custom-call(bf16[1536,1024]{1,0:T(8,128)(2,1)} %pad_maximum_fusion.in_ref), custom_call_target="tpu_custom_call" | custom-call | bytes 100000000 | tf_op jit(solution)/shard_map/scatter_ctx/pallas_call | solution.py:1212
  772.8 18.6 %project_back.1 = (bf16[768,1536]{1,0:T(8,128)(2,1)}, bf16[768,2048]{1,0:T(8,128)(2,1)}, f32[768,1]{1,0:T(8,128)}, f32[1,2048]{1,0:T(1,128)}, f32[2,128]{1,0:T(2,128)}) custom-call(f32[768,512]{1,0:T(8,128)} %get-tuple-element.81.query_grad_ref, bf16[768,1024]{1,0:T(8,128)(2,1)} %scatter_ctx.1.group_grad_ref, f32[768,1024]{1,0:T(8,128)} %get-tuple-element.86.pre_ref, ...), custom_call_target="tpu_custom_call" | custom-call | flops 4831838208 | bytes 8388608 | tf_op jit(solution)/shard_map/project_back/pallas_call | solution.py:1570
  791.4 9.2 %convolution_convert_fusion = bf16[2048,1536]{1,0:T(8,128)(2,1)} fusion(bf16[768,2048]{1,0:T(8,128)(2,1)} %get-tuple-element.98, bf16[768,1536]{1,0:T(8,128)(2,1)} %get-tuple-element.99), kind=kOutput, calls=%fused_computation | convolution fusion | flops 4834983936 | bytes 11796480 | tf_op jit(solution)/shard_map/dot_general | solution.py:2051
  802.5 59.7 %close_tp.1 = (f32[768,512]{1,0:T(8,128)}, f32[8,640]{1,0:T(8,128)}, f32[8,128]{1,0:T(8,128)}) custom-call(bf16[768,2048]{1,0:T(8,128)(2,1)} %get-tuple-element.88.in_ref, f32[8,768]{1,0:T(8,128)} %pad_maximum_fusion.3.small_ref), custom_call_target="tpu_custom_call" | custom-call | bytes 150000000 | tf_op jit(solution)/shard_map/close_tp/pallas_call | solution.py:1163
  862.2 1.3 convert_element_type.157
  863.8 0.9 copy.175
  864.7 3.6 all-to-all-start.1
  868.3 1.2 slice_convert_fusion
  871.2 1.0 convert_element_type.164
  872.2 1.3 slice.98
  873.5 0.8 slice_bitcast_fusion
  874.3 2.8 multiply_add_fusion
  877.2 9.0 all-to-all-done.1
  886.2 9.8 %reduce-scatter.9.cloned.1.call-done = bf16[256,1536]{1,0:T(8,128)(2,1)} async-done(((bf16[2048,1536]{1,0:T(8,128)(2,1)}), bf16[256,1536]{1,0:T(8,128)(2,1)}) %reduce-scatter.9.cloned.1.call-update) | async-done | bytes 786448 | tf_op jit(solution)/shard_map/reduce_scatter | solution.py:2064
  896.0 2.5 fusion.31
  898.4 0.9 copy.192
  899.3 7.8 copy.193
  907.1 4.3 copy.194
  911.4 1.0 slice-done.1
  912.3 3.4 copy.195
  (141 shorter events, 11.9 us)
Async XLA Ops:
  7.2 6.7 copy-start.19
  7.2 6.7 copy-start.24
  7.2 66.1 %all-gather.4.cloned.1.call-start = ((), (), s32[]{:S(2)}) async-start(), calls=%async_computation.6 | async-start | bytes 10027008 | tf_op jit(solution)/shard_map/all_gather | solution.py:1884
  13.8 59.6 %copy-start.13 = (s32[768,8]{0,1:T(8,128)S(1)}, s32[768,8]{0,1:T(8,128)}, u32[]{:S(2)}) copy-start(s32[768,8]{0,1:T(8,128)} %param.20) | copy-start | bytes 73732
  13.8 59.9 %copy-start.22 = (f32[128]{0:T(128)S(1)}, f32[128]{0:T(128)}, u32[]{:S(2)}) copy-start(f32[128]{0:T(128)} %param.26) | copy-start | bytes 1540
  13.8 59.9 %copy-start.23 = (f32[128]{0:T(128)S(1)}, f32[128]{0:T(128)}, u32[]{:S(2)}) copy-start(f32[128]{0:T(128)} %param.25) | copy-start | bytes 1540
  13.8 127.5 %all-gather.6.cloned.1.call-start = ((), (), s32[]{:S(2)}) async-start(), calls=%async_computation.7 | async-start | bytes 3932160 | tf_op jit(solution)/shard_map/all_gather | solution.py:1905
  14.2 58.8 %collective-permute-start = (f32[1,768]{1,0:T(1,128)S(1)}, f32[1,768]{1,0:T(1,128)S(1)}, u32[]{:S(2)}, u32[]{:S(2)}) collective-permute-start(f32[1,768]{1,0:T(1,128)S(1)} %convert_element_type.136), channel_id=1, source_target_pairs={{0,4},{4,0},{1,5},{5,1},{2,6},{6,2},{3,7},{7,3},{8,12},{12,8},{9,1... | collective-permute-start | bytes 9224 | tf_op jit(solution)/shard_map/ppermute | solution.py:1899
  73.3 220.7 %all-gather.8.cloned.1.call-start = ((), (), s32[]{:S(2)}) async-start(), calls=%async_computation.8 | async-start | bytes 30081024 | tf_op jit(solution)/shard_map/all_gather | solution.py:1931
  80.3 152.2 %copy-start.10 = (f32[2048]{0:T(1024)}, f32[2048]{0:T(1024)S(1)}, u32[]{:S(2)}) copy-start(f32[2048]{0:T(1024)S(1)} %get-tuple-element.104) | copy-start | bytes 24580
  147.4 577.0 %reduce-scatter.5.cloned.1.call-start = ((), (), s32[]{:S(2)}) async-start(), calls=%async_computation.9 | async-start | bytes 28311552 | tf_op jit(solution)/shard_map/reduce_scatter | solution.py:2013
  232.4 1.1 copy-start
  232.4 3.2 copy-start.15
  291.5 75.5 %collective-permute-start.1 = (bf16[768,2176]{1,0:T(8,128)(2,1)}, bf16[768,2176]{1,0:T(8,128)(2,1)}, u32[]{:S(2)}, u32[]{:S(2)}) collective-permute-start(bf16[768,2176]{1,0:T(8,128)(2,1)} %gather_tp.4.own_ref), channel_id=1, source_target_pairs={{0,8},{8,0},{16,24},{24,16},{1,9},{9,1},{17,25},{25,17},{2,10},{10... | collective-permute-start | bytes 10027016 | tf_op jit(solution)/shard_map/ppermute | solution.py:1348
  291.6 75.0 %collective-permute-start.2 = (bf16[768,2176]{1,0:T(8,128)(2,1)}, bf16[768,2176]{1,0:T(8,128)(2,1)}, u32[]{:S(2)}, u32[]{:S(2)}) collective-permute-start(bf16[768,2176]{1,0:T(8,128)(2,1)} %gather_tp.4.own_ref), channel_id=1, source_target_pairs={{0,16},{8,24},{16,0},{24,8},{1,17},{9,25},{17,1},{25,9},{2,18},{10... | collective-permute-start | bytes 10027016 | tf_op jit(solution)/shard_map/ppermute | solution.py:1352
  292.3 74.7 %collective-permute-start.3 = (bf16[768,2176]{1,0:T(8,128)(2,1)}, bf16[768,2176]{1,0:T(8,128)(2,1)}, u32[]{:S(2)}, u32[]{:S(2)}) collective-permute-start(bf16[768,2176]{1,0:T(8,128)(2,1)} %gather_tp.4.own_ref), channel_id=1, source_target_pairs={{0,4},{4,0},{1,5},{5,1},{2,6},{6,2},{3,7},{7,3},{8,12},{12,8},{9,1... | collective-permute-start | bytes 10027016 | tf_op jit(solution)/shard_map/ppermute | solution.py:1356
  293.9 1.4 slice-start.4
  296.3 58.1 %copy-start.4 = (s32[8,768,4]{2,1,0:T(8,128)}, s32[8,768,4]{2,1,0:T(8,128)S(1)}, u32[]{:S(2)}) copy-start(s32[8,768,4]{2,1,0:T(8,128)S(1)} %bitcast_dynamic-update-slice_fusion.column_ref) | copy-start | bytes 294916
  552.4 0.6 copy-start.21
  552.5 0.9 copy-start.12
  554.3 8.1 all-to-all-start
  557.7 304.5 %reduce-scatter.7.cloned.1.call-start = ((), (), s32[]{:S(2)}) async-start(), calls=%async_computation.10 | async-start | bytes 3932160 | tf_op jit(solution)/shard_map/reduce_scatter | solution.py:2023
  563.1 76.5 %copy-start.1 = (f32[192,2048]{1,0:T(8,128)S(1)}, f32[192,2048]{1,0:T(8,128)}, u32[]{:S(2)}) copy-start(f32[192,2048]{1,0:T(8,128)} %copy-done) | copy-start | bytes 4718596
  563.1 76.5 %copy-start.11 = (f32[2048]{0:T(1024)S(1)}, f32[2048]{0:T(1024)}, u32[]{:S(2)}) copy-start(f32[2048]{0:T(1024)} %copy-done.10) | copy-start | bytes 24580
  563.1 76.5 %copy-start.16 = (f32[192]{0:T(256)S(1)}, f32[192]{0:T(256)}, u32[]{:S(2)}) copy-start(f32[192]{0:T(256)} %copy-done.15) | copy-start | bytes 2308
  637.6 5.1 copy-start.2
  724.4 4.0 copy-start.25
  724.4 146.7 %reduce-scatter.11.cloned.1.call-start = ((), (), s32[]{:S(2)}) async-start(), calls=%async_computation.12 | async-start | bytes 2949120 | tf_op jit(solution)/shard_map/reduce_scatter | solution.py:2054
  724.6 3.8 copy-start.3
  730.3 2.0 copy-start.7
  732.3 163.6 %reduce-scatter.9.cloned.1.call-start = ((), (), s32[]{:S(2)}) async-start(), calls=%async_computation.11 | async-start | bytes 7077888 | tf_op jit(solution)/shard_map/reduce_scatter | solution.py:2064
  800.6 0.7 copy-start.20
  800.6 0.7 copy-start.17
  800.6 1.0 copy-start.9
  863.7 5.9 copy-start.8
  863.7 6.2 copy-start.14
  863.8 7.4 copy-start.18
  864.7 9.6 %copy-start.5 = (bf16[768,512]{1,0:T(8,128)(2,1)S(1)}, bf16[768,512]{1,0:T(8,128)(2,1)}, u32[]{:S(2)}) copy-start(bf16[768,512]{1,0:T(8,128)(2,1)} %in_ref.1) | copy-start | bytes 2359300
  864.7 21.5 %all-to-all-start.1 = ((bf16[192,4,512]{2,0,1:T(8,128)(2,1)}), bf16[192,4,512]{2,0,1:T(8,128)(2,1)S(1)}, u32[]{:S(2)}, u32[]{:S(2)}) async-start(bf16[192,4,512]{2,0,1:T(8,128)(2,1)} %bitcast.74), calls=%async_computation.3 | async-start | bytes 1572864 | tf_op jit(solution)/shard_map/all_to_all | solution.py:2043
  869.9 4.4 copy-start.6
  896.0 11.1 %slice-start.2 = ((s8[8388608]{0:T(1024)(128)(4,1)}), s8[4194304]{0:T(1024)(128)(4,1)S(1)}, s32[]{:S(2)}) async-start(s8[8388608]{0:T(1024)(128)(4,1)} %bitcast.79), calls=%async_computation.15 | async-start | bytes 8388608
  899.3 7.8 slice-start.3
  899.3 12.0 %slice-start = ((s8[8388608]{0:T(1024)(128)(4,1)}), s8[4194304]{0:T(1024)(128)(4,1)S(1)}, s32[]{:S(2)}) async-start(s8[8388608]{0:T(1024)(128)(4,1)} %bitcast.77), calls=%async_computation.13 | async-start | bytes 8388608
  907.1 5.2 slice-start.1
Sparse Core Ops, SparseCore 0:
  13.9 59.2 all-gather.3
  74.8 63.4 all-gather.5
  147.5 132.6 all-gather.7
  552.6 155.2 reduce-scatter.4
  724.5 58.3 reduce-scatter.6
  786.1 43.6 reduce-scatter.10
  833.8 62.1 reduce-scatter.8

commit v5 on v4

--- a/solution.py
+++ b/solution.py
@@ -2039,6 +2039,11 @@
     normed_grad, gains, along = close_tp(normed_part, gains, along, 7)
     along = along[:, None] / width
     normed_grad, out_sum = lax.optimization_barrier((normed_grad, out_sum))
+    grad_gate, grad_up, grad_down = then(normed_grad, grad_gate, grad_up, grad_down)
+    grad_gate, grad_up, grad_down = [
+        lax.clamp(jnp.float32(-jnp.inf), grad, jnp.float32(jnp.inf))
+        for grad in (grad_gate, grad_up, grad_down)
+    ]
     layer_sum = resid + out_sum
     layer_output = lax.all_to_all(
         layer_sum.astype(bf16), "tp", split_axis=1, concat_axis=0, tiled=True

time: 932 us -> 919 us (0.986)
  other arithmetic: 28 us -> 48.4 us
  waiting for transfers between devices: 35.4 us -> 16.6 us
  local copies, waits for them, and re-layouts: 48.9 us -> 33.1 us
    clamp x0 -> x3, other arithmetic: none -> 19 us  [on_device(): lax.clamp(jnp.float32(-jnp.inf), grad, jnp.float32(jnp.inf))]
    unnamed x76 -> x67, local copies, waits for them, and re-layouts: 23.8 us -> 7.47 us
    reduce_scatter x1, waiting for transfers between devices: 9.77 us -> 0.01 us  [on_device(): lax.psum_scatter(grad_qkv.astype(bf16), ROWS, scatter_dimension=0, tiled=...]
  transfers between devices with their start and end apart: 13 -> 13, of which waited for: 6 -> 4; matrix products, arithmetic and copies ran while one was open for 8% -> 10% of each run, Pallas kernels for 61% -> 62%
where the time goes in v5:
time: 919 us; the launch traced here: 910 us
  Pallas kernels  753 us (82%)
  other arithmetic  48.4 us (5%)
  local copies, waits for them, and re-layouts  33.1 us (4%)
  matrix products  30.7 us (3%)
  waiting for transfers between devices  16.6 us (2%)
  between operations  15.1 us (2%)
  starting transfers between devices  12.8 us (1%)
    pallas_call x1, Pallas kernels, run_exchange_pass(): pl.pallas_call(exchange_pass, grid=(2 * chunks, local), in_specs=[pl.Bloc...  185 us
    pallas_call x3, Pallas kernels, gather_tp(): pl.pallas_call(functools.partial(line_gather, size, columns), in_specs=[p...  162 us
    pallas_call x1, Pallas kernels, run_grads_scatter(): pl.pallas_call(functools.partial(grads_scatter, size, local), grid=(2 * l...  74.1 us
    pallas_call x1, Pallas kernels, close_tp(): pl.pallas_call(functools.partial(closing_sums, sizes, narrow), in_specs=[...  60.9 us
    pallas_call x1, Pallas kernels, scatter_tp(): pl.pallas_call(functools.partial(line_scatter, size, columns), in_specs=[...  59.3 us
    pallas_call x1, Pallas kernels, run_select_grads(): pl.pallas_call(select_grads, grid_spec=pltpu.PrefetchScalarGridSpec(num_s...  56.3 us
    pallas_call x1, Pallas kernels, gather_ctx(): pl.pallas_call(functools.partial(peer_gather, size), in_specs=[pl.BlockSp...  49.7 us
    pallas_call x1, Pallas kernels, scatter_ctx(): pl.pallas_call(functools.partial(peer_scatter, size), in_specs=[pl.BlockS...  37.1 us
  transfers between devices with their start and end apart: 13, of which 4 were waited for; matrix products, arithmetic and copies ran while one was open for 10% of the time, Pallas kernels for 62%

profile of v5, /device:TPU:0, one launch (start us, length us, event | category | flops | bytes accessed | tf_op | source)
XLA Modules:
  0.0 909.6 jit_solution(11591378711616366705)
XLA Ops:
  7.2 1.1 copy.126
  8.3 0.8 copy.127
  9.2 0.8 broadcast_in_dim.88
  9.9 0.8 broadcast_in_dim.89
  10.7 3.0 concatenate.28
  14.2 3.0 collective-permute-start
  17.2 55.7 %gather_tp.3.input_ref = bf16[768,2048]{1,0:T(8,128)(2,1)} custom-call(bf16[768,512]{1,0:T(8,128)(2,1)} %in_ref.1), custom_call_target="tpu_custom_call" | custom-call | bytes 150000000 | tf_op jit(solution)/shard_map/gather_tp/pallas_call | solution.py:1117
  74.3 1.4 fusion.20
  75.7 1.2 pad_maximum_fusion.1
  77.4 2.7 convert_reduce_fusion
  80.2 11.3 %project.1 = (bf16[768,2048]{1,0:T(8,128)(2,1)}, f32[768,1]{1,0:T(8,128)}, f32[768,1024]{1,0:T(8,128)}, bf16[768,512]{1,0:T(8,128)(2,1)}, bf16[768,1024]{1,0:T(8,128)(2,1)}) custom-call(bf16[768,2048]{1,0:T(8,128)(2,1)} %gather_tp.3.input_ref, f32[1,2048]{1,0:T(1,128)} %bitcast.86, bf16[2048,2176]{1,0:T(8,128)(2,1)} %all-gather.4.cloned.1.call-done.weight_ref, ...), custom_call_target="tpu_custom_call" | custom-call | flops 4831838208 | bytes 6291456 | tf_op jit(solution)/shard_map/project/pallas_call | solution.py:1528
  91.5 49.7 %gather_ctx.1.key_ref.value_ref = bf16[1536,1024]{1,0:T(8,128)(2,1)} custom-call(bf16[768,1024]{1,0:T(8,128)(2,1)} %get-tuple-element.66.in_ref), custom_call_target="tpu_custom_call" | custom-call | bytes 100000000 | tf_op jit(solution)/shard_map/gather_ctx/pallas_call | solution.py:1192
  141.2 6.0 concatenate.31
  148.5 1.3 copy.172
  149.8 16.0 %attend.1 = (bf16[768,512]{1,0:T(8,128)(2,1)}, f32[4,3,1,256]{3,2,1,0:T(1,128)}) custom-call(bf16[768,512]{1,0:T(8,128)(2,1)} %get-tuple-element.64.query_ref, bf16[1536,1024]{1,0:T(8,128)(2,1)} %gather_ctx.1.key_ref.value_ref, bf16[1536,1024]{1,0:T(8,128)(2,1)} %gather_ctx.1.key_ref.value_ref, f32[3,1,256]{2,1,0:T(1,128)} %convert_element_type.141.seg_row_ref, ...), custom_call_target="tpu_custom_call" | custom-call | flops 2415919104 | bytes 3145728 | tf_op jit(solution)/shard_map/attend/pallas_call | solution.py:1306
  165.8 5.3 convolution_convert_fusion.1.in_ref
  171.1 59.3 %scatter_tp.1 = f32[192,2048]{1,0:T(8,128)} custom-call(bf16[768,2048]{1,0:T(8,128)(2,1)} %convolution_convert_fusion.1.in_ref), custom_call_target="tpu_custom_call" | custom-call | bytes 150000000 | tf_op jit(solution)/shard_map/scatter_tp/pallas_call | solution.py:1137
  230.4 1.9 multiply_reduce_fusion.2
  232.4 1.1 copy-done
  233.7 1.5 fusion.34
  235.5 1.1 concatenate.32.in_ref
  236.7 54.7 %gather_tp.4.own_ref = bf16[768,2176]{1,0:T(8,128)(2,1)} custom-call(bf16[192,2176]{1,0:T(8,128)(2,1)} %concatenate.32.in_ref), custom_call_target="tpu_custom_call" | custom-call | bytes 150000000 | tf_op jit(solution)/shard_map/gather_tp/pallas_call | solution.py:1117
  291.5 0.7 collective-permute-start.2
  292.2 1.6 collective-permute-start.3
  293.8 1.4 slice-done.2
  296.2 1.8 copy.153.rank_ref
  298.0 56.3 %select_grads.1 = (bf16[8,4,256,2048]{3,2,1,0:T(8,128)(2,1)}, f32[8,4,256,256]{3,2,1,0:T(8,128)}) custom-call(s32[8]{0:T(128)} %stack.83.ids_ref, s32[8,4,1,768]{3,2,1,0:T(1,128)} %copy.153.rank_ref, bf16[6144,2176]{1,0:T(8,128)(2,1)} %all-gather.8.cloned.1.call-done.grad_ref, bf16[4,256,2048]{2,1,0:T(8,128)(2,1)} %down_ref.1), custom_call_target="tpu_custom_call" | custom-call | flops 34359738368 | bytes 58720256 | tf_op jit(solution)/shard_map/select_grads/pallas_call | solution.py:580
  354.3 12.3 %collective-permute-done.2.from_across_ref = bf16[768,2176]{1,0:T(8,128)(2,1)} collective-permute-done((bf16[768,2176]{1,0:T(8,128)(2,1)}, bf16[768,2176]{1,0:T(8,128)(2,1)}, u32[]{:S(2)}, u32[]{:S(2)}) %collective-permute-start.2) | collective-permute-done | bytes 3342368 | tf_op jit(solution)/shard_map/ppermute | solution.py:1352
  366.9 185.3 %exchange_pass.1 = (bf16[8,4,256,2048]{3,2,1,0:T(8,128)(2,1)}, bf16[8,4,256,256]{3,2,1,0:T(8,128)(2,1)}, bf16[8,4,256,256]{3,2,1,0:T(8,128)(2,1)}, bf16[8,4,256,...) custom-call(s32[8,4,1,768]{3,2,1,0:T(1,128)} %copy.153.rank_ref, ...), custom_call_target="tpu_custom_call" | custom-call | flops 85899345920 | bytes 71303168 | tf_op jit(solution)/shard_map/exchange_pass/pallas_call | solution.py:623
  553.2 0.9 select_reduce_fusion
  554.1 3.4 all-to-all-start
  557.6 0.9 slice.71
  558.7 3.6 all-to-all-done
  562.9 74.1 %grads_scatter.1 = (f32[192,2048]{1,0:T(8,128)}, f32[32,768]{1,0:T(8,128)}, f32[4,2048,256]{2,1,0:T(8,128)}, f32[4,2048,256]{2,1,0:T(8,128)}, f32[4,256,2048]{2,1,0:T(8,128)}) custom-call(bf16[768,2048]{1,0:T(8,128)(2,1)} %get-tuple-element.75.in_ref, f32[32,768]{1,0:T(8,128)} %reshape.181.small_ref, bf16[8,4,256,2048]{3,2,1,0:T(8,128)(2,1)} %get-tuple-element.77.rows_ref, ...), custom_call_target="tpu_custom_call" | custom-call | flops 25769803776 | bytes 150000000 | tf_op jit(solution)/shard_map/grads_scatter/pallas_call | solution.py:1776
  637.0 1.0 fusion.21
  638.1 0.9 fusion.22
  639.0 3.2 multiply_reduce_fusion
  642.3 2.6 add_convert_fusion.1.in_ref
  644.9 52.0 %gather_tp.5 = bf16[768,2048]{1,0:T(8,128)(2,1)} custom-call(bf16[192,2048]{1,0:T(8,128)(2,1)} %add_convert_fusion.1.in_ref), custom_call_target="tpu_custom_call" | custom-call | bytes 150000000 | tf_op jit(solution)/shard_map/gather_tp/pallas_call | solution.py:1117
  696.9 5.3 fusion.9.grad_ref
  702.2 22.0 %attend_back.1 = (f32[768,512]{1,0:T(8,128)}, bf16[1536,512]{1,0:T(8,128)(2,1)}, bf16[1536,512]{1,0:T(8,128)(2,1)}) custom-call(bf16[768,512]{1,0:T(8,128)(2,1)} %get-tuple-element.64.query_ref, bf16[1536,1024]{1,0:T(8,128)(2,1)} %gather_ctx.1.key_ref.value_ref, bf16[1536,1024]{1,0:T(8,128)(2,1)} %gather_ctx.1.key_ref.value_ref, ...), custom_call_target="tpu_custom_call" | custom-call | flops 6039797760 | bytes 6291456 | tf_op jit(solution)/shard_map/attend_back/pallas_call | solution.py:1328
  724.6 3.7 fusion.3
  728.3 1.9 convolution_convert_fusion.2
  730.2 2.0 maximum_maximum_fusion
  732.2 3.5 pad_maximum_fusion.in_ref
  735.7 37.1 %scatter_ctx.1.group_grad_ref = bf16[768,1024]{1,0:T(8,128)(2,1)} custom-call(bf16[1536,1024]{1,0:T(8,128)(2,1)} %pad_maximum_fusion.in_ref), custom_call_target="tpu_custom_call" | custom-call | bytes 100000000 | tf_op jit(solution)/shard_map/scatter_ctx/pallas_call | solution.py:1212
  772.8 18.5 %project_back.1 = (bf16[768,1536]{1,0:T(8,128)(2,1)}, bf16[768,2048]{1,0:T(8,128)(2,1)}, f32[768,1]{1,0:T(8,128)}, f32[1,2048]{1,0:T(1,128)}, f32[2,128]{1,0:T(2,128)}) custom-call(f32[768,512]{1,0:T(8,128)} %get-tuple-element.84.query_grad_ref, bf16[768,1024]{1,0:T(8,128)(2,1)} %scatter_ctx.1.group_grad_ref, f32[768,1024]{1,0:T(8,128)} %get-tuple-element.89.pre_ref, ...), custom_call_target="tpu_custom_call" | custom-call | flops 4831838208 | bytes 8388608 | tf_op jit(solution)/shard_map/project_back/pallas_call | solution.py:1570
  791.3 9.3 %convolution_convert_fusion = bf16[2048,1536]{1,0:T(8,128)(2,1)} fusion(bf16[768,2048]{1,0:T(8,128)(2,1)} %get-tuple-element.101, bf16[768,1536]{1,0:T(8,128)(2,1)} %get-tuple-element.102), kind=kOutput, calls=%fused_computation | convolution fusion | flops 4834983936 | bytes 11796480 | tf_op jit(solution)/shard_map/dot_general | solution.py:2056
  800.6 0.9 copy-done.9
  801.7 1.2 slice_convert_fusion
  804.0 60.9 %close_tp.1 = (f32[768,512]{1,0:T(8,128)}, f32[8,640]{1,0:T(8,128)}, f32[8,128]{1,0:T(8,128)}) custom-call(bf16[768,2048]{1,0:T(8,128)(2,1)} %get-tuple-element.91.in_ref, f32[8,768]{1,0:T(8,128)} %pad_maximum_fusion.3.small_ref), custom_call_target="tpu_custom_call" | custom-call | bytes 150000000 | tf_op jit(solution)/shard_map/close_tp/pallas_call | solution.py:1163
  864.9 0.7 reshape.184
  867.4 1.3 convert_element_type.157
  868.8 1.9 convert_element_type.164
  870.6 1.3 slice.98
  872.2 0.9 copy.175
  873.1 3.5 all-to-all-start.1
  876.6 0.8 slice_bitcast_fusion
  877.5 7.5 broadcast_clamp_fusion.2
  885.0 7.5 broadcast_clamp_fusion.1
  892.5 2.8 multiply_add_fusion
  895.3 4.0 broadcast_clamp_fusion
  899.3 2.3 fusion.31
  901.6 0.9 copy.189
  (134 shorter events, 10.9 us)
Async XLA Ops:
  7.2 6.7 copy-start.18
  7.2 6.7 copy-start.23
  7.2 66.1 %all-gather.4.cloned.1.call-start = ((), (), s32[]{:S(2)}) async-start(), calls=%async_computation.6 | async-start | bytes 10027008 | tf_op jit(solution)/shard_map/all_gather | solution.py:1884
  13.8 59.6 %copy-start.14 = (s32[768,8]{0,1:T(8,128)S(1)}, s32[768,8]{0,1:T(8,128)}, u32[]{:S(2)}) copy-start(s32[768,8]{0,1:T(8,128)} %param.20) | copy-start | bytes 73732
  13.8 59.9 %copy-start.21 = (f32[128]{0:T(128)S(1)}, f32[128]{0:T(128)}, u32[]{:S(2)}) copy-start(f32[128]{0:T(128)} %param.26) | copy-start | bytes 1540
  13.8 59.9 %copy-start.22 = (f32[128]{0:T(128)S(1)}, f32[128]{0:T(128)}, u32[]{:S(2)}) copy-start(f32[128]{0:T(128)} %param.25) | copy-start | bytes 1540
  13.8 127.4 %all-gather.6.cloned.1.call-start = ((), (), s32[]{:S(2)}) async-start(), calls=%async_computation.7 | async-start | bytes 3932160 | tf_op jit(solution)/shard_map/all_gather | solution.py:1905
  14.2 58.8 %collective-permute-start = (f32[1,768]{1,0:T(1,128)S(1)}, f32[1,768]{1,0:T(1,128)S(1)}, u32[]{:S(2)}, u32[]{:S(2)}) collective-permute-start(f32[1,768]{1,0:T(1,128)S(1)} %convert_element_type.136), channel_id=1, source_target_pairs={{0,4},{4,0},{1,5},{5,1},{2,6},{6,2},{3,7},{7,3},{8,12},{12,8},{9,1... | collective-permute-start | bytes 9224 | tf_op jit(solution)/shard_map/ppermute | solution.py:1899
  73.3 220.5 %all-gather.8.cloned.1.call-start = ((), (), s32[]{:S(2)}) async-start(), calls=%async_computation.8 | async-start | bytes 30081024 | tf_op jit(solution)/shard_map/all_gather | solution.py:1931
  80.2 152.2 %copy-start.11 = (f32[2048]{0:T(1024)}, f32[2048]{0:T(1024)S(1)}, u32[]{:S(2)}) copy-start(f32[2048]{0:T(1024)S(1)} %get-tuple-element.110) | copy-start | bytes 24580
  147.2 577.0 %reduce-scatter.5.cloned.1.call-start = ((), (), s32[]{:S(2)}) async-start(), calls=%async_computation.9 | async-start | bytes 28311552 | tf_op jit(solution)/shard_map/reduce_scatter | solution.py:2013
  232.3 1.1 copy-start
  232.4 3.2 copy-start.15
  291.4 75.5 %collective-permute-start.1 = (bf16[768,2176]{1,0:T(8,128)(2,1)}, bf16[768,2176]{1,0:T(8,128)(2,1)}, u32[]{:S(2)}, u32[]{:S(2)}) collective-permute-start(bf16[768,2176]{1,0:T(8,128)(2,1)} %gather_tp.4.own_ref), channel_id=1, source_target_pairs={{0,8},{8,0},{16,24},{24,16},{1,9},{9,1},{17,25},{25,17},{2,10},{10... | collective-permute-start | bytes 10027016 | tf_op jit(solution)/shard_map/ppermute | solution.py:1348
  291.5 75.0 %collective-permute-start.2 = (bf16[768,2176]{1,0:T(8,128)(2,1)}, bf16[768,2176]{1,0:T(8,128)(2,1)}, u32[]{:S(2)}, u32[]{:S(2)}) collective-permute-start(bf16[768,2176]{1,0:T(8,128)(2,1)} %gather_tp.4.own_ref), channel_id=1, source_target_pairs={{0,16},{8,24},{16,0},{24,8},{1,17},{9,25},{17,1},{25,9},{2,18},{10... | collective-permute-start | bytes 10027016 | tf_op jit(solution)/shard_map/ppermute | solution.py:1352
  292.2 74.7 %collective-permute-start.3 = (bf16[768,2176]{1,0:T(8,128)(2,1)}, bf16[768,2176]{1,0:T(8,128)(2,1)}, u32[]{:S(2)}, u32[]{:S(2)}) collective-permute-start(bf16[768,2176]{1,0:T(8,128)(2,1)} %gather_tp.4.own_ref), channel_id=1, source_target_pairs={{0,4},{4,0},{1,5},{5,1},{2,6},{6,2},{3,7},{7,3},{8,12},{12,8},{9,1... | collective-permute-start | bytes 10027016 | tf_op jit(solution)/shard_map/ppermute | solution.py:1356
  293.8 1.4 slice-start.2
  296.2 58.1 %copy-start.4 = (s32[8,768,4]{2,1,0:T(8,128)}, s32[8,768,4]{2,1,0:T(8,128)S(1)}, u32[]{:S(2)}) copy-start(s32[8,768,4]{2,1,0:T(8,128)S(1)} %bitcast_dynamic-update-slice_fusion.column_ref) | copy-start | bytes 294916
  552.3 0.6 copy-start.20
  552.3 0.9 copy-start.13
  554.1 8.1 all-to-all-start
  557.5 309.9 %reduce-scatter.7.cloned.1.call-start = ((), (), s32[]{:S(2)}) async-start(), calls=%async_computation.10 | async-start | bytes 3932160 | tf_op jit(solution)/shard_map/reduce_scatter | solution.py:2023
  562.9 76.1 %copy-start.1 = (f32[192,2048]{1,0:T(8,128)S(1)}, f32[192,2048]{1,0:T(8,128)}, u32[]{:S(2)}) copy-start(f32[192,2048]{1,0:T(8,128)} %copy-done) | copy-start | bytes 4718596
  562.9 76.1 %copy-start.12 = (f32[2048]{0:T(1024)S(1)}, f32[2048]{0:T(1024)}, u32[]{:S(2)}) copy-start(f32[2048]{0:T(1024)} %copy-done.11) | copy-start | bytes 24580
  562.9 76.1 %copy-start.16 = (f32[192]{0:T(256)S(1)}, f32[192]{0:T(256)}, u32[]{:S(2)}) copy-start(f32[192]{0:T(256)} %copy-done.15) | copy-start | bytes 2308
  637.0 5.2 copy-start.2
  724.2 4.0 copy-start.24
  724.2 144.5 %reduce-scatter.11.cloned.1.call-start = ((), (), s32[]{:S(2)}) async-start(), calls=%async_computation.12 | async-start | bytes 2949120 | tf_op jit(solution)/shard_map/reduce_scatter | solution.py:2059
  724.5 3.8 copy-start.3
  730.2 2.0 copy-start.8
  732.2 167.2 %reduce-scatter.9.cloned.1.call-start = ((), (), s32[]{:S(2)}) async-start(), calls=%async_computation.11 | async-start | bytes 7077888 | tf_op jit(solution)/shard_map/reduce_scatter | solution.py:2069
  800.5 1.0 copy-start.9
  800.5 2.6 copy-start.10
  800.5 2.8 copy-start.19
  800.6 2.8 copy-start.17
  872.2 4.5 copy-start.6
  873.1 26.2 %all-to-all-start.1 = ((bf16[192,4,512]{2,0,1:T(8,128)(2,1)}), bf16[192,4,512]{2,0,1:T(8,128)(2,1)S(1)}, u32[]{:S(2)}, u32[]{:S(2)}) async-start(bf16[192,4,512]{2,0,1:T(8,128)(2,1)} %bitcast.74), calls=%async_computation.3 | async-start | bytes 1572864 | tf_op jit(solution)/shard_map/all_to_all | solution.py:2048
  877.4 17.9 %slice-start = ((s8[8388608]{0:T(1024)(128)(4,1)}), s8[4194304]{0:T(1024)(128)(4,1)S(1)}, s32[]{:S(2)}) async-start(s8[8388608]{0:T(1024)(128)(4,1)} %bitcast.77), calls=%async_computation.13 | async-start | bytes 8388608
  885.0 7.5 copy-start.5
  885.0 7.5 copy-start.7
  885.0 10.4 %slice-start.1 = ((s8[8388608]{0:T(1024)(128)(4,1)}), s8[4194304]{0:T(1024)(128)(4,1)S(1)}, s32[]{:S(2)}) async-start(s8[8388608]{0:T(1024)(128)(4,1)} %bitcast.77), calls=%async_computation.14 | async-start | bytes 8388608
Sparse Core Ops, SparseCore 0:
  13.9 59.2 all-gather.3
  74.8 63.4 all-gather.5
  147.4 132.4 all-gather.7
  552.4 155.2 reduce-scatter.4
  724.4 58.4 reduce-scatter.6
  786.1 43.8 reduce-scatter.10
  833.4 61.7 reduce-scatter.8

commit v6 on v5

--- a/solution.py
+++ b/solution.py
@@ -364,7 +364,7 @@
         for peer in (beside_id, across_id, other_id):
             pl.semaphore_signal(barrier, inc=1, device_id=peer, device_id_type=MESH)
         pl.semaphore_wait(barrier, 3)
-        for number in range(4):
+        for number in (0, 2, 3):
             pass_copy(number).start()
         for at in range(local):
             weight_load(gate_in_ref, gate_ref, gate_sem, at).start()
@@ -373,6 +373,7 @@
         down_load.start()
         pass_copy(0).wait_recv()
         token_load(0).start()
+        pass_copy(1).start()
 
     @pl.when(jnp.logical_and(step == 3, expert == 0))
     def _():
@@ -1698,7 +1699,7 @@
 
     for stage in range(1, size - 1):
 
-        @pl.when(jnp.logical_and(step == min(2 * stage, 2 * local - 1), part == 0))
+        @pl.when(2 * step + part == min(3 * stage, 4 * local - 1))
         def _():
             receive(stage - 1)
             send(stage)

time: 919 us -> 926 us (level)
  transfers between devices with their start and end apart: 13 -> 13, of which waited for: 4 -> 4; matrix products, arithmetic and copies ran while one was open for 10% -> 10% of each run, Pallas kernels for 62% -> 63%
where the time goes in v6:
time: 926 us; the launch traced here: 916 us
  Pallas kernels  760 us (82%)
  other arithmetic  48.5 us (5%)
  local copies, waits for them, and re-layouts  33.1 us (4%)
  matrix products  30.7 us (3%)
  waiting for transfers between devices  16.6 us (2%)
  between operations  15.1 us (2%)
  starting transfers between devices  12.8 us (1%)
    pallas_call x1, Pallas kernels, run_exchange_pass(): pl.pallas_call(exchange_pass, grid=(2 * chunks, local), in_specs=[pl.Bloc...  185 us
    pallas_call x3, Pallas kernels, gather_tp(): pl.pallas_call(functools.partial(line_gather, size, columns), in_specs=[p...  171 us
    pallas_call x1, Pallas kernels, run_grads_scatter(): pl.pallas_call(functools.partial(grads_scatter, size, local), grid=(2 * l...  74.1 us
    pallas_call x1, Pallas kernels, close_tp(): pl.pallas_call(functools.partial(closing_sums, sizes, narrow), in_specs=[...  59.4 us
    pallas_call x1, Pallas kernels, scatter_tp(): pl.pallas_call(functools.partial(line_scatter, size, columns), in_specs=[...  59.3 us
    pallas_call x1, Pallas kernels, run_select_grads(): pl.pallas_call(select_grads, grid_spec=pltpu.PrefetchScalarGridSpec(num_s...  56.3 us
    pallas_call x1, Pallas kernels, gather_ctx(): pl.pallas_call(functools.partial(peer_gather, size), in_specs=[pl.BlockSp...  49.7 us
    pallas_call x1, Pallas kernels, scatter_ctx(): pl.pallas_call(functools.partial(peer_scatter, size), in_specs=[pl.BlockS...  37 us
  transfers between devices with their start and end apart: 13, of which 4 were waited for; matrix products, arithmetic and copies ran while one was open for 10% of the time, Pallas kernels for 63%

profile of v6, /device:TPU:0, one launch (start us, length us, event | category | flops | bytes accessed | tf_op | source)
XLA Modules:
  0.0 916.3 jit_solution(15448568131614890959)
XLA Ops:
  7.2 1.1 copy.126
  8.3 0.8 copy.127
  9.2 0.8 broadcast_in_dim.88
  9.9 0.8 broadcast_in_dim.89
  10.7 3.0 concatenate.28
  14.2 3.0 collective-permute-start
  17.2 55.7 %gather_tp.3.input_ref = bf16[768,2048]{1,0:T(8,128)(2,1)} custom-call(bf16[768,512]{1,0:T(8,128)(2,1)} %in_ref.1), custom_call_target="tpu_custom_call" | custom-call | bytes 150000000 | tf_op jit(solution)/shard_map/gather_tp/pallas_call | solution.py:1118
  74.3 1.4 fusion.20
  75.7 1.2 pad_maximum_fusion.1
  77.4 2.7 convert_reduce_fusion
  80.2 11.3 %project.1 = (bf16[768,2048]{1,0:T(8,128)(2,1)}, f32[768,1]{1,0:T(8,128)}, f32[768,1024]{1,0:T(8,128)}, bf16[768,512]{1,0:T(8,128)(2,1)}, bf16[768,1024]{1,0:T(8,128)(2,1)}) custom-call(bf16[768,2048]{1,0:T(8,128)(2,1)} %gather_tp.3.input_ref, f32[1,2048]{1,0:T(1,128)} %bitcast.86, bf16[2048,2176]{1,0:T(8,128)(2,1)} %all-gather.4.cloned.1.call-done.weight_ref, ...), custom_call_target="tpu_custom_call" | custom-call | flops 4831838208 | bytes 6291456 | tf_op jit(solution)/shard_map/project/pallas_call | solution.py:1529
  91.5 49.7 %gather_ctx.1.key_ref.value_ref = bf16[1536,1024]{1,0:T(8,128)(2,1)} custom-call(bf16[768,1024]{1,0:T(8,128)(2,1)} %get-tuple-element.66.in_ref), custom_call_target="tpu_custom_call" | custom-call | bytes 100000000 | tf_op jit(solution)/shard_map/gather_ctx/pallas_call | solution.py:1193
  141.2 6.0 concatenate.31
  148.5 1.3 copy.172
  149.8 16.0 %attend.1 = (bf16[768,512]{1,0:T(8,128)(2,1)}, f32[4,3,1,256]{3,2,1,0:T(1,128)}) custom-call(bf16[768,512]{1,0:T(8,128)(2,1)} %get-tuple-element.64.query_ref, bf16[1536,1024]{1,0:T(8,128)(2,1)} %gather_ctx.1.key_ref.value_ref, bf16[1536,1024]{1,0:T(8,128)(2,1)} %gather_ctx.1.key_ref.value_ref, f32[3,1,256]{2,1,0:T(1,128)} %convert_element_type.141.seg_row_ref, ...), custom_call_target="tpu_custom_call" | custom-call | flops 2415919104 | bytes 3145728 | tf_op jit(solution)/shard_map/attend/pallas_call | solution.py:1307
  165.8 5.3 convolution_convert_fusion.1.in_ref
  171.1 59.3 %scatter_tp.1 = f32[192,2048]{1,0:T(8,128)} custom-call(bf16[768,2048]{1,0:T(8,128)(2,1)} %convolution_convert_fusion.1.in_ref), custom_call_target="tpu_custom_call" | custom-call | bytes 150000000 | tf_op jit(solution)/shard_map/scatter_tp/pallas_call | solution.py:1138
  230.4 1.9 multiply_reduce_fusion.2
  232.4 1.1 copy-done
  233.7 1.5 fusion.34
  235.5 1.1 concatenate.32.in_ref
  236.7 54.7 %gather_tp.4.own_ref = bf16[768,2176]{1,0:T(8,128)(2,1)} custom-call(bf16[192,2176]{1,0:T(8,128)(2,1)} %concatenate.32.in_ref), custom_call_target="tpu_custom_call" | custom-call | bytes 150000000 | tf_op jit(solution)/shard_map/gather_tp/pallas_call | solution.py:1118
  291.5 0.7 collective-permute-start.2
  292.2 1.6 collective-permute-start.3
  293.8 1.4 slice-done.2
  296.2 1.8 copy.153.rank_ref
  298.0 56.3 %select_grads.1 = (bf16[8,4,256,2048]{3,2,1,0:T(8,128)(2,1)}, f32[8,4,256,256]{3,2,1,0:T(8,128)}) custom-call(s32[8]{0:T(128)} %stack.83.ids_ref, s32[8,4,1,768]{3,2,1,0:T(1,128)} %copy.153.rank_ref, bf16[6144,2176]{1,0:T(8,128)(2,1)} %all-gather.8.cloned.1.call-done.grad_ref, bf16[4,256,2048]{2,1,0:T(8,128)(2,1)} %down_ref.1), custom_call_target="tpu_custom_call" | custom-call | flops 34359738368 | bytes 58720256 | tf_op jit(solution)/shard_map/select_grads/pallas_call | solution.py:581
  354.3 12.3 %collective-permute-done.2.from_across_ref = bf16[768,2176]{1,0:T(8,128)(2,1)} collective-permute-done((bf16[768,2176]{1,0:T(8,128)(2,1)}, bf16[768,2176]{1,0:T(8,128)(2,1)}, u32[]{:S(2)}, u32[]{:S(2)}) %collective-permute-start.2) | collective-permute-done | bytes 3342368 | tf_op jit(solution)/shard_map/ppermute | solution.py:1353
  366.9 185.3 %exchange_pass.1 = (bf16[8,4,256,2048]{3,2,1,0:T(8,128)(2,1)}, bf16[8,4,256,256]{3,2,1,0:T(8,128)(2,1)}, bf16[8,4,256,256]{3,2,1,0:T(8,128)(2,1)}, bf16[8,4,256,...) custom-call(s32[8,4,1,768]{3,2,1,0:T(1,128)} %copy.153.rank_ref, ...), custom_call_target="tpu_custom_call" | custom-call | flops 85899345920 | bytes 71303168 | tf_op jit(solution)/shard_map/exchange_pass/pallas_call | solution.py:624
  553.2 0.9 select_reduce_fusion
  554.1 3.4 all-to-all-start
  557.6 0.9 slice.71
  558.7 3.6 all-to-all-done
  562.9 74.1 %grads_scatter.1 = (f32[192,2048]{1,0:T(8,128)}, f32[32,768]{1,0:T(8,128)}, f32[4,2048,256]{2,1,0:T(8,128)}, f32[4,2048,256]{2,1,0:T(8,128)}, f32[4,256,2048]{2,1,0:T(8,128)}) custom-call(bf16[768,2048]{1,0:T(8,128)(2,1)} %get-tuple-element.75.in_ref, f32[32,768]{1,0:T(8,128)} %reshape.181.small_ref, bf16[8,4,256,2048]{3,2,1,0:T(8,128)(2,1)} %get-tuple-element.77.rows_ref, ...), custom_call_target="tpu_custom_call" | custom-call | flops 25769803776 | bytes 150000000 | tf_op jit(solution)/shard_map/grads_scatter/pallas_call | solution.py:1777
  637.0 1.0 fusion.21
  638.1 0.9 fusion.22
  639.0 3.2 multiply_reduce_fusion
  642.3 2.6 add_convert_fusion.1.in_ref
  644.9 60.2 %gather_tp.5 = bf16[768,2048]{1,0:T(8,128)(2,1)} custom-call(bf16[192,2048]{1,0:T(8,128)(2,1)} %add_convert_fusion.1.in_ref), custom_call_target="tpu_custom_call" | custom-call | bytes 150000000 | tf_op jit(solution)/shard_map/gather_tp/pallas_call | solution.py:1118
  705.1 5.2 fusion.9.grad_ref
  710.3 22.0 %attend_back.1 = (f32[768,512]{1,0:T(8,128)}, bf16[1536,512]{1,0:T(8,128)(2,1)}, bf16[1536,512]{1,0:T(8,128)(2,1)}) custom-call(bf16[768,512]{1,0:T(8,128)(2,1)} %get-tuple-element.64.query_ref, bf16[1536,1024]{1,0:T(8,128)(2,1)} %gather_ctx.1.key_ref.value_ref, bf16[1536,1024]{1,0:T(8,128)(2,1)} %gather_ctx.1.key_ref.value_ref, ...), custom_call_target="tpu_custom_call" | custom-call | flops 6039797760 | bytes 6291456 | tf_op jit(solution)/shard_map/attend_back/pallas_call | solution.py:1329
  732.7 3.7 fusion.3
  736.4 1.9 convolution_convert_fusion.2
  738.3 2.0 maximum_maximum_fusion
  740.3 3.5 pad_maximum_fusion.in_ref
  743.8 37.0 %scatter_ctx.1.group_grad_ref = bf16[768,1024]{1,0:T(8,128)(2,1)} custom-call(bf16[1536,1024]{1,0:T(8,128)(2,1)} %pad_maximum_fusion.in_ref), custom_call_target="tpu_custom_call" | custom-call | bytes 100000000 | tf_op jit(solution)/shard_map/scatter_ctx/pallas_call | solution.py:1213
  780.8 18.5 %project_back.1 = (bf16[768,1536]{1,0:T(8,128)(2,1)}, bf16[768,2048]{1,0:T(8,128)(2,1)}, f32[768,1]{1,0:T(8,128)}, f32[1,2048]{1,0:T(1,128)}, f32[2,128]{1,0:T(2,128)}) custom-call(f32[768,512]{1,0:T(8,128)} %get-tuple-element.84.query_grad_ref, bf16[768,1024]{1,0:T(8,128)(2,1)} %scatter_ctx.1.group_grad_ref, f32[768,1024]{1,0:T(8,128)} %get-tuple-element.89.pre_ref, ...), custom_call_target="tpu_custom_call" | custom-call | flops 4831838208 | bytes 8388608 | tf_op jit(solution)/shard_map/project_back/pallas_call | solution.py:1571
  799.4 9.3 %convolution_convert_fusion = bf16[2048,1536]{1,0:T(8,128)(2,1)} fusion(bf16[768,2048]{1,0:T(8,128)(2,1)} %get-tuple-element.101, bf16[768,1536]{1,0:T(8,128)(2,1)} %get-tuple-element.102), kind=kOutput, calls=%fused_computation | convolution fusion | flops 4834983936 | bytes 11796480 | tf_op jit(solution)/shard_map/dot_general | solution.py:2057
  808.7 0.9 copy-done.9
  809.8 1.2 slice_convert_fusion
  812.1 59.4 %close_tp.1 = (f32[768,512]{1,0:T(8,128)}, f32[8,640]{1,0:T(8,128)}, f32[8,128]{1,0:T(8,128)}) custom-call(bf16[768,2048]{1,0:T(8,128)(2,1)} %get-tuple-element.91.in_ref, f32[8,768]{1,0:T(8,128)} %pad_maximum_fusion.3.small_ref), custom_call_target="tpu_custom_call" | custom-call | bytes 150000000 | tf_op jit(solution)/shard_map/close_tp/pallas_call | solution.py:1164
  871.5 0.7 reshape.184
  874.1 1.3 convert_element_type.157
  875.4 1.9 convert_element_type.164
  877.2 1.3 slice.98
  878.8 0.9 copy.175
  879.7 3.5 all-to-all-start.1
  883.2 0.8 slice_bitcast_fusion
  884.1 7.6 broadcast_clamp_fusion.2
  891.7 7.5 broadcast_clamp_fusion.1
  899.2 2.8 multiply_add_fusion
  902.0 4.0 broadcast_clamp_fusion
  906.0 2.3 fusion.31
  908.3 0.9 copy.189
  (134 shorter events, 10.9 us)
Async XLA Ops:
  7.2 6.7 copy-start.18
  7.2 6.7 copy-start.23
  7.2 66.1 %all-gather.4.cloned.1.call-start = ((), (), s32[]{:S(2)}) async-start(), calls=%async_computation.6 | async-start | bytes 10027008 | tf_op jit(solution)/shard_map/all_gather | solution.py:1885
  13.8 59.6 %copy-start.14 = (s32[768,8]{0,1:T(8,128)S(1)}, s32[768,8]{0,1:T(8,128)}, u32[]{:S(2)}) copy-start(s32[768,8]{0,1:T(8,128)} %param.20) | copy-start | bytes 73732
  13.8 59.9 %copy-start.21 = (f32[128]{0:T(128)S(1)}, f32[128]{0:T(128)}, u32[]{:S(2)}) copy-start(f32[128]{0:T(128)} %param.26) | copy-start | bytes 1540
  13.8 59.9 %copy-start.22 = (f32[128]{0:T(128)S(1)}, f32[128]{0:T(128)}, u32[]{:S(2)}) copy-start(f32[128]{0:T(128)} %param.25) | copy-start | bytes 1540
  13.8 127.4 %all-gather.6.cloned.1.call-start = ((), (), s32[]{:S(2)}) async-start(), calls=%async_computation.7 | async-start | bytes 3932160 | tf_op jit(solution)/shard_map/all_gather | solution.py:1906
  14.2 58.8 %collective-permute-start = (f32[1,768]{1,0:T(1,128)S(1)}, f32[1,768]{1,0:T(1,128)S(1)}, u32[]{:S(2)}, u32[]{:S(2)}) collective-permute-start(f32[1,768]{1,0:T(1,128)S(1)} %convert_element_type.136), channel_id=1, source_target_pairs={{0,4},{4,0},{1,5},{5,1},{2,6},{6,2},{3,7},{7,3},{8,12},{12,8},{9,1... | collective-permute-start | bytes 9224 | tf_op jit(solution)/shard_map/ppermute | solution.py:1900
  73.3 220.5 %all-gather.8.cloned.1.call-start = ((), (), s32[]{:S(2)}) async-start(), calls=%async_computation.8 | async-start | bytes 30081024 | tf_op jit(solution)/shard_map/all_gather | solution.py:1932
  80.2 152.2 %copy-start.11 = (f32[2048]{0:T(1024)}, f32[2048]{0:T(1024)S(1)}, u32[]{:S(2)}) copy-start(f32[2048]{0:T(1024)S(1)} %get-tuple-element.110) | copy-start | bytes 24580
  147.2 585.1 %reduce-scatter.5.cloned.1.call-start = ((), (), s32[]{:S(2)}) async-start(), calls=%async_computation.9 | async-start | bytes 28311552 | tf_op jit(solution)/shard_map/reduce_scatter | solution.py:2014
  232.3 1.1 copy-start
  232.4 3.2 copy-start.15
  291.4 75.5 %collective-permute-start.1 = (bf16[768,2176]{1,0:T(8,128)(2,1)}, bf16[768,2176]{1,0:T(8,128)(2,1)}, u32[]{:S(2)}, u32[]{:S(2)}) collective-permute-start(bf16[768,2176]{1,0:T(8,128)(2,1)} %gather_tp.4.own_ref), channel_id=1, source_target_pairs={{0,8},{8,0},{16,24},{24,16},{1,9},{9,1},{17,25},{25,17},{2,10},{10... | collective-permute-start | bytes 10027016 | tf_op jit(solution)/shard_map/ppermute | solution.py:1349
  291.5 75.0 %collective-permute-start.2 = (bf16[768,2176]{1,0:T(8,128)(2,1)}, bf16[768,2176]{1,0:T(8,128)(2,1)}, u32[]{:S(2)}, u32[]{:S(2)}) collective-permute-start(bf16[768,2176]{1,0:T(8,128)(2,1)} %gather_tp.4.own_ref), channel_id=1, source_target_pairs={{0,16},{8,24},{16,0},{24,8},{1,17},{9,25},{17,1},{25,9},{2,18},{10... | collective-permute-start | bytes 10027016 | tf_op jit(solution)/shard_map/ppermute | solution.py:1353
  292.2 74.7 %collective-permute-start.3 = (bf16[768,2176]{1,0:T(8,128)(2,1)}, bf16[768,2176]{1,0:T(8,128)(2,1)}, u32[]{:S(2)}, u32[]{:S(2)}) collective-permute-start(bf16[768,2176]{1,0:T(8,128)(2,1)} %gather_tp.4.own_ref), channel_id=1, source_target_pairs={{0,4},{4,0},{1,5},{5,1},{2,6},{6,2},{3,7},{7,3},{8,12},{12,8},{9,1... | collective-permute-start | bytes 10027016 | tf_op jit(solution)/shard_map/ppermute | solution.py:1357
  293.8 1.4 slice-start.2
  296.2 58.1 %copy-start.4 = (s32[8,768,4]{2,1,0:T(8,128)}, s32[8,768,4]{2,1,0:T(8,128)S(1)}, u32[]{:S(2)}) copy-start(s32[8,768,4]{2,1,0:T(8,128)S(1)} %bitcast_dynamic-update-slice_fusion.column_ref) | copy-start | bytes 294916
  552.3 0.6 copy-start.20
  552.3 0.9 copy-start.13
  554.1 8.1 all-to-all-start
  557.5 316.5 %reduce-scatter.7.cloned.1.call-start = ((), (), s32[]{:S(2)}) async-start(), calls=%async_computation.10 | async-start | bytes 3932160 | tf_op jit(solution)/shard_map/reduce_scatter | solution.py:2024
  562.9 76.1 %copy-start.1 = (f32[192,2048]{1,0:T(8,128)S(1)}, f32[192,2048]{1,0:T(8,128)}, u32[]{:S(2)}) copy-start(f32[192,2048]{1,0:T(8,128)} %copy-done) | copy-start | bytes 4718596
  562.9 76.1 %copy-start.12 = (f32[2048]{0:T(1024)S(1)}, f32[2048]{0:T(1024)}, u32[]{:S(2)}) copy-start(f32[2048]{0:T(1024)} %copy-done.11) | copy-start | bytes 24580
  562.9 76.1 %copy-start.16 = (f32[192]{0:T(256)S(1)}, f32[192]{0:T(256)}, u32[]{:S(2)}) copy-start(f32[192]{0:T(256)} %copy-done.15) | copy-start | bytes 2308
  637.0 5.2 copy-start.2
  732.3 4.0 copy-start.24
  732.3 143.0 %reduce-scatter.11.cloned.1.call-start = ((), (), s32[]{:S(2)}) async-start(), calls=%async_computation.12 | async-start | bytes 2949120 | tf_op jit(solution)/shard_map/reduce_scatter | solution.py:2060
  732.6 3.8 copy-start.3
  738.3 2.0 copy-start.8
  740.3 165.8 %reduce-scatter.9.cloned.1.call-start = ((), (), s32[]{:S(2)}) async-start(), calls=%async_computation.11 | async-start | bytes 7077888 | tf_op jit(solution)/shard_map/reduce_scatter | solution.py:2070
  808.6 1.0 copy-start.9
  808.6 2.6 copy-start.10
  808.7 2.8 copy-start.19
  808.7 2.8 copy-start.17
  878.8 4.5 copy-start.6
  879.7 26.3 %all-to-all-start.1 = ((bf16[192,4,512]{2,0,1:T(8,128)(2,1)}), bf16[192,4,512]{2,0,1:T(8,128)(2,1)S(1)}, u32[]{:S(2)}, u32[]{:S(2)}) async-start(bf16[192,4,512]{2,0,1:T(8,128)(2,1)} %bitcast.74), calls=%async_computation.3 | async-start | bytes 1572864 | tf_op jit(solution)/shard_map/all_to_all | solution.py:2049
  884.1 18.0 %slice-start = ((s8[8388608]{0:T(1024)(128)(4,1)}), s8[4194304]{0:T(1024)(128)(4,1)S(1)}, s32[]{:S(2)}) async-start(s8[8388608]{0:T(1024)(128)(4,1)} %bitcast.77), calls=%async_computation.13 | async-start | bytes 8388608
  891.7 7.5 copy-start.5
  891.7 7.5 copy-start.7
  891.7 10.3 %slice-start.1 = ((s8[8388608]{0:T(1024)(128)(4,1)}), s8[4194304]{0:T(1024)(128)(4,1)S(1)}, s32[]{:S(2)}) async-start(s8[8388608]{0:T(1024)(128)(4,1)} %bitcast.77), calls=%async_computation.14 | async-start | bytes 8388608
Sparse Core Ops, SparseCore 0:
  13.9 59.2 all-gather.3
  74.8 63.4 all-gather.5
  147.4 132.4 all-gather.7
  552.4 155.2 reduce-scatter.4
  732.5 58.1 reduce-scatter.6
  793.9 43.8 reduce-scatter.10
  841.2 61.7 reduce-scatter.8

commit v7 on v5

--- a/solution.py
+++ b/solution.py
@@ -7,7 +7,7 @@
 from jax.experimental.pallas import tpu as pltpu
 from jax.sharding import PartitionSpec as P
 
-QUERY_BLOCK = 256
+QUERY_BLOCK = 384
 CHUNK = 768
 SLOTS = 256
 EXTRA = 128

time: 919 us -> 926 us (level)
  Pallas kernels: 753 us -> 766 us
    pallas_call x1, Pallas kernels: 185 us -> 201 us  [run_exchange_pass(): pl.pallas_call(exchange_pass, grid=(2 * chunks, local), in_specs=[pl.Bloc...]
  transfers between devices with their start and end apart: 13 -> 13, of which waited for: 4 -> 4; matrix products, arithmetic and copies ran while one was open for 10% -> 10% of each run, Pallas kernels for 62% -> 61%
where the time goes in v7:
time: 926 us; the launch traced here: 924 us
  Pallas kernels  766 us (83%)
  other arithmetic  48.5 us (5%)
  local copies, waits for them, and re-layouts  33.1 us (4%)
  matrix products  30.9 us (3%)
  waiting for transfers between devices  16.5 us (2%)
  between operations  15.1 us (2%)
  starting transfers between devices  13.1 us (1%)
    pallas_call x1, Pallas kernels, run_exchange_pass(): pl.pallas_call(exchange_pass, grid=(2 * chunks, local), in_specs=[pl.Bloc...  201 us
    pallas_call x3, Pallas kernels, gather_tp(): pl.pallas_call(functools.partial(line_gather, size, columns), in_specs=[p...  163 us
    pallas_call x1, Pallas kernels, run_grads_scatter(): pl.pallas_call(functools.partial(grads_scatter, size, local), grid=(2 * l...  74.1 us
    pallas_call x1, Pallas kernels, close_tp(): pl.pallas_call(functools.partial(closing_sums, sizes, narrow), in_specs=[...  60.9 us
    pallas_call x1, Pallas kernels, scatter_tp(): pl.pallas_call(functools.partial(line_scatter, size, columns), in_specs=[...  58.9 us
    pallas_call x1, Pallas kernels, run_select_grads(): pl.pallas_call(select_grads, grid_spec=pltpu.PrefetchScalarGridSpec(num_s...  56.3 us
    pallas_call x1, Pallas kernels, gather_ctx(): pl.pallas_call(functools.partial(peer_gather, size), in_specs=[pl.BlockSp...  49.8 us
    pallas_call x1, Pallas kernels, scatter_ctx(): pl.pallas_call(functools.partial(peer_scatter, size), in_specs=[pl.BlockS...  37.1 us
  transfers between devices with their start and end apart: 13, of which 4 were waited for; matrix products, arithmetic and copies ran while one was open for 10% of the time, Pallas kernels for 61%

profile of v7, /device:TPU:0, one launch (start us, length us, event | category | flops | bytes accessed | tf_op | source)
XLA Modules:
  0.0 923.5 jit_solution(6926966595174262743)
XLA Ops:
  7.2 1.1 copy.126
  8.3 0.8 copy.127
  9.2 0.8 broadcast_in_dim.88
  9.9 0.8 broadcast_in_dim.89
  10.7 3.0 concatenate.28
  14.2 3.0 collective-permute-start
  17.2 55.7 %gather_tp.3.input_ref = bf16[768,2048]{1,0:T(8,128)(2,1)} custom-call(bf16[768,512]{1,0:T(8,128)(2,1)} %in_ref.1), custom_call_target="tpu_custom_call" | custom-call | bytes 150000000 | tf_op jit(solution)/shard_map/gather_tp/pallas_call | solution.py:1117
  74.3 1.4 fusion.20
  75.7 1.2 pad_maximum_fusion.1
  77.4 2.7 convert_reduce_fusion
  80.2 11.3 %project.1 = (bf16[768,2048]{1,0:T(8,128)(2,1)}, f32[768,1]{1,0:T(8,128)}, f32[768,1024]{1,0:T(8,128)}, bf16[768,512]{1,0:T(8,128)(2,1)}, bf16[768,1024]{1,0:T(8,128)(2,1)}) custom-call(bf16[768,2048]{1,0:T(8,128)(2,1)} %gather_tp.3.input_ref, f32[1,2048]{1,0:T(1,128)} %bitcast.86, bf16[2048,2176]{1,0:T(8,128)(2,1)} %all-gather.4.cloned.1.call-done.weight_ref, ...), custom_call_target="tpu_custom_call" | custom-call | flops 4831838208 | bytes 6291456 | tf_op jit(solution)/shard_map/project/pallas_call | solution.py:1528
  91.5 49.8 %gather_ctx.1.key_ref.value_ref = bf16[1536,1024]{1,0:T(8,128)(2,1)} custom-call(bf16[768,1024]{1,0:T(8,128)(2,1)} %get-tuple-element.66.in_ref), custom_call_target="tpu_custom_call" | custom-call | bytes 100000000 | tf_op jit(solution)/shard_map/gather_ctx/pallas_call | solution.py:1192
  141.3 6.0 concatenate.31
  148.6 1.3 copy.172
  149.9 13.6 %attend.1 = (bf16[768,512]{1,0:T(8,128)(2,1)}, f32[4,2,1,384]{3,2,1,0:T(1,128)}) custom-call(bf16[768,512]{1,0:T(8,128)(2,1)} %get-tuple-element.64.query_ref, bf16[1536,1024]{1,0:T(8,128)(2,1)} %gather_ctx.1.key_ref.value_ref, bf16[1536,1024]{1,0:T(8,128)(2,1)} %gather_ctx.1.key_ref.value_ref, f32[2,1,384]{2,1,0:T(1,128)} %convert_element_type.141.seg_row_ref, ...), custom_call_target="tpu_custom_call" | custom-call | flops 2415919104 | bytes 3145728 | tf_op jit(solution)/shard_map/attend/pallas_call | solution.py:1306
  163.4 5.3 convolution_convert_fusion.1.in_ref
  168.8 58.9 %scatter_tp.1 = f32[192,2048]{1,0:T(8,128)} custom-call(bf16[768,2048]{1,0:T(8,128)(2,1)} %convolution_convert_fusion.1.in_ref), custom_call_target="tpu_custom_call" | custom-call | bytes 150000000 | tf_op jit(solution)/shard_map/scatter_tp/pallas_call | solution.py:1137
  227.7 1.9 multiply_reduce_fusion.2
  229.6 1.1 copy-done
  230.9 1.5 fusion.34
  232.8 1.1 concatenate.32.in_ref
  233.9 54.7 %gather_tp.4.own_ref = bf16[768,2176]{1,0:T(8,128)(2,1)} custom-call(bf16[192,2176]{1,0:T(8,128)(2,1)} %concatenate.32.in_ref), custom_call_target="tpu_custom_call" | custom-call | bytes 150000000 | tf_op jit(solution)/shard_map/gather_tp/pallas_call | solution.py:1117
  288.8 0.8 collective-permute-start.2
  289.6 1.7 collective-permute-start.3
  291.3 1.4 slice-done.2
  293.7 1.8 copy.153.rank_ref
  295.5 56.3 %select_grads.1 = (bf16[8,4,256,2048]{3,2,1,0:T(8,128)(2,1)}, f32[8,4,256,256]{3,2,1,0:T(8,128)}) custom-call(s32[8]{0:T(128)} %stack.83.ids_ref, s32[8,4,1,768]{3,2,1,0:T(1,128)} %copy.153.rank_ref, bf16[6144,2176]{1,0:T(8,128)(2,1)} %all-gather.8.cloned.1.call-done.grad_ref, bf16[4,256,2048]{2,1,0:T(8,128)(2,1)} %down_ref.1), custom_call_target="tpu_custom_call" | custom-call | flops 34359738368 | bytes 58720256 | tf_op jit(solution)/shard_map/select_grads/pallas_call | solution.py:580
  351.8 12.0 %collective-permute-done.2.from_across_ref = bf16[768,2176]{1,0:T(8,128)(2,1)} collective-permute-done((bf16[768,2176]{1,0:T(8,128)(2,1)}, bf16[768,2176]{1,0:T(8,128)(2,1)}, u32[]{:S(2)}, u32[]{:S(2)}) %collective-permute-start.2) | collective-permute-done | bytes 3342368 | tf_op jit(solution)/shard_map/ppermute | solution.py:1352
  364.3 201.0 %exchange_pass.1 = (bf16[8,4,256,2048]{3,2,1,0:T(8,128)(2,1)}, bf16[8,4,256,256]{3,2,1,0:T(8,128)(2,1)}, bf16[8,4,256,256]{3,2,1,0:T(8,128)(2,1)}, bf16[8,4,256,...) custom-call(s32[8,4,1,768]{3,2,1,0:T(1,128)} %copy.153.rank_ref, ...), custom_call_target="tpu_custom_call" | custom-call | flops 85899345920 | bytes 71303168 | tf_op jit(solution)/shard_map/exchange_pass/pallas_call | solution.py:623
  566.2 0.9 select_reduce_fusion
  567.2 3.4 all-to-all-start
  570.6 0.9 slice.71
  571.7 3.6 all-to-all-done
  576.0 74.1 %grads_scatter.1 = (f32[192,2048]{1,0:T(8,128)}, f32[32,768]{1,0:T(8,128)}, f32[4,2048,256]{2,1,0:T(8,128)}, f32[4,2048,256]{2,1,0:T(8,128)}, f32[4,256,2048]{2,1,0:T(8,128)}) custom-call(bf16[768,2048]{1,0:T(8,128)(2,1)} %get-tuple-element.75.in_ref, f32[32,768]{1,0:T(8,128)} %reshape.181.small_ref, bf16[8,4,256,2048]{3,2,1,0:T(8,128)(2,1)} %get-tuple-element.77.rows_ref, ...), custom_call_target="tpu_custom_call" | custom-call | flops 25769803776 | bytes 150000000 | tf_op jit(solution)/shard_map/grads_scatter/pallas_call | solution.py:1776
  650.1 1.0 fusion.21
  651.2 0.9 fusion.22
  652.1 3.3 multiply_reduce_fusion
  655.4 2.6 add_convert_fusion.1.in_ref
  658.0 52.2 %gather_tp.5 = bf16[768,2048]{1,0:T(8,128)(2,1)} custom-call(bf16[192,2048]{1,0:T(8,128)(2,1)} %add_convert_fusion.1.in_ref), custom_call_target="tpu_custom_call" | custom-call | bytes 150000000 | tf_op jit(solution)/shard_map/gather_tp/pallas_call | solution.py:1117
  710.2 5.2 fusion.9.grad_ref
  715.5 20.7 %attend_back.1 = (f32[768,512]{1,0:T(8,128)}, bf16[1536,512]{1,0:T(8,128)(2,1)}, bf16[1536,512]{1,0:T(8,128)(2,1)}) custom-call(bf16[768,512]{1,0:T(8,128)(2,1)} %get-tuple-element.64.query_ref, bf16[1536,1024]{1,0:T(8,128)(2,1)} %gather_ctx.1.key_ref.value_ref, bf16[1536,1024]{1,0:T(8,128)(2,1)} %gather_ctx.1.key_ref.value_ref, ...), custom_call_target="tpu_custom_call" | custom-call | flops 6039797760 | bytes 6291456 | tf_op jit(solution)/shard_map/attend_back/pallas_call | solution.py:1328
  736.3 3.7 fusion.3
  740.0 1.9 convolution_convert_fusion.2
  741.9 2.0 maximum_maximum_fusion
  744.0 3.5 pad_maximum_fusion.in_ref
  747.5 37.1 %scatter_ctx.1.group_grad_ref = bf16[768,1024]{1,0:T(8,128)(2,1)} custom-call(bf16[1536,1024]{1,0:T(8,128)(2,1)} %pad_maximum_fusion.in_ref), custom_call_target="tpu_custom_call" | custom-call | bytes 100000000 | tf_op jit(solution)/shard_map/scatter_ctx/pallas_call | solution.py:1212
  784.6 20.0 %project_back.1 = (bf16[768,1536]{1,0:T(8,128)(2,1)}, bf16[768,2048]{1,0:T(8,128)(2,1)}, f32[768,1]{1,0:T(8,128)}, f32[1,2048]{1,0:T(1,128)}, f32[2,128]{1,0:T(2,128)}) custom-call(f32[768,512]{1,0:T(8,128)} %get-tuple-element.84.query_grad_ref, bf16[768,1024]{1,0:T(8,128)(2,1)} %scatter_ctx.1.group_grad_ref, f32[768,1024]{1,0:T(8,128)} %get-tuple-element.89.pre_ref, ...), custom_call_target="tpu_custom_call" | custom-call | flops 4831838208 | bytes 8388608 | tf_op jit(solution)/shard_map/project_back/pallas_call | solution.py:1570
  804.6 9.4 %convolution_convert_fusion = bf16[2048,1536]{1,0:T(8,128)(2,1)} fusion(bf16[768,2048]{1,0:T(8,128)(2,1)} %get-tuple-element.101, bf16[768,1536]{1,0:T(8,128)(2,1)} %get-tuple-element.102), kind=kOutput, calls=%fused_computation | convolution fusion | flops 4834983936 | bytes 11796480 | tf_op jit(solution)/shard_map/dot_general | solution.py:2056
  814.1 0.9 copy-done.9
  815.2 1.2 slice_convert_fusion
  817.5 60.9 %close_tp.1 = (f32[768,512]{1,0:T(8,128)}, f32[8,640]{1,0:T(8,128)}, f32[8,128]{1,0:T(8,128)}) custom-call(bf16[768,2048]{1,0:T(8,128)(2,1)} %get-tuple-element.91.in_ref, f32[8,768]{1,0:T(8,128)} %pad_maximum_fusion.3.small_ref), custom_call_target="tpu_custom_call" | custom-call | bytes 150000000 | tf_op jit(solution)/shard_map/close_tp/pallas_call | solution.py:1163
  878.4 0.7 reshape.184
  881.0 1.3 convert_element_type.157
  882.4 1.9 convert_element_type.164
  884.2 1.3 slice.98
  885.7 0.9 copy.175
  886.7 3.7 all-to-all-start.1
  890.4 0.8 slice_bitcast_fusion
  891.3 7.5 broadcast_clamp_fusion.2
  898.8 7.6 broadcast_clamp_fusion.1
  906.4 2.8 multiply_add_fusion
  909.2 4.0 broadcast_clamp_fusion
  913.2 2.3 fusion.31
  915.5 0.9 copy.189
  (134 shorter events, 10.8 us)
Async XLA Ops:
  7.2 6.7 copy-start.18
  7.2 6.7 copy-start.23
  7.2 66.1 %all-gather.4.cloned.1.call-start = ((), (), s32[]{:S(2)}) async-start(), calls=%async_computation.6 | async-start | bytes 10027008 | tf_op jit(solution)/shard_map/all_gather | solution.py:1884
  13.8 59.6 %copy-start.14 = (s32[768,8]{0,1:T(8,128)S(1)}, s32[768,8]{0,1:T(8,128)}, u32[]{:S(2)}) copy-start(s32[768,8]{0,1:T(8,128)} %param.20) | copy-start | bytes 73732
  13.8 59.9 %copy-start.21 = (f32[128]{0:T(128)S(1)}, f32[128]{0:T(128)}, u32[]{:S(2)}) copy-start(f32[128]{0:T(128)} %param.26) | copy-start | bytes 1540
  13.8 59.9 %copy-start.22 = (f32[128]{0:T(128)S(1)}, f32[128]{0:T(128)}, u32[]{:S(2)}) copy-start(f32[128]{0:T(128)} %param.25) | copy-start | bytes 1540
  13.8 127.5 %all-gather.6.cloned.1.call-start = ((), (), s32[]{:S(2)}) async-start(), calls=%async_computation.7 | async-start | bytes 3932160 | tf_op jit(solution)/shard_map/all_gather | solution.py:1905
  14.2 58.8 %collective-permute-start = (f32[1,768]{1,0:T(1,128)S(1)}, f32[1,768]{1,0:T(1,128)S(1)}, u32[]{:S(2)}, u32[]{:S(2)}) collective-permute-start(f32[1,768]{1,0:T(1,128)S(1)} %convert_element_type.136), channel_id=1, source_target_pairs={{0,4},{4,0},{1,5},{5,1},{2,6},{6,2},{3,7},{7,3},{8,12},{12,8},{9,1... | collective-permute-start | bytes 9224 | tf_op jit(solution)/shard_map/ppermute | solution.py:1899
  73.3 218.0 %all-gather.8.cloned.1.call-start = ((), (), s32[]{:S(2)}) async-start(), calls=%async_computation.8 | async-start | bytes 30081024 | tf_op jit(solution)/shard_map/all_gather | solution.py:1931
  80.2 149.4 %copy-start.11 = (f32[2048]{0:T(1024)}, f32[2048]{0:T(1024)S(1)}, u32[]{:S(2)}) copy-start(f32[2048]{0:T(1024)S(1)} %get-tuple-element.110) | copy-start | bytes 24580
  147.3 588.8 %reduce-scatter.5.cloned.1.call-start = ((), (), s32[]{:S(2)}) async-start(), calls=%async_computation.9 | async-start | bytes 28311552 | tf_op jit(solution)/shard_map/reduce_scatter | solution.py:2013
  229.6 1.1 copy-start
  229.6 3.2 copy-start.15
  288.7 75.6 %collective-permute-start.1 = (bf16[768,2176]{1,0:T(8,128)(2,1)}, bf16[768,2176]{1,0:T(8,128)(2,1)}, u32[]{:S(2)}, u32[]{:S(2)}) collective-permute-start(bf16[768,2176]{1,0:T(8,128)(2,1)} %gather_tp.4.own_ref), channel_id=1, source_target_pairs={{0,8},{8,0},{16,24},{24,16},{1,9},{9,1},{17,25},{25,17},{2,10},{10... | collective-permute-start | bytes 10027016 | tf_op jit(solution)/shard_map/ppermute | solution.py:1348
  288.8 75.0 %collective-permute-start.2 = (bf16[768,2176]{1,0:T(8,128)(2,1)}, bf16[768,2176]{1,0:T(8,128)(2,1)}, u32[]{:S(2)}, u32[]{:S(2)}) collective-permute-start(bf16[768,2176]{1,0:T(8,128)(2,1)} %gather_tp.4.own_ref), channel_id=1, source_target_pairs={{0,16},{8,24},{16,0},{24,8},{1,17},{9,25},{17,1},{25,9},{2,18},{10... | collective-permute-start | bytes 10027016 | tf_op jit(solution)/shard_map/ppermute | solution.py:1352
  289.6 74.7 %collective-permute-start.3 = (bf16[768,2176]{1,0:T(8,128)(2,1)}, bf16[768,2176]{1,0:T(8,128)(2,1)}, u32[]{:S(2)}, u32[]{:S(2)}) collective-permute-start(bf16[768,2176]{1,0:T(8,128)(2,1)} %gather_tp.4.own_ref), channel_id=1, source_target_pairs={{0,4},{4,0},{1,5},{5,1},{2,6},{6,2},{3,7},{7,3},{8,12},{12,8},{9,1... | collective-permute-start | bytes 10027016 | tf_op jit(solution)/shard_map/ppermute | solution.py:1356
  291.3 1.4 slice-start.2
  293.7 58.1 %copy-start.4 = (s32[8,768,4]{2,1,0:T(8,128)}, s32[8,768,4]{2,1,0:T(8,128)S(1)}, u32[]{:S(2)}) copy-start(s32[8,768,4]{2,1,0:T(8,128)S(1)} %bitcast_dynamic-update-slice_fusion.column_ref) | copy-start | bytes 294916
  565.3 0.6 copy-start.20
  565.3 0.9 copy-start.13
  567.2 8.1 all-to-all-start
  570.6 310.4 %reduce-scatter.7.cloned.1.call-start = ((), (), s32[]{:S(2)}) async-start(), calls=%async_computation.10 | async-start | bytes 3932160 | tf_op jit(solution)/shard_map/reduce_scatter | solution.py:2023
  576.0 76.1 %copy-start.1 = (f32[192,2048]{1,0:T(8,128)S(1)}, f32[192,2048]{1,0:T(8,128)}, u32[]{:S(2)}) copy-start(f32[192,2048]{1,0:T(8,128)} %copy-done) | copy-start | bytes 4718596
  576.0 76.1 %copy-start.12 = (f32[2048]{0:T(1024)S(1)}, f32[2048]{0:T(1024)}, u32[]{:S(2)}) copy-start(f32[2048]{0:T(1024)} %copy-done.11) | copy-start | bytes 24580
  576.0 76.1 %copy-start.16 = (f32[192]{0:T(256)S(1)}, f32[192]{0:T(256)}, u32[]{:S(2)}) copy-start(f32[192]{0:T(256)} %copy-done.15) | copy-start | bytes 2308
  650.1 5.3 copy-start.2
  736.1 3.9 copy-start.24
  736.2 146.2 %reduce-scatter.11.cloned.1.call-start = ((), (), s32[]{:S(2)}) async-start(), calls=%async_computation.12 | async-start | bytes 2949120 | tf_op jit(solution)/shard_map/reduce_scatter | solution.py:2059
  736.2 3.8 copy-start.3
  741.9 2.0 copy-start.8
  743.9 169.3 %reduce-scatter.9.cloned.1.call-start = ((), (), s32[]{:S(2)}) async-start(), calls=%async_computation.11 | async-start | bytes 7077888 | tf_op jit(solution)/shard_map/reduce_scatter | solution.py:2069
  814.0 1.0 copy-start.9
  814.0 2.6 copy-start.10
  814.0 2.8 copy-start.19
  814.0 2.8 copy-start.17
  885.7 4.7 copy-start.6
  886.7 26.5 %all-to-all-start.1 = ((bf16[192,4,512]{2,0,1:T(8,128)(2,1)}), bf16[192,4,512]{2,0,1:T(8,128)(2,1)S(1)}, u32[]{:S(2)}, u32[]{:S(2)}) async-start(bf16[192,4,512]{2,0,1:T(8,128)(2,1)} %bitcast.74), calls=%async_computation.3 | async-start | bytes 1572864 | tf_op jit(solution)/shard_map/all_to_all | solution.py:2048
  891.3 17.9 %slice-start = ((s8[8388608]{0:T(1024)(128)(4,1)}), s8[4194304]{0:T(1024)(128)(4,1)S(1)}, s32[]{:S(2)}) async-start(s8[8388608]{0:T(1024)(128)(4,1)} %bitcast.77), calls=%async_computation.13 | async-start | bytes 8388608
  898.8 7.6 copy-start.5
  898.8 7.6 copy-start.7
  898.8 10.4 %slice-start.1 = ((s8[8388608]{0:T(1024)(128)(4,1)}), s8[4194304]{0:T(1024)(128)(4,1)S(1)}, s32[]{:S(2)}) async-start(s8[8388608]{0:T(1024)(128)(4,1)} %bitcast.77), calls=%async_computation.14 | async-start | bytes 8388608
Sparse Core Ops, SparseCore 0:
  13.9 59.2 all-gather.3
  74.8 63.4 all-gather.5
  147.4 132.4 all-gather.7
  565.5 155.5 reduce-scatter.4
  736.3 58.4 reduce-scatter.6
  798.0 43.9 reduce-scatter.10
  845.3 61.5 reduce-scatter.8
